TPU v7x, 32 devices: a whole 2x2x4 slice. The times are simulated.
32 devices in a mesh: dp: 8 (over z, x), chan: 4 (over y, core).
Axes of the slice: x: 2, y: 2, z: 4, core: 2. Of those that a mesh axis runs over, the one named last changes fastest.
Arguments:
- features: bfloat16 [12800, 512], P('dp', 'chan'), may hold values from -6 to 6
- shortcut: bfloat16 [12800, 2048], P('dp', 'chan'), may hold values from -6 to 6
- valid_masks: int32 [128, 100], P('dp'), may hold values from 0 to 1, as said below
- labels: int32 [128], P('dp'), may hold values from 0 to 999
- w_conv: float32 [4608, 512], P('dp', 'chan'), may hold values from -0.09375 to 0.09375
- w_proj: float32 [512, 2048], P('dp', 'chan'), may hold values from -0.25 to 0.25
- w_cls: float32 [2048, 1000], P(('chan', 'dp')), may hold values from -0.25 to 0.25
- cls_bias: float32 [1000], replicated, may hold values from -1.5 to 1.5
- norm_one: float32 [2, 512], P(None, 'chan'), may hold values from -0.6 to 1.5
- norm_two: float32 [2, 2048], P(None, 'chan'), may hold values from -0.6 to 1.5
- conv_moment: float32 [4608, 512], P('dp', 'chan'), may hold values from -0.0048828125 to 0.0048828125
- conv_second: float32 [4608, 512], P('dp', 'chan'), may hold values from 6.1035155e-07 to 2.4414062e-06
- proj_moment: float32 [512, 2048], P('dp', 'chan'), may hold values from -0.0078125 to 0.0078125
- proj_second: float32 [512, 2048], P('dp', 'chan'), may hold values from 1.8692017e-06 to 7.476807e-06
- cls_moment: float32 [2048, 1000], P(('chan', 'dp')), may hold values from -0.0234375 to 0.0234375
- cls_second: float32 [2048, 1000], P(('chan', 'dp')), may hold values from 1.7578124e-05 to 7.03125e-05
- bias_moment: float32 [1000], replicated, may hold values from -0.0390625 to 0.0390625
- bias_second: float32 [1000], replicated, may hold values from 4.8828126e-05 to 0.0001953125
- one_moment: float32 [2, 512], P(None, 'chan'), may hold values from -0.00140625 to 0.00140625
- one_second: float32 [2, 512], P(None, 'chan'), may hold values from 4.943848e-07 to 1.9775391e-06
- two_moment: float32 [2, 2048], P(None, 'chan'), may hold values from -0.0048828125 to 0.0048828125
- two_second: float32 [2, 2048], P(None, 'chan'), may hold values from 3.0899048e-06 to 2.3841858e-05
Outputs:
- new_w_conv: float32 [4608, 512], P('dp', 'chan')
- new_conv_moment: float32 [4608, 512], P('dp', 'chan')
- new_conv_second: float32 [4608, 512], P('dp', 'chan')
- new_w_proj: float32 [512, 2048], P('dp', 'chan')
- new_proj_moment: float32 [512, 2048], P('dp', 'chan')
- new_proj_second: float32 [512, 2048], P('dp', 'chan')
- new_w_cls: float32 [2048, 1000], P(('chan', 'dp'))
- new_cls_moment: float32 [2048, 1000], P(('chan', 'dp'))
- new_cls_second: float32 [2048, 1000], P(('chan', 'dp'))
- new_cls_bias: float32 [1000], replicated
- new_bias_moment: float32 [1000], replicated
- new_bias_second: float32 [1000], replicated
- new_norm_one: float32 [2, 512], P(None, 'chan')
- new_one_moment: float32 [2, 512], P(None, 'chan')
- new_one_second: float32 [2, 512], P(None, 'chan')
- new_norm_two: float32 [2, 2048], P(None, 'chan')
- new_two_moment: float32 [2, 2048], P(None, 'chan')
- new_two_second: float32 [2, 2048], P(None, 'chan')
- conv_copy: bfloat16 [4608, 512], P('dp', 'chan')
- proj_copy: bfloat16 [512, 2048], P('dp', 'chan')
- cls_copy: bfloat16 [2048, 1000], P(('chan', 'dp'))
- train_loss: float32 [], replicated
Inputs may be any that keep to these rules, and one draw needn't show every extreme that they name: `valid_masks`: each image's valid pixels form a rectangle of 6 to 10 rows by 6 to 10 columns at the top left of its buffer.
All inputs are finite; a program needn't handle non-finite values.
Results may differ from a plain program's by a relative error of at most 0.015.
Values may be sent and summed in bfloat16 or wider, within the bound.
A program may use at most 128 MiB of HBM per device.

v0:
```python
import jax
import jax.numpy as jnp
from jax import lax
from jax.sharding import PartitionSpec as P

SIDE = 10
MICRO = 4
STEP = 3


norm_eps = 1e-05
adam_eps = 1e-08
beta_decay = 0.5
rate_matrix = 0.02
rate_small = 0.5
weight_decay = 0.01


def tap_columns(flat, images):
    width = flat.shape[1]
    grid = flat.reshape(images, SIDE, SIDE, width)
    padded = jnp.pad(grid, ((0, 0), (1, 1), (1, 1), (0, 0)))
    pieces = [
        padded[:, down : down + SIDE, across : across + SIDE, :]
        for down in range(3)
        for across in range(3)
    ]
    return jnp.concatenate(pieces, axis=3).reshape(images * SIDE * SIDE, 9 * width)


def silu_slope(value):
    sigma = jax.nn.sigmoid(value)
    return sigma * (1.0 + value * (1.0 - sigma))


def norm_forward(hidden, weights, params):
    sums, squares, count = lax.psum(
        (
            jnp.sum(hidden * weights, axis=0),
            jnp.sum(hidden * hidden * weights, axis=0),
            jnp.sum(weights),
        ),
        "dp",
    )
    center = sums / count
    scale = lax.rsqrt(squares / count - center * center + norm_eps)
    normed = (hidden - center) * scale
    return (params[0] * normed + params[1], normed, scale, count)


def norm_backward(upstream, normed, scale, count, weights, params):
    total, along = lax.psum((jnp.sum(upstream, axis=0), jnp.sum(upstream * normed, axis=0)), "dp")
    grad = weights * params[0] * scale * (upstream - (total + normed * along) / count)
    return (grad, jnp.stack([along, total]))


def contract_rows(left, right):
    return lax.dot_general(
        left, right, (((0,), (0,)), ((), ())), preferred_element_type=jnp.float32
    )


def contract_cols(left, right):
    return lax.dot_general(
        left, right, (((1,), (1,)), ((), ())), preferred_element_type=jnp.float32
    )


def adam_step(weight, moment, second, grad, rate, decay):
    moment = beta_decay * moment + (1.0 - beta_decay) * grad
    second = beta_decay * second + (1.0 - beta_decay) * grad * grad
    correct = 1.0 - beta_decay**STEP
    weight = weight - rate * (
        moment / correct / (jnp.sqrt(second / correct) + adam_eps) + decay * weight
    )
    return (weight, moment, second)


def per_device(
    features,
    shortcut,
    valid_masks,
    labels,
    w_conv,
    w_proj,
    w_cls,
    cls_bias,
    norm_one,
    norm_two,
    conv_moment,
    conv_second,
    proj_moment,
    proj_second,
    cls_moment,
    cls_second,
    bias_moment,
    bias_second,
    one_moment,
    one_second,
    two_moment,
    two_second,
):
    images = valid_masks.shape[0]
    per_block = images // MICRO
    pixels = per_block * SIDE * SIDE
    total_images = images * lax.axis_size("dp")
    classes = w_cls.shape[1]
    conv_full, proj_full, cls_full = (
        lax.all_gather(w_conv.astype(jnp.bfloat16), "dp", axis=0, tiled=True),
        lax.all_gather(w_proj.astype(jnp.bfloat16), "dp", axis=0, tiled=True),
        lax.all_gather(w_cls.astype(jnp.bfloat16), "dp", axis=0, tiled=True),
    )
    sum_conv = jnp.zeros(w_conv.shape, jnp.float32)
    sum_proj = jnp.zeros(w_proj.shape, jnp.float32)
    sum_cls = jnp.zeros(w_cls.shape, jnp.float32)
    grad_one = jnp.zeros(norm_one.shape, jnp.float32)
    grad_two = jnp.zeros(norm_two.shape, jnp.float32)
    grad_bias = jnp.zeros((classes,), jnp.float32)
    loss_sum = jnp.zeros((), jnp.float32)
    class_ids = jnp.arange(classes)[None, :]
    for block in range(MICRO):
        start = block * pixels
        inputs = features[start : start + pixels]
        residual = shortcut[start : start + pixels].astype(jnp.float32)
        image_mask = valid_masks[block * per_block : (block + 1) * per_block].astype(jnp.float32)
        targets = labels[block * per_block : (block + 1) * per_block]
        pixel_counts = jnp.sum(image_mask, axis=1)
        weights = image_mask.reshape(pixels, 1)
        masked = inputs * weights.astype(jnp.bfloat16)
        gathered = lax.all_gather(masked, "chan", axis=1, tiled=True)
        columns = tap_columns(gathered, per_block)
        hidden = jnp.dot(columns, conv_full, preferred_element_type=jnp.float32)
        shifted, normed_one, scale_one, count = norm_forward(hidden, weights, norm_one)
        active = (jax.nn.silu(shifted) * weights).astype(jnp.bfloat16)
        active_full = lax.all_gather(active, "chan", axis=1, tiled=True)
        second = jnp.dot(active_full, proj_full, preferred_element_type=jnp.float32)
        shifted_two, normed_two, scale_two, count_again = norm_forward(second, weights, norm_two)
        summed = shifted_two + residual
        output = jax.nn.silu(summed) * weights
        channels = output.shape[1]
        pooled = (
            jnp.sum(output.reshape(per_block, SIDE * SIDE, channels), axis=1)
            / pixel_counts[:, None]
        ).astype(jnp.bfloat16)
        partial_value = jnp.dot(pooled, cls_full, preferred_element_type=jnp.float32)
        logits = lax.psum(partial_value, "chan") + cls_bias
        top = jnp.max(logits, axis=1, keepdims=True)
        expo = jnp.exp(logits - top)
        expo_sum = jnp.sum(expo, axis=1, keepdims=True)
        onehot = (targets[:, None] == class_ids).astype(jnp.float32)
        picked = jnp.sum(logits * onehot, axis=1)
        loss_sum = loss_sum + jnp.sum(top[:, 0] + jnp.log(expo_sum[:, 0]) - picked)
        dlogits = ((expo / expo_sum - onehot) / total_images).astype(jnp.bfloat16)
        grad_bias = grad_bias + jnp.sum(dlogits.astype(jnp.float32), axis=0)
        local_cls = contract_rows(pooled, dlogits)
        grad_pool = contract_cols(dlogits, cls_full)
        spread_back = jnp.broadcast_to(
            (grad_pool / pixel_counts[:, None])[:, None, :], (per_block, SIDE * SIDE, channels)
        ).reshape(pixels, channels)
        upstream_two = spread_back * weights * silu_slope(summed)
        grad_second, pair_two = norm_backward(
            upstream_two, normed_two, scale_two, count, weights, norm_two
        )
        grad_second = grad_second.astype(jnp.bfloat16)
        local_proj = contract_rows(active_full, grad_second)
        partial_act = contract_cols(grad_second, proj_full)
        grad_active = lax.psum_scatter(
            partial_act.astype(jnp.bfloat16), "chan", scatter_dimension=1, tiled=True
        ).astype(jnp.float32)
        upstream_one = grad_active * weights * silu_slope(shifted)
        grad_hidden, pair_one = norm_backward(
            upstream_one, normed_one, scale_one, count, weights, norm_one
        )
        local_conv = contract_rows(columns, grad_hidden.astype(jnp.bfloat16))
        grad_one = grad_one + pair_one
        grad_two = grad_two + pair_two
        part_conv, part_proj, part_cls = (
            lax.psum_scatter(
                local_conv.astype(jnp.bfloat16), "dp", scatter_dimension=0, tiled=True
            ).astype(jnp.float32),
            lax.psum_scatter(
                local_proj.astype(jnp.bfloat16), "dp", scatter_dimension=0, tiled=True
            ).astype(jnp.float32),
            lax.psum_scatter(
                local_cls.astype(jnp.bfloat16), "dp", scatter_dimension=0, tiled=True
            ).astype(jnp.float32),
        )
        sum_conv = sum_conv + part_conv
        sum_proj = sum_proj + part_proj
        sum_cls = sum_cls + part_cls
    loss_total, bias_total = lax.psum((loss_sum, grad_bias), "dp")
    train_loss = loss_total / total_images
    conv_w, conv_m, conv_v = adam_step(
        w_conv, conv_moment, conv_second, sum_conv, rate_matrix, weight_decay
    )
    proj_w, proj_m, proj_v = adam_step(
        w_proj, proj_moment, proj_second, sum_proj, rate_matrix, weight_decay
    )
    cls_w, cls_m, cls_v = adam_step(
        w_cls, cls_moment, cls_second, sum_cls, rate_matrix, weight_decay
    )
    bias_w, bias_m, bias_v = adam_step(
        cls_bias, bias_moment, bias_second, bias_total, rate_small, 0.0
    )
    one_w, one_m, one_v = adam_step(norm_one, one_moment, one_second, grad_one, rate_small, 0.0)
    two_w, two_m, two_v = adam_step(norm_two, two_moment, two_second, grad_two, rate_small, 0.0)
    return (
        conv_w,
        conv_m,
        conv_v,
        proj_w,
        proj_m,
        proj_v,
        cls_w,
        cls_m,
        cls_v,
        bias_w,
        bias_m,
        bias_v,
        one_w,
        one_m,
        one_v,
        two_w,
        two_m,
        two_v,
        conv_w.astype(jnp.bfloat16),
        proj_w.astype(jnp.bfloat16),
        cls_w.astype(jnp.bfloat16),
        train_loss,
    )


def solution(mesh):
    placed = (
        P("dp", "chan"),
        P("dp", "chan"),
        P("dp", None),
        P("dp"),
        P("dp", "chan"),
        P("dp", "chan"),
        P(("chan", "dp"), None),
        P(),
        P(None, "chan"),
        P(None, "chan"),
        P("dp", "chan"),
        P("dp", "chan"),
        P("dp", "chan"),
        P("dp", "chan"),
        P(("chan", "dp"), None),
        P(("chan", "dp"), None),
        P(),
        P(),
        P(None, "chan"),
        P(None, "chan"),
        P(None, "chan"),
        P(None, "chan"),
    )
    return jax.shard_map(
        per_device,
        mesh=mesh,
        in_specs=placed,
        out_specs=(
            P("dp", "chan"),
            P("dp", "chan"),
            P("dp", "chan"),
            P("dp", "chan"),
            P("dp", "chan"),
            P("dp", "chan"),
            P(("chan", "dp"), None),
            P(("chan", "dp"), None),
            P(("chan", "dp"), None),
            P(),
            P(),
            P(),
            P(None, "chan"),
            P(None, "chan"),
            P(None, "chan"),
            P(None, "chan"),
            P(None, "chan"),
            P(None, "chan"),
            P("dp", "chan"),
            P("dp", "chan"),
            P(("chan", "dp"), None),
            P(),
        ),
        check_vma=False,
    )
```

profile of v0, /device:TPU:0, one launch (start us, length us, event | category | flops | bytes accessed | tf_op | source)
XLA Modules:
  0.0 1312.9 jit_solution(438460147472299722)
XLA Ops:
  14.5 8.0 all_gather.40
  22.5 6.7 all_gather.38
  29.2 6.7 all_gather.33
  35.9 6.7 all_gather.42
  44.8 5.3 pad_slice_fusion.8
  61.3 2.0 concatenate.104
  73.4 2.7 pad_slice_fusion.16
  98.5 2.5 pad_slice_fusion.24
  100.9 2.1 concatenate.87
  109.0 2.0 concatenate.84
  121.9 2.5 pad_slice_fusion
  124.4 2.0 concatenate.114
  130.5 2.0 concatenate.110
  152.4 32.0 %all_gather.36 = bf16[512,512]{1,0:T(8,128)(2,1)S(1)} all-gather(bf16[64,512]{1,0:T(8,128)(2,1)S(1)} %convert_element_type.263), channel_id=1, replica_groups=mesh['dp'=8,'chan'=4] {'dp'}, dimensions={0}, use_global_device_ids=true | all-gather | bytes 589824 | tf_op jit(solution)/shard_map/all_gather | solution.py:110
  184.4 33.0 %all_gather.37 = bf16[512,1000]{1,0:T(8,128)(2,1)S(1)} all-gather(bf16[64,1000]{1,0:T(8,128)(2,1)S(1)} %convert_element_type.266), channel_id=1, replica_groups=mesh['dp'=8,'chan'=4] {'dp'}, dimensions={0}, use_global_device_ids=true | all-gather | bytes 1152000 | tf_op jit(solution)/shard_map/all_gather | solution.py:111
  217.4 3.6 multiply_reduce_fusion.17
  221.1 3.3 multiply_reduce_fusion.20
  224.4 3.3 multiply_reduce_fusion.23
  228.9 22.9 %all-reduce.7 = (f32[]{:T(128)}, f32[128]{0:T(128)S(1)}, f32[128]{0:T(128)S(1)}, f32[128]{0:T(128)S(1)}, f32[]{:T(128)}, /*index=5*/f32[128]{0:T(128)S(1)}, f32[...) all-reduce(f32[]{:T(128)} %get-tuple-element.63, ...), channel_id=1, replica_groups=mesh['dp'=8,'chan'=4] {'dp'}, use_global_device_ids=true, to_apply=%region_78.79 | all-reduce | flops 1028 | bytes 8224 | tf_op jit(solution)/shard_map/psum | solution.py:37
  254.8 6.2 all_gather.41
  261.0 6.7 all_gather.35
  267.7 6.7 all_gather.39
  274.4 6.7 all_gather.43
  285.4 33.0 %all-reduce.6 = (f32[512]{0:T(512)S(1)}, f32[512]{0:T(512)S(1)}, f32[512]{0:T(512)S(1)}, f32[512]{0:T(512)S(1)}, f32[512]{0:T(512)S(1)}, /*index=5*/f32[512]{0:T(512)S(1)}, f32[512]{0:T(512)S(1)}, f32[512]{0:T(512)S(1)}) all-reduce(f32[512]{0:T(512)S(1)} %get-tuple-element.29, ...), channel_id=1, replica_groups=mesh['dp'=8,'chan'=4] {'dp'}, use_global_device_ids=true, to_apply=%region_82.83 | all-reduce | flops 4096 | bytes 32768 | tf_op jit(solution)/shard_map/psum | solution.py:37
  319.7 2.5 multiply_multiply_fusion.7
  322.3 2.1 reshape.223
  325.8 3.9 multiply_multiply_fusion.3
  329.7 2.2 reshape.231
  334.4 2.1 reshape.235
  337.8 2.1 reshape.227
  344.1 11.4 all-reduce.8
  366.4 2.2 reshape.224
  369.6 2.1 reshape.236
  372.7 2.2 reshape.232
  375.0 4.3 fusion.58
  379.4 2.3 fusion.60
  381.6 33.0 %all-reduce.5 = (f32[512]{0:T(512)S(1)}, f32[512]{0:T(512)S(1)}, f32[512]{0:T(512)S(1)}, f32[512]{0:T(512)S(1)}, f32[512]{0:T(512)S(1)}, /*index=5*/f32[512]{0:T(512)S(1)}, f32[512]{0:T(512)S(1)}, f32[512]{0:T(512)S(1)}) all-reduce(f32[512]{0:T(512)S(1)} %get-tuple-element.168, ...), channel_id=1, replica_groups=mesh['dp'=8,'chan'=4] {'dp'}, use_global_device_ids=true, to_apply=%region_93.94 | all-reduce | flops 4096 | bytes 32768 | tf_op jit(solution)/shard_map/psum | solution.py:52
  414.7 4.1 multiply_convert_fusion.3
  420.7 2.0 copy.44
  422.8 2.2 convolution_convert_fusion.12
  427.0 3.7 multiply_convert_fusion.1
  435.6 2.3 convolution_convert_fusion.11
  455.4 10.3 reduce-scatter.55.cloned.1.call-done
  466.7 23.0 %reduce-scatter.51.cloned.1.call-done = bf16[128,400]{1,0:T(8,128)(2,1)} async-done(((bf16[512,400]{1,0:T(8,128)(2,1)}), bf16[128,400]{1,0:T(8,128)(2,1)}) %reduce-scatter.51.cloned.1.call-update) | async-done | bytes 102416
  490.7 23.2 %reduce-scatter.53.cloned.1.call-done = bf16[128,400]{1,0:T(8,128)(2,1)} async-done(((bf16[512,400]{1,0:T(8,128)(2,1)}), bf16[128,400]{1,0:T(8,128)(2,1)}) %reduce-scatter.53.cloned.1.call-update) | async-done | bytes 102416
  515.6 22.4 %all-reduce.4 = (f32[128]{0:T(128)S(1)}, f32[128]{0:T(128)S(1)}, f32[128]{0:T(128)S(1)}, f32[128]{0:T(128)S(1)}, f32[128]{0:T(128)S(1)}, /*index=5*/f32[128]{0:T...) all-reduce(f32[128]{0:T(128)S(1)} %get-tuple-element.45, ...), channel_id=1, replica_groups=mesh['dp'=8,'chan'=4] {'dp'}, use_global_device_ids=true, to_apply=%region_98.99 | all-reduce | flops 2025 | bytes 16200 | tf_op jit(solution)/shard_map/psum | solution.py:52
  538.0 5.3 convolution_convert_fusion
  543.4 5.3 convolution_convert_fusion.1
  548.8 5.4 convolution_convert_fusion.2
  554.4 5.3 convolution_convert_fusion.3
  562.4 16.7 %reduce-scatter.33.cloned.1.call-done = bf16[64,512]{1,0:T(8,128)(2,1)} async-done(((bf16[512,512]{1,0:T(8,128)(2,1)}), bf16[64,512]{1,0:T(8,128)(2,1)}) %reduce-scatter.33.cloned.1.call-update) | async-done | bytes 65552 | tf_op jit(solution)/shard_map/reduce_scatter | solution.py:181
  579.1 64.6 %reduce-scatter.39.cloned.1.call-done = bf16[64,512]{1,0:T(8,128)(2,1)} async-done(((bf16[512,512]{1,0:T(8,128)(2,1)}), bf16[64,512]{1,0:T(8,128)(2,1)}) %reduce-scatter.39.cloned.1.call-update) | async-done | bytes 65552 | tf_op jit(solution)/shard_map/reduce_scatter | solution.py:181
  643.7 64.4 %reduce-scatter.35.cloned.1.call-done = bf16[64,512]{1,0:T(8,128)(2,1)} async-done(((bf16[512,512]{1,0:T(8,128)(2,1)}), bf16[64,512]{1,0:T(8,128)(2,1)}) %reduce-scatter.35.cloned.1.call-update) | async-done | bytes 65552 | tf_op jit(solution)/shard_map/reduce_scatter | solution.py:181
  708.1 64.6 %reduce-scatter.37.cloned.1.call-done = bf16[64,512]{1,0:T(8,128)(2,1)} async-done(((bf16[512,512]{1,0:T(8,128)(2,1)}), bf16[64,512]{1,0:T(8,128)(2,1)}) %reduce-scatter.37.cloned.1.call-update) | async-done | bytes 65552 | tf_op jit(solution)/shard_map/reduce_scatter | solution.py:181
  774.5 64.1 %reduce-scatter.43.cloned.1.call-done = bf16[64,1000]{1,0:T(8,128)(2,1)} async-done(((bf16[512,1000]{1,0:T(8,128)(2,1)}), bf16[64,1000]{1,0:T(8,128)(2,1)}) %reduce-scatter.43.cloned.1.call-update) | async-done | bytes 128016 | tf_op jit(solution)/shard_map/reduce_scatter | solution.py:184
  838.6 66.2 %reduce-scatter.41.cloned.1.call-done = bf16[64,1000]{1,0:T(8,128)(2,1)} async-done(((bf16[512,1000]{1,0:T(8,128)(2,1)}), bf16[64,1000]{1,0:T(8,128)(2,1)}) %reduce-scatter.41.cloned.1.call-update) | async-done | bytes 128016 | tf_op jit(solution)/shard_map/reduce_scatter | solution.py:184
  904.8 65.8 %reduce-scatter.47.cloned.1.call-done = bf16[64,1000]{1,0:T(8,128)(2,1)} async-done(((bf16[512,1000]{1,0:T(8,128)(2,1)}), bf16[64,1000]{1,0:T(8,128)(2,1)}) %reduce-scatter.47.cloned.1.call-update) | async-done | bytes 128016 | tf_op jit(solution)/shard_map/reduce_scatter | solution.py:184
  970.6 66.3 %reduce-scatter.45.cloned.1.call-done = bf16[64,1000]{1,0:T(8,128)(2,1)} async-done(((bf16[512,1000]{1,0:T(8,128)(2,1)}), bf16[64,1000]{1,0:T(8,128)(2,1)}) %reduce-scatter.45.cloned.1.call-update) | async-done | bytes 128016 | tf_op jit(solution)/shard_map/reduce_scatter | solution.py:184
  1036.9 2.2 fusion.62
  1039.1 64.1 %reduce-scatter.31.cloned.1.call-done = bf16[576,128]{1,0:T(8,128)(2,1)} async-done(((bf16[4608,128]{1,0:T(8,128)(2,1)}), bf16[576,128]{1,0:T(8,128)(2,1)}) %reduce-scatter.31.cloned.1.call-update) | async-done | bytes 147472 | tf_op jit(solution)/shard_map/reduce_scatter | solution.py:178
  1103.2 66.7 %reduce-scatter.29.cloned.1.call-done = bf16[576,128]{1,0:T(8,128)(2,1)} async-done(((bf16[4608,128]{1,0:T(8,128)(2,1)}), bf16[576,128]{1,0:T(8,128)(2,1)}) %reduce-scatter.29.cloned.1.call-update) | async-done | bytes 147472 | tf_op jit(solution)/shard_map/reduce_scatter | solution.py:178
  1169.9 66.3 %reduce-scatter.27.cloned.1.call-done = bf16[576,128]{1,0:T(8,128)(2,1)} async-done(((bf16[4608,128]{1,0:T(8,128)(2,1)}), bf16[576,128]{1,0:T(8,128)(2,1)}) %reduce-scatter.27.cloned.1.call-update) | async-done | bytes 147472 | tf_op jit(solution)/shard_map/reduce_scatter | solution.py:178
  1236.2 66.3 %reduce-scatter.25.cloned.1.call-done = bf16[576,128]{1,0:T(8,128)(2,1)} async-done(((bf16[4608,128]{1,0:T(8,128)(2,1)}), bf16[576,128]{1,0:T(8,128)(2,1)}) %reduce-scatter.25.cloned.1.call-update) | async-done | bytes 147472 | tf_op jit(solution)/shard_map/reduce_scatter | solution.py:178
  1302.5 2.3 fusion.66
  (489 shorter events, 156.0 us)
Async XLA Ops:
  7.2 210.2 %all-gather.2.cloned.1.call-start = ((), (), s32[]{:S(2)}) async-start(), calls=%async_computation.16 | async-start | bytes 1327104 | tf_op jit(solution)/shard_map/all_gather | solution.py:109
  8.9 445.4 %reduce-scatter.49.cloned.1.call-start = ((), (), s32[]{:S(2)}) async-start(), calls=%async_computation.29 | async-start | bytes 655360
  10.5 25.4 %copy-start.54 = (f32[400]{0:T(512)}, f32[400]{0:T(512)S(1)}, u32[]{:S(2)}) copy-start(f32[400]{0:T(512)S(1)} %reshape.225) | copy-start | bytes 4804
  11.2 24.6 %copy-start.59 = (f32[400]{0:T(512)}, f32[400]{0:T(512)S(1)}, u32[]{:S(2)}) copy-start(f32[400]{0:T(512)S(1)} %reshape.233) | copy-start | bytes 4804
  100.9 12.0 copy-start.6
  147.2 70.2 %copy-start.57 = (f32[400]{0:T(512)S(1)}, f32[400]{0:T(512)}, u32[]{:S(2)}) copy-start(f32[400]{0:T(512)} %copy-done.56) | copy-start | bytes 4804
  150.6 33.8 %copy-start.69 = (bf16[400,4608]{1,0:T(8,128)(2,1)}, bf16[400,4608]{1,0:T(8,128)(2,1)S(1)}, u32[]{:S(2)}) copy-start(bf16[400,4608]{1,0:T(8,128)(2,1)S(1)} %constant_dynamic-update-slice_fusion.27) | copy-start | bytes 11059204
  150.6 103.8 %copy-start.104 = (f32[128]{0:T(128)}, f32[128]{0:T(128)S(1)}, u32[]{:S(2)}) copy-start(f32[128]{0:T(128)S(1)} %get-tuple-element.238) | copy-start | bytes 1540
  150.6 103.8 %copy-start.106 = (f32[128]{0:T(128)}, f32[128]{0:T(128)S(1)}, u32[]{:S(2)}) copy-start(f32[128]{0:T(128)S(1)} %get-tuple-element.239) | copy-start | bytes 1540
  184.4 36.6 %copy-start.55 = (f32[400]{0:T(512)S(1)}, f32[400]{0:T(512)}, u32[]{:S(2)}) copy-start(f32[400]{0:T(512)} %copy-done.54) | copy-start | bytes 4804
  221.1 33.4 %copy-start.34 = (f32[400,128]{1,0:T(8,128)}, f32[400,128]{1,0:T(8,128)S(1)}, u32[]{:S(2)}) copy-start(f32[400,128]{1,0:T(8,128)S(1)} %get-tuple-element.247) | copy-start | bytes 614404
  224.3 30.1 %copy-start.32 = (f32[400,128]{1,0:T(8,128)}, f32[400,128]{1,0:T(8,128)S(1)}, u32[]{:S(2)}) copy-start(f32[400,128]{1,0:T(8,128)S(1)} %get-tuple-element.246) | copy-start | bytes 614404
  228.9 52.3 %copy-start.36 = (f32[400,128]{1,0:T(8,128)}, f32[400,128]{1,0:T(8,128)S(1)}, u32[]{:S(2)}) copy-start(f32[400,128]{1,0:T(8,128)S(1)} %get-tuple-element.244) | copy-start | bytes 614404
  252.4 31.2 %copy-start.129 = (f32[128]{0:T(128)}, f32[128]{0:T(128)S(1)}, u32[]{:S(2)}) copy-start(f32[128]{0:T(128)S(1)} %get-tuple-element.163) | copy-start | bytes 1540
  252.4 31.2 %copy-start.131 = (f32[128]{0:T(128)}, f32[128]{0:T(128)S(1)}, u32[]{:S(2)}) copy-start(f32[128]{0:T(128)S(1)} %get-tuple-element.164) | copy-start | bytes 1540
  253.0 14.7 %copy-start.117 = (f32[128]{0:T(128)}, f32[128]{0:T(128)S(1)}, u32[]{:S(2)}) copy-start(f32[128]{0:T(128)S(1)} %get-tuple-element.161) | copy-start | bytes 1540
  253.7 27.4 %copy-start.121 = (f32[128]{0:T(128)}, f32[128]{0:T(128)S(1)}, u32[]{:S(2)}) copy-start(f32[128]{0:T(128)S(1)} %get-tuple-element.159) | copy-start | bytes 1540
  253.8 29.9 %copy-start.123 = (f32[128]{0:T(128)}, f32[128]{0:T(128)S(1)}, u32[]{:S(2)}) copy-start(f32[128]{0:T(128)S(1)} %get-tuple-element.160) | copy-start | bytes 1540
  254.4 29.2 %copy-start.125 = (f32[128]{0:T(128)}, f32[128]{0:T(128)S(1)}, u32[]{:S(2)}) copy-start(f32[128]{0:T(128)S(1)} %get-tuple-element.157) | copy-start | bytes 1540
  254.4 29.2 %copy-start.127 = (f32[128]{0:T(128)}, f32[128]{0:T(128)S(1)}, u32[]{:S(2)}) copy-start(f32[128]{0:T(128)S(1)} %get-tuple-element.158) | copy-start | bytes 1540
  261.0 23.9 %copy-start.39 = (bf16[400,512]{1,0:T(8,128)(2,1)}, bf16[400,512]{1,0:T(8,128)(2,1)S(1)}, u32[]{:S(2)}) copy-start(bf16[400,512]{1,0:T(8,128)(2,1)S(1)} %all_gather.41) | copy-start | bytes 1228804
  267.7 15.9 %copy-start.45 = (bf16[400,512]{1,0:T(8,128)(2,1)}, bf16[400,512]{1,0:T(8,128)(2,1)S(1)}, u32[]{:S(2)}) copy-start(bf16[400,512]{1,0:T(8,128)(2,1)S(1)} %all_gather.35) | copy-start | bytes 1228804
  267.7 17.2 %copy-start.58 = (f32[400]{0:T(512)S(1)}, f32[400]{0:T(512)}, u32[]{:S(2)}) copy-start(f32[400]{0:T(512)} %copy-done.56) | copy-start | bytes 4804
  283.2 36.6 %copy-start.53 = (f32[1,512]{1,0:T(1,128)S(1)}, f32[1,512]{1,0:T(1,128)}, u32[]{:S(2)}) copy-start(f32[1,512]{1,0:T(1,128)} %get-tuple-element.220) | copy-start | bytes 6148
  283.2 36.6 %copy-start.67 = (f32[1,512]{1,0:T(1,128)S(1)}, f32[1,512]{1,0:T(1,128)}, u32[]{:S(2)}) copy-start(f32[1,512]{1,0:T(1,128)} %get-tuple-element.221) | copy-start | bytes 6148
  336.5 19.1 %copy-start.52 = (f32[1000]{0:T(1024)S(1)}, f32[1000]{0:T(1024)}, u32[]{:S(2)}) copy-start(f32[1000]{0:T(1024)} %param.29) | copy-start | bytes 12004
  414.7 12.4 copy-start.94
  422.7 43.0 %reduce-scatter.55.cloned.1.call-start = ((), (), s32[]{:S(2)}) async-start(), calls=%async_computation.32 | async-start | bytes 655360
  427.0 62.8 %reduce-scatter.51.cloned.1.call-start = ((), (), s32[]{:S(2)}) async-start(), calls=%async_computation.30 | async-start | bytes 655360
  432.9 81.0 %reduce-scatter.53.cloned.1.call-start = ((), (), s32[]{:S(2)}) async-start(), calls=%async_computation.31 | async-start | bytes 655360
  435.5 143.5 %reduce-scatter.33.cloned.1.call-start = ((), (), s32[]{:S(2)}) async-start(), calls=%async_computation.21 | async-start | bytes 589824 | tf_op jit(solution)/shard_map/reduce_scatter | solution.py:181
  438.0 205.7 %reduce-scatter.39.cloned.1.call-start = ((), (), s32[]{:S(2)}) async-start(), calls=%async_computation.24 | async-start | bytes 589824 | tf_op jit(solution)/shard_map/reduce_scatter | solution.py:181
  439.3 268.8 %reduce-scatter.35.cloned.1.call-start = ((), (), s32[]{:S(2)}) async-start(), calls=%async_computation.22 | async-start | bytes 589824 | tf_op jit(solution)/shard_map/reduce_scatter | solution.py:181
  440.7 332.0 %reduce-scatter.37.cloned.1.call-start = ((), (), s32[]{:S(2)}) async-start(), calls=%async_computation.23 | async-start | bytes 589824 | tf_op jit(solution)/shard_map/reduce_scatter | solution.py:181
  442.0 396.5 %reduce-scatter.43.cloned.1.call-start = ((), (), s32[]{:S(2)}) async-start(), calls=%async_computation.26 | async-start | bytes 1179648 | tf_op jit(solution)/shard_map/reduce_scatter | solution.py:184
  443.8 71.2 %copy-start.37 = (f32[400,128]{1,0:T(8,128)S(1)}, f32[400,128]{1,0:T(8,128)}, u32[]{:S(2)}) copy-start(f32[400,128]{1,0:T(8,128)} %copy-done.36) | copy-start | bytes 614404
  443.8 71.1 %copy-start.105 = (f32[128]{0:T(128)S(1)}, f32[128]{0:T(128)}, u32[]{:S(2)}) copy-start(f32[128]{0:T(128)} %copy-done.104) | copy-start | bytes 1540
  443.8 71.1 %copy-start.107 = (f32[128]{0:T(128)S(1)}, f32[128]{0:T(128)}, u32[]{:S(2)}) copy-start(f32[128]{0:T(128)} %copy-done.106) | copy-start | bytes 1540
  443.8 71.1 %copy-start.130 = (f32[128]{0:T(128)S(1)}, f32[128]{0:T(128)}, u32[]{:S(2)}) copy-start(f32[128]{0:T(128)} %copy-done.129) | copy-start | bytes 1540
  443.8 71.1 %copy-start.132 = (f32[128]{0:T(128)S(1)}, f32[128]{0:T(128)}, u32[]{:S(2)}) copy-start(f32[128]{0:T(128)} %copy-done.131) | copy-start | bytes 1540
  443.8 71.3 %copy-start.33 = (f32[400,128]{1,0:T(8,128)S(1)}, f32[400,128]{1,0:T(8,128)}, u32[]{:S(2)}) copy-start(f32[400,128]{1,0:T(8,128)} %copy-done.32) | copy-start | bytes 614404
  443.9 71.3 %copy-start.35 = (f32[400,128]{1,0:T(8,128)S(1)}, f32[400,128]{1,0:T(8,128)}, u32[]{:S(2)}) copy-start(f32[400,128]{1,0:T(8,128)} %copy-done.34) | copy-start | bytes 614404
  443.9 71.3 %copy-start.118 = (f32[128]{0:T(128)S(1)}, f32[128]{0:T(128)}, u32[]{:S(2)}) copy-start(f32[128]{0:T(128)} %copy-done.117) | copy-start | bytes 1540
  443.9 71.3 %copy-start.120 = (f32[128]{0:T(128)S(1)}, f32[128]{0:T(128)}, u32[]{:S(2)}) copy-start(f32[128]{0:T(128)} %copy-done.119) | copy-start | bytes 1540
  443.9 71.3 %copy-start.122 = (f32[128]{0:T(128)S(1)}, f32[128]{0:T(128)}, u32[]{:S(2)}) copy-start(f32[128]{0:T(128)} %copy-done.121) | copy-start | bytes 1540
  443.9 71.3 %copy-start.124 = (f32[128]{0:T(128)S(1)}, f32[128]{0:T(128)}, u32[]{:S(2)}) copy-start(f32[128]{0:T(128)} %copy-done.123) | copy-start | bytes 1540
  443.9 71.3 %copy-start.126 = (f32[128]{0:T(128)S(1)}, f32[128]{0:T(128)}, u32[]{:S(2)}) copy-start(f32[128]{0:T(128)} %copy-done.125) | copy-start | bytes 1540
  443.9 71.3 %copy-start.128 = (f32[128]{0:T(128)S(1)}, f32[128]{0:T(128)}, u32[]{:S(2)}) copy-start(f32[128]{0:T(128)} %copy-done.127) | copy-start | bytes 1540
  443.9 460.9 %reduce-scatter.41.cloned.1.call-start = ((), (), s32[]{:S(2)}) async-start(), calls=%async_computation.25 | async-start | bytes 1179648 | tf_op jit(solution)/shard_map/reduce_scatter | solution.py:184
  445.6 525.0 %reduce-scatter.47.cloned.1.call-start = ((), (), s32[]{:S(2)}) async-start(), calls=%async_computation.28 | async-start | bytes 1179648 | tf_op jit(solution)/shard_map/reduce_scatter | solution.py:184
  447.2 589.7 %reduce-scatter.45.cloned.1.call-start = ((), (), s32[]{:S(2)}) async-start(), calls=%async_computation.27 | async-start | bytes 1179648 | tf_op jit(solution)/shard_map/reduce_scatter | solution.py:184
  448.8 654.3 %reduce-scatter.31.cloned.1.call-start = ((), (), s32[]{:S(2)}) async-start(), calls=%async_computation.20 | async-start | bytes 1327104 | tf_op jit(solution)/shard_map/reduce_scatter | solution.py:178
  543.4 626.6 %reduce-scatter.29.cloned.1.call-start = ((), (), s32[]{:S(2)}) async-start(), calls=%async_computation.19 | async-start | bytes 1327104 | tf_op jit(solution)/shard_map/reduce_scatter | solution.py:178
  548.7 687.5 %reduce-scatter.27.cloned.1.call-start = ((), (), s32[]{:S(2)}) async-start(), calls=%async_computation.18 | async-start | bytes 1327104 | tf_op jit(solution)/shard_map/reduce_scatter | solution.py:178
  554.2 748.3 %reduce-scatter.25.cloned.1.call-start = ((), (), s32[]{:S(2)}) async-start(), calls=%async_computation.17 | async-start | bytes 1327104 | tf_op jit(solution)/shard_map/reduce_scatter | solution.py:178
  554.3 218.4 %copy-start.38 = (f32[64,512]{1,0:T(8,128)S(1)}, f32[64,512]{1,0:T(8,128)}, u32[]{:S(2)}) copy-start(f32[64,512]{1,0:T(8,128)} %param.27) | copy-start | bytes 393220
  554.3 218.4 %copy-start.50 = (f32[64,512]{1,0:T(8,128)S(1)}, f32[64,512]{1,0:T(8,128)}, u32[]{:S(2)}) copy-start(f32[64,512]{1,0:T(8,128)} %param.34) | copy-start | bytes 393220
  554.3 218.4 %copy-start.51 = (f32[64,512]{1,0:T(8,128)S(1)}, f32[64,512]{1,0:T(8,128)}, u32[]{:S(2)}) copy-start(f32[64,512]{1,0:T(8,128)} %param.35) | copy-start | bytes 393220
  554.4 482.5 %copy-start.31 = (f32[64,1000]{1,0:T(8,128)S(1)}, f32[64,1000]{1,0:T(8,128)}, u32[]{:S(2)}) copy-start(f32[64,1000]{1,0:T(8,128)} %param.28) | copy-start | bytes 768004
  554.4 482.5 %copy-start.48 = (f32[64,1000]{1,0:T(8,128)S(1)}, f32[64,1000]{1,0:T(8,128)}, u32[]{:S(2)}) copy-start(f32[64,1000]{1,0:T(8,128)} %param.36) | copy-start | bytes 768004
  554.4 482.5 %copy-start.49 = (f32[64,1000]{1,0:T(8,128)S(1)}, f32[64,1000]{1,0:T(8,128)}, u32[]{:S(2)}) copy-start(f32[64,1000]{1,0:T(8,128)} %param.37) | copy-start | bytes 768004
  559.7 742.7 %copy-start.30 = (f32[576,128]{1,0:T(8,128)S(1)}, f32[576,128]{1,0:T(8,128)}, u32[]{:S(2)}) copy-start(f32[576,128]{1,0:T(8,128)} %param.26) | copy-start | bytes 884740
  559.7 742.7 %copy-start.46 = (f32[576,128]{1,0:T(8,128)S(1)}, f32[576,128]{1,0:T(8,128)}, u32[]{:S(2)}) copy-start(f32[576,128]{1,0:T(8,128)} %param.32) | copy-start | bytes 884740
  559.7 742.7 %copy-start.47 = (f32[576,128]{1,0:T(8,128)S(1)}, f32[576,128]{1,0:T(8,128)}, u32[]{:S(2)}) copy-start(f32[576,128]{1,0:T(8,128)} %param.33) | copy-start | bytes 884740
  (107 other events, 694.6 us)
Sparse Core Ops, SparseCore 0:
  10.8 43.7 all-gather.1
  422.8 18.4 reduce-scatter.48
  444.0 21.6 reduce-scatter.54
  468.0 21.6 reduce-scatter.50
  492.2 21.6 reduce-scatter.52
  517.1 61.9 reduce-scatter.32
  582.8 60.8 reduce-scatter.38
  647.0 61.0 reduce-scatter.34
  711.8 60.8 reduce-scatter.36
  776.0 62.5 reduce-scatter.42
  842.4 62.3 reduce-scatter.40
  908.1 62.4 reduce-scatter.46
  974.4 62.4 reduce-scatter.44
  1040.1 63.0 reduce-scatter.30
  1106.4 63.4 reduce-scatter.28
  1173.2 62.9 reduce-scatter.26
  1239.4 62.9 reduce-scatter.24
where the time goes:
time: 1320 us; the launch traced here: 1310 us
  waiting for transfers between devices  793 us (60%)
  blocking collectives  242 us (18%)
  local copies, waits for them, and re-layouts  143 us (11%)
  matrix products  60.6 us (5%)
  other arithmetic  53.2 us (4%)
  between operations  20.6 us (2%)
    reduce_scatter x4, waiting for transfers between devices, per_device(): lax.psum_scatter(local_conv.astype(jnp.bfloat16), 'dp', scatter_dimension...  263 us
    reduce_scatter x4, waiting for transfers between devices, per_device(): lax.psum_scatter(local_cls.astype(jnp.bfloat16), 'dp', scatter_dimension=...  262 us
    reduce_scatter x4, waiting for transfers between devices, per_device(): lax.psum_scatter(local_proj.astype(jnp.bfloat16), 'dp', scatter_dimension...  210 us
    concatenate x36, local copies, waits for them, and re-layouts, tap_columns(): jnp.concatenate(pieces, axis=3).reshape(images * SIDE * SIDE, 9 * width)  58.5 us
    unnamed x21, waiting for transfers between devices  56.8 us
    psum x2, blocking collectives, norm_forward(): lax.psum((jnp.sum(hidden * weights, axis=0), jnp.sum(hidden * hidden * we...  55.9 us
    psum x2, blocking collectives, norm_backward(): lax.psum((jnp.sum(upstream, axis=0), jnp.sum(upstream * normed, axis=0)),...  55.4 us
    unnamed x348, local copies, waits for them, and re-layouts  47.5 us
  transfers between devices with their start and end apart: 17, of which 15 were waited for; matrix products, arithmetic and copies ran while one was open for 13% of the time, Pallas kernels for 0%

commit v1 on v0

v1 whole, which is shorter than its diff:
```python
import jax
import jax.numpy as jnp
from jax import lax
from jax.sharding import PartitionSpec as P

SIDE = 10
MICRO = 4
STEP = 3


norm_eps = 1e-05
adam_eps = 1e-08
beta_decay = 0.5
rate_matrix = 0.02
rate_small = 0.5
weight_decay = 0.01


def tap_columns(flat, images):
    width = flat.shape[1]
    grid = flat.reshape(images, SIDE, SIDE, width)
    padded = jnp.pad(grid, ((0, 0), (1, 1), (1, 1), (0, 0)))
    pieces = [
        padded[:, down : down + SIDE, across : across + SIDE, :]
        for down in range(3)
        for across in range(3)
    ]
    return jnp.concatenate(pieces, axis=3).reshape(images * SIDE * SIDE, 9 * width)


def silu_slope(value):
    sigma = jax.nn.sigmoid(value)
    return sigma * (1.0 + value * (1.0 - sigma))


def norm_forward(hidden, weights, params):
    sums, squares, count = lax.psum(
        (
            jnp.sum(hidden * weights, axis=1),
            jnp.sum(hidden * hidden * weights, axis=1),
            jnp.sum(weights, axis=1),
        ),
        "dp",
    )
    center = sums / count
    scale = lax.rsqrt(squares / count - center * center + norm_eps)
    normed = (hidden - center[:, None]) * scale[:, None]
    return (params[0] * normed + params[1], normed, scale[:, None], count[:, None])


def norm_backward(upstream, normed, scale, count, weights, params):
    total, along = lax.psum((jnp.sum(upstream, axis=1), jnp.sum(upstream * normed, axis=1)), "dp")
    grad = (
        weights
        * params[0]
        * scale
        * (upstream - (total[:, None] + normed * along[:, None]) / count)
    )
    return (grad, jnp.stack([jnp.sum(along, axis=0), jnp.sum(total, axis=0)]))


def contract_rows(left, right):
    return lax.dot_general(
        left, right, (((0,), (0,)), ((), ())), preferred_element_type=jnp.float32
    )


def contract_cols(left, right):
    return lax.dot_general(
        left, right, (((1,), (1,)), ((), ())), preferred_element_type=jnp.float32
    )


def adam_step(weight, moment, second, grad, rate, decay):
    moment = beta_decay * moment + (1.0 - beta_decay) * grad
    second = beta_decay * second + (1.0 - beta_decay) * grad * grad
    correct = 1.0 - beta_decay**STEP
    weight = weight - rate * (
        moment / correct / (jnp.sqrt(second / correct) + adam_eps) + decay * weight
    )
    return (weight, moment, second)


def per_device(
    features,
    shortcut,
    valid_masks,
    labels,
    w_conv,
    w_proj,
    w_cls,
    cls_bias,
    norm_one,
    norm_two,
    conv_moment,
    conv_second,
    proj_moment,
    proj_second,
    cls_moment,
    cls_second,
    bias_moment,
    bias_second,
    one_moment,
    one_second,
    two_moment,
    two_second,
):
    images = valid_masks.shape[0]
    area = SIDE * SIDE
    pixels = images * area
    total_images = images * lax.axis_size("dp")
    classes = w_cls.shape[1]
    conv_full, proj_full, cls_full = (
        lax.all_gather(w_conv.astype(jnp.bfloat16), "dp", axis=0, tiled=True),
        lax.all_gather(w_proj.astype(jnp.bfloat16), "dp", axis=0, tiled=True),
        lax.all_gather(w_cls.astype(jnp.bfloat16), "dp", axis=0, tiled=True),
    )

    def split(flat):
        return flat.reshape((MICRO, -1) + flat.shape[1:])

    def join(parts):
        return parts.reshape((-1,) + parts.shape[2:])

    image_mask = valid_masks.astype(jnp.float32)
    pixel_counts = jnp.sum(image_mask, axis=1)
    weights = split(image_mask.reshape(pixels, 1))
    masked = features * join(weights).astype(jnp.bfloat16)
    gathered = lax.all_gather(masked, "chan", axis=1, tiled=True)
    columns = tap_columns(gathered, images)
    hidden = jnp.dot(columns, conv_full, preferred_element_type=jnp.float32)
    shifted, normed_one, scale_one, count = norm_forward(split(hidden), weights, norm_one)
    active = join((jax.nn.silu(shifted) * weights).astype(jnp.bfloat16))
    active_full = lax.all_gather(active, "chan", axis=1, tiled=True)
    second = jnp.dot(active_full, proj_full, preferred_element_type=jnp.float32)
    shifted_two, normed_two, scale_two, _ = norm_forward(split(second), weights, norm_two)
    summed = shifted_two + split(shortcut.astype(jnp.float32))
    output = jax.nn.silu(summed) * weights
    channels = shortcut.shape[1]
    pooled = (
        jnp.sum(output.reshape(images, area, channels), axis=1) / pixel_counts[:, None]
    ).astype(jnp.bfloat16)
    partial_value = jnp.dot(pooled, cls_full, preferred_element_type=jnp.float32)
    logits = lax.psum(partial_value, "chan") + cls_bias
    top = jnp.max(logits, axis=1, keepdims=True)
    expo = jnp.exp(logits - top)
    expo_sum = jnp.sum(expo, axis=1, keepdims=True)
    onehot = (labels[:, None] == jnp.arange(classes)[None, :]).astype(jnp.float32)
    picked = jnp.sum(logits * onehot, axis=1)
    loss_sum = jnp.sum(top[:, 0] + jnp.log(expo_sum[:, 0]) - picked)
    dlogits = ((expo / expo_sum - onehot) / total_images).astype(jnp.bfloat16)
    grad_bias = jnp.sum(dlogits.astype(jnp.float32), axis=0)
    local_cls = contract_rows(pooled, dlogits)
    grad_pool = contract_cols(dlogits, cls_full)
    spread_back = jnp.broadcast_to(
        (grad_pool / pixel_counts[:, None])[:, None, :], (images, area, channels)
    ).reshape(MICRO, -1, channels)
    upstream_two = spread_back * weights * silu_slope(summed)
    grad_second, grad_two = norm_backward(
        upstream_two, normed_two, scale_two, count, weights, norm_two
    )
    grad_second = join(grad_second.astype(jnp.bfloat16))
    local_proj = contract_rows(active_full, grad_second)
    partial_act = contract_cols(grad_second, proj_full)
    grad_active = lax.psum_scatter(
        partial_act.astype(jnp.bfloat16), "chan", scatter_dimension=1, tiled=True
    ).astype(jnp.float32)
    upstream_one = split(grad_active) * weights * silu_slope(shifted)
    grad_hidden, grad_one = norm_backward(
        upstream_one, normed_one, scale_one, count, weights, norm_one
    )
    local_conv = contract_rows(columns, join(grad_hidden.astype(jnp.bfloat16)))
    sum_conv, sum_proj, sum_cls = (
        lax.psum_scatter(
            local_conv.astype(jnp.bfloat16), "dp", scatter_dimension=0, tiled=True
        ).astype(jnp.float32),
        lax.psum_scatter(
            local_proj.astype(jnp.bfloat16), "dp", scatter_dimension=0, tiled=True
        ).astype(jnp.float32),
        lax.psum_scatter(
            local_cls.astype(jnp.bfloat16), "dp", scatter_dimension=0, tiled=True
        ).astype(jnp.float32),
    )
    loss_total, bias_total = lax.psum((loss_sum, grad_bias), "dp")
    train_loss = loss_total / total_images
    conv_w, conv_m, conv_v = adam_step(
        w_conv, conv_moment, conv_second, sum_conv, rate_matrix, weight_decay
    )
    proj_w, proj_m, proj_v = adam_step(
        w_proj, proj_moment, proj_second, sum_proj, rate_matrix, weight_decay
    )
    cls_w, cls_m, cls_v = adam_step(
        w_cls, cls_moment, cls_second, sum_cls, rate_matrix, weight_decay
    )
    bias_w, bias_m, bias_v = adam_step(
        cls_bias, bias_moment, bias_second, bias_total, rate_small, 0.0
    )
    one_w, one_m, one_v = adam_step(norm_one, one_moment, one_second, grad_one, rate_small, 0.0)
    two_w, two_m, two_v = adam_step(norm_two, two_moment, two_second, grad_two, rate_small, 0.0)
    return (
        conv_w,
        conv_m,
        conv_v,
        proj_w,
        proj_m,
        proj_v,
        cls_w,
        cls_m,
        cls_v,
        bias_w,
        bias_m,
        bias_v,
        one_w,
        one_m,
        one_v,
        two_w,
        two_m,
        two_v,
        conv_w.astype(jnp.bfloat16),
        proj_w.astype(jnp.bfloat16),
        cls_w.astype(jnp.bfloat16),
        train_loss,
    )


def solution(mesh):
    placed = (
        P("dp", "chan"),
        P("dp", "chan"),
        P("dp", None),
        P("dp"),
        P("dp", "chan"),
        P("dp", "chan"),
        P(("chan", "dp"), None),
        P(),
        P(None, "chan"),
        P(None, "chan"),
        P("dp", "chan"),
        P("dp", "chan"),
        P("dp", "chan"),
        P("dp", "chan"),
        P(("chan", "dp"), None),
        P(("chan", "dp"), None),
        P(),
        P(),
        P(None, "chan"),
        P(None, "chan"),
        P(None, "chan"),
        P(None, "chan"),
    )
    return jax.shard_map(
        per_device,
        mesh=mesh,
        in_specs=placed,
        out_specs=(
            P("dp", "chan"),
            P("dp", "chan"),
            P("dp", "chan"),
            P("dp", "chan"),
            P("dp", "chan"),
            P("dp", "chan"),
            P(("chan", "dp"), None),
            P(("chan", "dp"), None),
            P(("chan", "dp"), None),
            P(),
            P(),
            P(),
            P(None, "chan"),
            P(None, "chan"),
            P(None, "chan"),
            P(None, "chan"),
            P(None, "chan"),
            P(None, "chan"),
            P("dp", "chan"),
            P("dp", "chan"),
            P(("chan", "dp"), None),
            P(),
        ),
        check_vma=False,
    )
```

time: 1320 us -> 573 us (0.43)
  waiting for transfers between devices: 793 us -> 166 us
  blocking collectives: 242 us -> 188 us
  matrix products: 60.6 us -> 26.5 us
  other arithmetic: 53.2 us -> 38.8 us
    reduce_scatter x4 -> x1, waiting for transfers between devices: 263 us -> 63 us  [per_device(): lax.psum_scatter(local_conv.astype(jnp.bfloat16), 'dp', scatter_dimension...]
    reduce_scatter x4 -> x1, waiting for transfers between devices: 262 us -> 64 us  [per_device(): lax.psum_scatter(local_cls.astype(jnp.bfloat16), 'dp', scatter_dimension=...]
    reduce_scatter x4 -> x1, waiting for transfers between devices: 210 us -> 19.3 us  [per_device(): lax.psum_scatter(local_proj.astype(jnp.bfloat16), 'dp', scatter_dimension...]
    unnamed x21 -> x8, waiting for transfers between devices: 56.8 us -> 0.12 us
    all_gather x8 -> x0, blocking collectives: 54.4 us -> none  [the longest x4 28.1 us: per_device(): gathered = lax.all_gather(masked, 'chan', axis=1, tiled=True)]
    dot_general x12 -> x3, matrix products: 33.6 us -> 12.6 us  [contract_rows(): lax.dot_general(left, right, (((0,), (0,)), ((), ())), preferred_element_...]
    all_gather x0 -> x2, waiting for transfers between devices: none -> 19.4 us  [the longest x1 19.4 us: per_device(): gathered = lax.all_gather(masked, 'chan', axis=1, tiled=True)]
    unnamed x348 -> x174, local copies, waits for them, and re-layouts: 47.5 us -> 33.2 us
  transfers between devices with their start and end apart: 17 -> 7, of which waited for: 15 -> 4; matrix products, arithmetic and copies ran while one was open for 13% -> 22% of each run, Pallas kernels for 0% -> 0%
where the time goes in v1:
time: 573 us; the launch traced here: 571 us
  blocking collectives  188 us (33%)
  waiting for transfers between devices  166 us (29%)
  local copies, waits for them, and re-layouts  135 us (24%)
  other arithmetic  38.8 us (7%)
  matrix products  26.5 us (5%)
  between operations  16.6 us (3%)
    reduce_scatter x1, waiting for transfers between devices, per_device(): lax.psum_scatter(local_cls.astype(jnp.bfloat16), 'dp', scatter_dimension=...  64 us
    reduce_scatter x1, waiting for transfers between devices, per_device(): lax.psum_scatter(local_conv.astype(jnp.bfloat16), 'dp', scatter_dimension...  63 us
    concatenate x18, local copies, waits for them, and re-layouts, tap_columns(): jnp.concatenate(pieces, axis=3).reshape(images * SIDE * SIDE, 9 * width)  60.2 us
    psum x2, blocking collectives, norm_forward(): lax.psum((jnp.sum(hidden * weights, axis=1), jnp.sum(hidden * hidden * we...  55.3 us
    psum x2, blocking collectives, norm_backward(): lax.psum((jnp.sum(upstream, axis=1), jnp.sum(upstream * normed, axis=1)),...  52.6 us
    all_gather x1, blocking collectives, per_device(): lax.all_gather(w_cls.astype(jnp.bfloat16), 'dp', axis=0, tiled=True)  34.4 us
    all_gather x1, blocking collectives, per_device(): lax.all_gather(w_proj.astype(jnp.bfloat16), 'dp', axis=0, tiled=True)  33.7 us
    unnamed x174, local copies, waits for them, and re-layouts  33.2 us
  transfers between devices with their start and end apart: 7, of which 4 were waited for; matrix products, arithmetic and copies ran while one was open for 22% of the time, Pallas kernels for 0%

profile of v1, /device:TPU:0, one launch (start us, length us, event | category | flops | bytes accessed | tf_op | source)
XLA Modules:
  0.0 571.0 jit_solution(8868377327286479215)
XLA Ops:
  8.1 2.0 broadcast_multiply_fusion
  10.2 1.6 convert_element_type.80
  13.8 19.4 %all-gather.4.cloned.1.call-done = bf16[1600,512]{1,0:T(8,128)(2,1)} async-done(((bf16[1600,128]{1,0:T(8,128)(2,1)}), bf16[1600,512]{1,0:T(8,128)(2,1)}) %all-gather.4.cloned.1.call-update) | async-done | bytes 1638416 | tf_op jit(solution)/shard_map/all_gather | solution.py:129
  33.2 3.9 reshape.162
  37.1 16.6 %pad_slice_fusion = (bf16[16,10,10,512]{3,2,1,0:T(8,128)(2,1)S(1)}, bf16[16,10,10,512]{3,2,1,0:T(8,128)(2,1)}, bf16[16,10,10,512]{3,2,1,0:T(8,128)(2,1)}, bf16[1...) fusion(bf16[16,10,10,512]{3,2,1,0:T(8,128)(2,1)} %reshape.162), kind=kLoop, calls=%fused_computation.19 | loop fusion | bytes 14745600 | tf_op jit(solution)/shard_map/slice | solution.py:24
  53.8 4.6 concatenate.50
  58.4 4.2 concatenate.51
  62.5 4.1 concatenate.52
  66.6 4.0 concatenate.53
  70.6 4.0 concatenate.55
  74.7 4.0 concatenate.56
  78.7 4.0 concatenate.57
  82.8 2.0 concatenate.58
  84.7 3.0 constant_dynamic-update-slice_fusion.17
  90.3 1.4 constant_dynamic-update-slice_fusion.14
  91.7 1.4 constant_dynamic-update-slice_fusion.13
  95.7 1.4 constant_dynamic-update-slice_fusion.10
  97.1 1.3 constant_dynamic-update-slice_fusion.9
  98.4 7.8 %multiply_reduce_fusion.6 = (f32[4,128]{1,0:T(4,128)S(1)}, f32[4,128]{1,0:T(4,128)S(1)}, f32[4,400,128]{2,1,0:T(8,128)S(1)}) fusion(f32[4,400]{1,0:T(4,128)S(1)} %mul.396, bf16[4,400,4608]{2,1,0:T(8,128)(2,1)} %constant_dynamic-update-slice_fusion.9, bf16[4608,128]{1,0:T(8,128)(2,1)} %all-gather.6.cloned.1.call-done), kind=kOutput, calls=%fused_computation.41 | convolution fusion | flops 1888459776 | bytes 16754944 | tf_op jit(solution)/shard_map/dot_general | solution.py:131
  106.2 21.5 %all-reduce.4 = (f32[4]{0:T(128)S(1)}, f32[4,128]{1,0:T(4,128)S(1)}, f32[4,128]{1,0:T(4,128)S(1)}) all-reduce(f32[4]{0:T(128)S(1)} %reduce_sum.196, f32[4,128]{1,0:T(4,128)S(1)} %get-tuple-element.28, f32[4,128]{1,0:T(4,128)S(1)} %get-tuple-element.29), channel_id=1, replica_groups=mesh['dp'=8,'chan'=4] {'dp'}, use_global_device_ids=true, to_apply=%region_4.5 | all-reduce | flops 1028 | bytes 8224 | tf_op jit(solution)/shard_map/psum | solution.py:37
  129.0 2.0 reshape.166
  131.6 33.7 %all_gather.18 = bf16[512,512]{1,0:T(8,128)(2,1)} all-gather(bf16[64,512]{1,0:T(8,128)(2,1)S(1)} %convert_element_type.82), channel_id=1, replica_groups=mesh['dp'=8,'chan'=4] {'dp'}, dimensions={0}, use_global_device_ids=true | all-gather | bytes 589824 | tf_op jit(solution)/shard_map/all_gather | solution.py:115
  165.3 34.4 %all_gather.19 = bf16[512,1000]{1,0:T(8,128)(2,1)} all-gather(bf16[64,1000]{1,0:T(8,128)(2,1)S(1)} %convert_element_type.85), channel_id=1, replica_groups=mesh['dp'=8,'chan'=4] {'dp'}, dimensions={0}, use_global_device_ids=true | all-gather | bytes 1152000 | tf_op jit(solution)/shard_map/all_gather | solution.py:116
  200.5 2.5 fusion.28
  203.0 1.9 reshape.165
  206.1 33.9 %all-reduce.3 = (f32[4,512]{1,0:T(4,128)}, f32[4,512]{1,0:T(4,128)}) all-reduce(f32[4,512]{1,0:T(4,128)} %get-tuple-element.25, f32[4,512]{1,0:T(4,128)} %get-tuple-element.24), channel_id=1, replica_groups=mesh['dp'=8,'chan'=4] {'dp'}, use_global_device_ids=true, to_apply=%region_10.11 | all-reduce | flops 4096 | bytes 32768 | tf_op jit(solution)/shard_map/psum | solution.py:37
  240.0 1.4 add_rsqrt_fusion
  242.6 1.4 mul.425
  245.3 1.4 sub.91
  246.7 3.9 multiply_reduce_fusion.1
  252.1 11.9 %psum.92 = f32[16,1000]{1,0:T(8,128)} all-reduce(f32[16,1000]{1,0:T(8,128)} %fusion.15), channel_id=1, replica_groups=mesh['dp'=8,'chan'=4] {'chan'}, use_global_device_ids=true, to_apply=%region_12.13 | all-reduce | flops 16000 | bytes 128000 | tf_op jit(solution)/shard_map/psum | solution.py:144
  265.0 1.6 select_reduce_fusion
  266.6 1.5 convert_reduce_fusion
  268.8 1.6 convolution_divide_fusion
  270.4 5.3 fusion.17
  275.6 1.4 reduce_sum.204
  277.0 1.4 reduce_sum.205
  278.4 1.4 reduce_sum.207
  279.8 1.4 reduce_sum.208
  281.2 3.0 broadcast_in_dim.2
  284.2 4.3 reshape.167
  288.5 33.9 %all-reduce.2 = (f32[4,512]{1,0:T(4,128)}, f32[4,512]{1,0:T(4,128)}) all-reduce(f32[4,512]{1,0:T(4,128)} %reduce_sum.208, f32[4,512]{1,0:T(4,128)} %reduce_sum.205), channel_id=1, replica_groups=mesh['dp'=8,'chan'=4] {'dp'}, use_global_device_ids=true, to_apply=%region_20.21 | all-reduce | flops 4096 | bytes 32768 | tf_op jit(solution)/shard_map/psum | solution.py:52
  322.4 4.5 fusion.1
  329.1 2.5 copy.44
  331.6 4.2 concatenate.41
  335.8 2.0 concatenate.42
  337.8 4.1 concatenate.43
  341.9 4.2 concatenate.44
  346.1 1.9 concatenate.45
  348.1 4.2 concatenate.46
  352.2 4.0 concatenate.47
  356.3 2.0 concatenate.48
  358.2 1.7 constant_dynamic-update-slice_fusion.8
  362.3 5.9 %copy-done.41 = bf16[1600,4608]{1,0:T(8,128)(2,1)} copy-done((bf16[1600,4608]{1,0:T(8,128)(2,1)}, bf16[1600,4608]{1,0:T(8,128)(2,1)S(1)}, u32[]{:S(2)}) %copy-start.41) | copy-done | bytes 14745624
  368.2 2.0 convolution_convert_fusion.3
  374.3 1.5 convolution_convert_fusion.2
  379.7 18.7 %all-reduce.1 = (f32[4,128]{1,0:T(4,128)S(1)}, f32[4,128]{1,0:T(4,128)S(1)}, f32[1000]{0:T(1024)S(1)}, f32[]{:T(128)}) all-reduce(f32[4,128]{1,0:T(4,128)S(1)} %get-tuple-element.27, f32[4,128]{1,0:T(4,128)S(1)} %get-tuple-element.26, f32[1000]{0:T(1024)S(1)} %copy-done.56, ...), channel_id=1, replica_groups=mesh['dp'=8,'chan'=4] {'dp'}, use_global_device_ids=true, to_apply=%region_25.26 | all-reduce | flops 2025 | bytes 16200 | tf_op jit(solution)/shard_map/psum | solution.py:52
  399.2 9.2 %convolution_convert_fusion = bf16[4608,128]{1,0:T(8,128)(2,1)} fusion(bf16[1600,4608]{1,0:T(8,128)(2,1)} %constant_dynamic-update-slice_fusion, bf16[1600,128]{1,0:T(8,128)(2,1)S(1)} %bitcast.70), kind=kOutput, calls=%fused_computation | convolution fusion | flops 1888026624 | bytes 16334848 | tf_op jit(solution)/shard_map/dot_general | solution.py:63
  409.2 19.3 %reduce-scatter.9.cloned.1.call-done = bf16[64,512]{1,0:T(8,128)(2,1)} async-done(((bf16[512,512]{1,0:T(8,128)(2,1)}), bf16[64,512]{1,0:T(8,128)(2,1)}) %reduce-scatter.9.cloned.1.call-update) | async-done | bytes 65552 | tf_op jit(solution)/shard_map/reduce_scatter | solution.py:177
  428.5 1.7 fusion.20
  430.2 64.0 %reduce-scatter.11.cloned.1.call-done = bf16[64,1000]{1,0:T(8,128)(2,1)} async-done(((bf16[512,1000]{1,0:T(8,128)(2,1)}), bf16[64,1000]{1,0:T(8,128)(2,1)}) %reduce-scatter.11.cloned.1.call-update) | async-done | bytes 128016 | tf_op jit(solution)/shard_map/reduce_scatter | solution.py:180
  494.2 1.9 fusion.18
  498.0 63.0 %reduce-scatter.7.cloned.1.call-done = bf16[576,128]{1,0:T(8,128)(2,1)} async-done(((bf16[4608,128]{1,0:T(8,128)(2,1)}), bf16[576,128]{1,0:T(8,128)(2,1)}) %reduce-scatter.7.cloned.1.call-update) | async-done | bytes 147472 | tf_op jit(solution)/shard_map/reduce_scatter | solution.py:174
  561.0 2.0 fusion.22
  (216 shorter events, 32.7 us)
Async XLA Ops:
  7.2 26.0 %all-gather.4.cloned.1.call-start = ((), (), s32[]{:S(2)}) async-start(), calls=%async_computation.4 | async-start | bytes 2048000 | tf_op jit(solution)/shard_map/all_gather | solution.py:129
  8.0 25.2 %copy-start.44 = (f32[1600]{0:T(1024)}, f32[1600]{0:T(1024)S(1)}, u32[]{:S(2)}) copy-start(f32[1600]{0:T(1024)S(1)} %reshape_reshape_reshape.3) | copy-start | bytes 19204
  10.1 88.3 %all-gather.6.cloned.1.call-start = ((), (), s32[]{:S(2)}) async-start(), calls=%async_computation.5 | async-start | bytes 1327104 | tf_op jit(solution)/shard_map/all_gather | solution.py:114
  11.8 188.6 %all-gather.8.cloned.1.call-start = ((), (), s32[]{:S(2)}) async-start(), calls=%async_computation.6 | async-start | bytes 2048000 | tf_op jit(solution)/shard_map/all_gather | solution.py:134
  12.6 115.2 %copy-start.60 = (f32[128]{0:T(128)}, f32[128]{0:T(128)S(1)}, u32[]{:S(2)}) copy-start(f32[128]{0:T(128)S(1)} %get-tuple-element.80) | copy-start | bytes 1540
  12.6 115.2 %copy-start.62 = (f32[128]{0:T(128)}, f32[128]{0:T(128)S(1)}, u32[]{:S(2)}) copy-start(f32[128]{0:T(128)S(1)} %get-tuple-element.81) | copy-start | bytes 1540
  13.5 19.7 %copy-start.57 = (f32[16]{0:T(128)}, f32[16]{0:T(128)S(1)}, u32[]{:S(2)}) copy-start(f32[16]{0:T(128)S(1)} %convert_reduce_fusion.1) | copy-start | bytes 196
  53.8 29.0 %copy-start = (bf16[16,10,10,512]{3,2,1,0:T(8,128)(2,1)}, bf16[16,10,10,512]{3,2,1,0:T(8,128)(2,1)S(1)}, u32[]{:S(2)}) copy-start(bf16[16,10,10,512]{3,2,1,0:T(8,128)(2,1)S(1)} %get-tuple-element.68) | copy-start | bytes 4915204
  84.7 3.0 copy-start.23
  84.7 4.3 copy-start.22
  90.3 2.7 copy-start.17
  98.4 30.6 %copy-start.30 = (f32[64,512]{1,0:T(8,128)S(1)}, f32[64,512]{1,0:T(8,128)}, u32[]{:S(2)}) copy-start(f32[64,512]{1,0:T(8,128)} %param.27) | copy-start | bytes 393220
  98.4 30.6 %copy-start.24 = (bf16[1600,512]{1,0:T(8,128)(2,1)S(1)}, bf16[1600,512]{1,0:T(8,128)(2,1)}, u32[]{:S(2)}) copy-start(bf16[1600,512]{1,0:T(8,128)(2,1)} %param.23) | copy-start | bytes 4915204
  106.2 24.8 %copy-start.8 = (f32[4,400,128]{2,1,0:T(8,128)}, f32[4,400,128]{2,1,0:T(8,128)S(1)}, u32[]{:S(2)}) copy-start(f32[4,400,128]{2,1,0:T(8,128)S(1)} %get-tuple-element.82) | copy-start | bytes 2457604
  127.7 72.0 %copy-start.66 = (f32[4]{0:T(128)}, f32[4]{0:T(128)S(1)}, u32[]{:S(2)}) copy-start(f32[4]{0:T(128)S(1)} %get-tuple-element.40) | copy-start | bytes 52
  127.8 3.2 copy-start.29
  128.9 248.9 %reduce-scatter.13.cloned.1.call-start = ((), (), s32[]{:S(2)}) async-start(), calls=%async_computation.10 | async-start | bytes 2129920
  246.7 4.5 copy-start.7
  246.7 4.5 copy-start.58
  265.0 3.1 copy-start.64
  270.4 5.3 copy-start.32
  284.2 38.2 %copy-start.45 = (f32[1600]{0:T(1024)S(1)}, f32[1600]{0:T(1024)}, u32[]{:S(2)}) copy-start(f32[1600]{0:T(1024)} %copy-done.44) | copy-start | bytes 19204
  322.3 5.6 copy-start.27
  331.5 4.3 copy-start.3
  331.6 96.9 %reduce-scatter.9.cloned.1.call-start = ((), (), s32[]{:S(2)}) async-start(), calls=%async_computation.8 | async-start | bytes 589824 | tf_op jit(solution)/shard_map/reduce_scatter | solution.py:177
  337.8 8.3 %copy-start.2 = (bf16[16,10,10,512]{3,2,1,0:T(8,128)(2,1)S(1)}, bf16[16,10,10,512]{3,2,1,0:T(8,128)(2,1)}, u32[]{:S(2)}) copy-start(bf16[16,10,10,512]{3,2,1,0:T(8,128)(2,1)} %get-tuple-element.72) | copy-start | bytes 4915204
  348.0 8.2 %copy-start.1 = (bf16[16,10,10,512]{3,2,1,0:T(8,128)(2,1)S(1)}, bf16[16,10,10,512]{3,2,1,0:T(8,128)(2,1)}, u32[]{:S(2)}) copy-start(bf16[16,10,10,512]{3,2,1,0:T(8,128)(2,1)} %copy-done) | copy-start | bytes 4915204
  361.7 6.5 %copy-start.6 = (bf16[1600,512]{1,0:T(8,128)(2,1)S(1)}, bf16[1600,512]{1,0:T(8,128)(2,1)}, u32[]{:S(2)}) copy-start(bf16[1600,512]{1,0:T(8,128)(2,1)} %all-gather.8.cloned.1.call-done) | copy-start | bytes 4915204
  361.7 6.5 %copy-start.26 = (bf16[1600,512]{1,0:T(8,128)(2,1)S(1)}, bf16[1600,512]{1,0:T(8,128)(2,1)}, u32[]{:S(2)}) copy-start(bf16[1600,512]{1,0:T(8,128)(2,1)} %copy-done.25) | copy-start | bytes 4915204
  362.2 8.1 %copy-start.13 = (bf16[1600,512]{1,0:T(8,128)(2,1)S(1)}, bf16[1600,512]{1,0:T(8,128)(2,1)}, u32[]{:S(2)}) copy-start(bf16[1600,512]{1,0:T(8,128)(2,1)} %concatenate.45) | copy-start | bytes 4915204
  362.3 5.9 %copy-start.41 = (bf16[1600,4608]{1,0:T(8,128)(2,1)}, bf16[1600,4608]{1,0:T(8,128)(2,1)S(1)}, u32[]{:S(2)}) copy-start(bf16[1600,4608]{1,0:T(8,128)(2,1)S(1)} %constant_dynamic-update-slice_fusion.4) | copy-start | bytes 44236804
  368.2 3.4 copy-start.12
  370.2 123.9 %reduce-scatter.11.cloned.1.call-start = ((), (), s32[]{:S(2)}) async-start(), calls=%async_computation.9 | async-start | bytes 1179648 | tf_op jit(solution)/shard_map/reduce_scatter | solution.py:180
  372.9 3.0 copy-start.10
  374.2 3.0 copy-start.65
  374.2 3.0 copy-start.69
  374.2 3.0 copy-start.75
  374.3 4.8 copy-start.9
  374.3 4.8 copy-start.49
  374.3 4.8 copy-start.51
  374.3 4.8 copy-start.61
  374.3 4.8 copy-start.63
  375.8 3.8 copy-start.56
  375.8 22.6 %copy-start.67 = (f32[4]{0:T(128)S(1)}, f32[4]{0:T(128)}, u32[]{:S(2)}) copy-start(f32[4]{0:T(128)} %copy-done.66) | copy-start | bytes 52
  375.9 185.1 %reduce-scatter.7.cloned.1.call-start = ((), (), s32[]{:S(2)}) async-start(), calls=%async_computation.7 | async-start | bytes 1327104 | tf_op jit(solution)/shard_map/reduce_scatter | solution.py:174
  399.1 9.4 %copy-start.53 = (f32[4,512]{1,0:T(4,128)S(1)}, f32[4,512]{1,0:T(4,128)}, u32[]{:S(2)}) copy-start(f32[4,512]{1,0:T(4,128)} %get-tuple-element.36) | copy-start | bytes 24580
  399.1 9.4 %copy-start.52 = (f32[4,512]{1,0:T(4,128)S(1)}, f32[4,512]{1,0:T(4,128)}, u32[]{:S(2)}) copy-start(f32[4,512]{1,0:T(4,128)} %get-tuple-element.37) | copy-start | bytes 24580
  399.1 9.4 %copy-start.55 = (f32[2,512]{1,0:T(2,128)S(1)}, f32[2,512]{1,0:T(2,128)}, u32[]{:S(2)}) copy-start(f32[2,512]{1,0:T(2,128)} %param.31) | copy-start | bytes 12292
  399.1 9.4 %copy-start.70 = (f32[2,512]{1,0:T(2,128)S(1)}, f32[2,512]{1,0:T(2,128)}, u32[]{:S(2)}) copy-start(f32[2,512]{1,0:T(2,128)} %param.42) | copy-start | bytes 12292
  399.1 9.4 %copy-start.71 = (f32[2,512]{1,0:T(2,128)S(1)}, f32[2,512]{1,0:T(2,128)}, u32[]{:S(2)}) copy-start(f32[2,512]{1,0:T(2,128)} %param.43) | copy-start | bytes 12292
  399.1 29.4 %copy-start.31 = (f32[64,512]{1,0:T(8,128)S(1)}, f32[64,512]{1,0:T(8,128)}, u32[]{:S(2)}) copy-start(f32[64,512]{1,0:T(8,128)} %param.27) | copy-start | bytes 393220
  399.1 29.4 %copy-start.42 = (f32[64,512]{1,0:T(8,128)S(1)}, f32[64,512]{1,0:T(8,128)}, u32[]{:S(2)}) copy-start(f32[64,512]{1,0:T(8,128)} %param.34) | copy-start | bytes 393220
  399.2 29.4 %copy-start.43 = (f32[64,512]{1,0:T(8,128)S(1)}, f32[64,512]{1,0:T(8,128)}, u32[]{:S(2)}) copy-start(f32[64,512]{1,0:T(8,128)} %param.35) | copy-start | bytes 393220
  399.2 95.0 %copy-start.39 = (f32[64,1000]{1,0:T(8,128)S(1)}, f32[64,1000]{1,0:T(8,128)}, u32[]{:S(2)}) copy-start(f32[64,1000]{1,0:T(8,128)} %param.36) | copy-start | bytes 768004
  399.2 95.0 %copy-start.40 = (f32[64,1000]{1,0:T(8,128)S(1)}, f32[64,1000]{1,0:T(8,128)}, u32[]{:S(2)}) copy-start(f32[64,1000]{1,0:T(8,128)} %param.37) | copy-start | bytes 768004
  408.3 88.4 %copy-start.74 = (f32[2,128]{1,0:T(2,128)S(1)}, f32[2,128]{1,0:T(2,128)}, u32[]{:S(2)}) copy-start(f32[2,128]{1,0:T(2,128)} %param.30) | copy-start | bytes 3076
  408.3 88.4 %copy-start.76 = (f32[2,128]{1,0:T(2,128)S(1)}, f32[2,128]{1,0:T(2,128)}, u32[]{:S(2)}) copy-start(f32[2,128]{1,0:T(2,128)} %param.40) | copy-start | bytes 3076
  408.3 88.5 %copy-start.77 = (f32[2,128]{1,0:T(2,128)S(1)}, f32[2,128]{1,0:T(2,128)}, u32[]{:S(2)}) copy-start(f32[2,128]{1,0:T(2,128)} %param.41) | copy-start | bytes 3076
  408.3 89.1 %copy-start.47 = (f32[1000]{0:T(1024)S(1)}, f32[1000]{0:T(1024)}, u32[]{:S(2)}) copy-start(f32[1000]{0:T(1024)} %param.29) | copy-start | bytes 12004
  408.4 89.1 %copy-start.72 = (f32[1000]{0:T(1024)S(1)}, f32[1000]{0:T(1024)}, u32[]{:S(2)}) copy-start(f32[1000]{0:T(1024)} %param.38) | copy-start | bytes 12004
  408.4 89.0 %copy-start.73 = (f32[1000]{0:T(1024)S(1)}, f32[1000]{0:T(1024)}, u32[]{:S(2)}) copy-start(f32[1000]{0:T(1024)} %param.39) | copy-start | bytes 12004
  408.4 152.6 %copy-start.28 = (f32[576,128]{1,0:T(8,128)S(1)}, f32[576,128]{1,0:T(8,128)}, u32[]{:S(2)}) copy-start(f32[576,128]{1,0:T(8,128)} %param.26) | copy-start | bytes 884740
  408.4 152.6 %copy-start.37 = (f32[576,128]{1,0:T(8,128)S(1)}, f32[576,128]{1,0:T(8,128)}, u32[]{:S(2)}) copy-start(f32[576,128]{1,0:T(8,128)} %param.32) | copy-start | bytes 884740
  408.4 152.6 %copy-start.38 = (f32[576,128]{1,0:T(8,128)S(1)}, f32[576,128]{1,0:T(8,128)}, u32[]{:S(2)}) copy-start(f32[576,128]{1,0:T(8,128)} %param.33) | copy-start | bytes 884740
  (21 other events, 40.3 us)
Sparse Core Ops, SparseCore 0:
  10.2 22.9 all-gather.3
  35.9 41.0 all-gather.5
  129.0 16.5 all-gather.7
  331.7 25.0 reduce-scatter.12
  370.3 58.1 reduce-scatter.8
  431.8 62.3 reduce-scatter.10
  497.9 63.0 reduce-scatter.6

commit v2 on v1

--- a/solution.py
+++ b/solution.py
@@ -1,6 +1,10 @@
+import functools
+
 import jax
 import jax.numpy as jnp
 from jax import lax
+from jax.experimental import pallas as pl
+from jax.experimental.pallas import tpu as pltpu
 from jax.sharding import PartitionSpec as P
 
 SIDE = 10
@@ -223,6 +227,754 @@
     )
 
 
+MESH = pl.DeviceIdType.MESH
+AREA = SIDE * SIDE
+PAD = 16
+BF = jnp.bfloat16
+F32 = jnp.float32
+
+
+def flip(value, bits):
+    bit = 1
+    while bit <= bits:
+        if bits & bit:
+            value = value + bit - 2 * bit * (lax.div(value, bit) % 2)
+        bit *= 2
+    return value
+
+
+def nt_dot(left, right):
+    return lax.dot_general(left, right, (((1,), (1,)), ((), ())), preferred_element_type=F32)
+
+
+def mm(left, right):
+    return jnp.dot(left, right, preferred_element_type=F32)
+
+
+def sigmoid(value):
+    return 1.0 / (1.0 + jnp.exp(-value))
+
+
+def row_iota(shape):
+    return lax.broadcasted_iota(jnp.int32, shape, 0)
+
+
+def lane_iota(shape):
+    return lax.broadcasted_iota(jnp.int32, shape, 1)
+
+
+def fused_kernel(dims, *refs):
+    nd, nc, pm, imb, c1l, c2l, r1, rp, rc, classes, total_images = dims
+    (
+        feat, short, masks, labels, wconv, wproj, wcls, cbias, n1, n2,
+        gconv, gproj, gcls, gbias, gone, gtwo, gloss,
+        wf, pf, cf, wfull, pfull, cfull, xv, sv, xm, xt, yb, hid, mk, edge, cntm, cnti,
+        af, at, sec, slp, bn1, bn2, tsum, pool, lgt, dlm, dpd, dsb, da, dab, sr, es, er,
+        du, dhp, acc, pacc, st0, st1, st2, st3, st4,
+        gcs, gcx, gcz, gcr, gps, gpx, gpz, gpr, dla, pla, plt,
+        ld_s, cw_s, cw_r, pw_s, pw_r, kw_s, kw_r, fx_s, fx_r, af_s, af_r, s0_s, s0_r, s1_s, s1_r,
+        s2_s, s2_r, s3_s, s3_r, s4_s, s4_r, lg_s, lg_r, sr_s, sr_r, er_s, er_r,
+        dl_s, dl_r, pl_s, pl_r, gcx_s, gcx_r, gcz_s, gcz_r, gpx_s, gpx_r, gpz_s, gpz_r,
+    ) = refs
+    nz = nd // 2
+    c1 = c1l * nc
+    nq = c2l // 128
+    d = lax.axis_index("dp")
+    c = lax.axis_index("chan")
+    z, x = lax.div(d, 2), d % 2
+    y, k = lax.div(c, 2), c % 2
+    sib = y * 2 + 1 - k
+    opp = (1 - y) * 2 + k
+    dia = (1 - y) * 2 + 1 - k
+    xdev = (z * 2 + 1 - x, c)
+    sibdev = (d, sib)
+    oppdev = (d, opp)
+
+    def zdev(j):
+        return (flip(z, j) * 2 + x, c)
+
+    def remote(src, dst, ssem, rsem, dev):
+        return pltpu.make_async_remote_copy(
+            src_ref=src, dst_ref=dst, send_sem=ssem, recv_sem=rsem,
+            device_id=dev, device_id_type=MESH,
+        )
+
+    def unit(buf, u, rows):
+        return buf.at[pl.ds(pl.multiple_of(u * rows, rows), rows)]
+
+    def gather_start(buf, rows, ss, rr):
+        mine = unit(buf, d, rows)
+        remote(mine, mine, ss.at[0], rr.at[d], xdev).start()
+        for j in range(1, nz):
+            remote(mine, mine, ss.at[j], rr.at[d], zdev(j)).start()
+
+    def gather_forward(buf, rows, ss, rr, j):
+        u = flip(z, j) * 2 + x
+        got = unit(buf, u, rows)
+        copy = remote(got, got, ss.at[nz + j], rr.at[u], xdev)
+        copy.wait_recv()
+        copy.start()
+
+    def gather_finish(buf, rows, ss, rr):
+        for j in range(nz):
+            u = flip(z, j) * 2 + 1 - x
+            got = unit(buf, u, rows)
+            remote(got, got, ss.at[0], rr.at[u], xdev).wait_recv()
+
+    def gather_drain(buf, rows, ss, rr):
+        mine = unit(buf, d, rows)
+        for j in range(2 * nz):
+            if j != nz:
+                remote(mine, mine, ss.at[j], rr.at[d], xdev).wait_send()
+
+    def peers():
+        return [flip(d, p) for p in range(1, nd)]
+
+    def stats_send(buf, ss, rr):
+        for p in range(1, nd):
+            u = flip(d, p)
+            remote(buf.at[d], buf.at[d], ss.at[p], rr.at[d], (u, c)).start()
+
+    def stats_wait(buf, ss, rr):
+        for p in range(1, nd):
+            u = flip(d, p)
+            remote(buf.at[u], buf.at[u], ss.at[p], rr.at[u], (u, c)).wait_recv()
+
+    def stats_sum(buf):
+        total = buf[0]
+        for p in range(1, nd):
+            total = total + buf[p]
+        return total
+
+    def stats_drain(buf, ss, rr):
+        for p in range(1, nd):
+            u = flip(d, p)
+            remote(buf.at[d], buf.at[d], ss.at[p], rr.at[d], (u, c)).wait_send()
+
+    def rows(m):
+        return pl.ds(pl.multiple_of(m * pm, pm), pm)
+
+    def lanes(chunk):
+        return pl.ds(pl.multiple_of(chunk * c1l, c1l), c1l)
+
+    def part(buf, m, chunk):
+        return buf.at[rows(m), lanes(chunk)]
+
+    def local(src, dst, i):
+        return pltpu.make_async_copy(src, dst, ld_s.at[i])
+
+    loads = [
+        local(wconv, wf, 0),
+        local(wproj, pf, 1),
+        local(wcls, cf, 2),
+        local(feat, xv.at[:, lanes(c)], 3),
+        local(short, sv, 4),
+    ]
+    for load in loads:
+        load.start()
+
+    barrier = pltpu.get_barrier_semaphore()
+    others = [(u, c) for u in peers()] + [sibdev, oppdev, (d, dia)]
+    for dev in others:
+        pl.semaphore_signal(barrier, inc=1, device_id=dev, device_id_type=MESH)
+    loads[0].wait()
+    wfull[pl.ds(pl.multiple_of(d * r1, r1), r1), :] = wf[...].astype(BF)
+    pl.semaphore_wait(barrier, len(others))
+
+    gather_start(wfull, r1, cw_s, cw_r)
+    for m in range(MICRO):
+        src = feat.at[pl.ds(m * pm, pm)]
+        remote(src, part(xv, m, c), fx_s.at[0, m], fx_r.at[c, m], oppdev).start()
+        remote(src, part(xv, m, c), fx_s.at[1, m], fx_r.at[c, m], sibdev).start()
+
+    loads[1].wait()
+    pfull[pl.ds(pl.multiple_of(d * rp, rp), rp), :] = pf[...].astype(BF)
+    loads[2].wait()
+    cfull[pl.ds(pl.multiple_of(d * rc, rc), rc), :] = cf[...].astype(BF)
+
+    pixel = row_iota((pm, 128))
+    image = jnp.zeros((pm, 128), jnp.int32)
+    for i in range(1, imb):
+        image = image + (pixel >= AREA * i).astype(jnp.int32)
+    pixel = pixel - AREA * image
+    line = jnp.zeros((pm, 128), jnp.int32)
+    for i in range(1, SIDE):
+        line = line + (pixel >= SIDE * i).astype(jnp.int32)
+    across = pixel - SIDE * line
+    edge[0] = (line > 0).astype(F32)
+    edge[1] = (line < SIDE - 1).astype(F32)
+    edge[2] = (across > 0).astype(F32)
+    edge[3] = (across < SIDE - 1).astype(F32)
+    mask_bf = masks[...].astype(F32).astype(BF)
+    images = imb * MICRO
+    chosen = (pixel[:, :AREA] == lane_iota((pm, AREA))).astype(F32)
+    ones = jnp.ones((AREA, 128), BF)
+    image_count = jnp.sum(masks[...].astype(F32), axis=1, keepdims=True)
+    for m in range(MICRO):
+        away = row_iota((pm, images)) - AREA * (lane_iota((pm, images)) - imb * m)
+        owner = jnp.where((away >= 0) & (away < AREA), 1.0, 0.0).astype(BF)
+        spread = mm((mm(owner, mask_bf) * chosen).astype(BF), ones)
+        mk[m] = spread
+        cntm[m] = jnp.sum(spread, axis=0, keepdims=True)
+        cnti[m] = jnp.broadcast_to(image_count[m * imb : (m + 1) * imb], (imb, 128))
+        st0[d, m : m + 1, :] = cntm[m]
+    stats_send(st0, s0_s, s0_r)
+
+    yb[:, 0:PAD, :] = jnp.zeros((9, PAD, c1l), F32)
+    yb[:, PAD + pm :, :] = jnp.zeros((9, PAD, c1l), F32)
+    dhp[0:PAD, :] = jnp.zeros((PAD, c1l), F32)
+    dhp[PAD + pm :, :] = jnp.zeros((PAD, c1l), F32)
+
+    for m in range(MICRO):
+        got = part(xv, m, opp)
+        copy = remote(got, got, fx_s.at[2, m], fx_r.at[opp, m], sibdev)
+        copy.wait_recv()
+        copy.start()
+        if 1 <= m < nz:
+            gather_forward(wfull, r1, cw_s, cw_r, m)
+    for j in range(MICRO, nz):
+        gather_forward(wfull, r1, cw_s, cw_r, j)
+    loads[3].wait()
+
+    def take_features(m, carry):
+        for chunk in (sib, dia):
+            got = part(xv, m, chunk)
+            remote(got, got, fx_s.at[2, m], fx_r.at[chunk, m], sibdev).wait_recv()
+        flat_mask = mk[m].astype(BF)
+        for q in range(nc):
+            piece = xv[rows(m), q * c1l : (q + 1) * c1l] * flat_mask
+            xm[m, :, q * c1l : (q + 1) * c1l] = piece
+            xt[m, q * c1l : (q + 1) * c1l, :] = piece.T
+        return carry
+
+    lax.fori_loop(0, MICRO, take_features, 0)
+    gather_finish(wfull, r1, cw_s, cw_r)
+    gather_start(pfull, rp, pw_s, pw_r)
+
+    def tap(t):
+        return wfull[t * c1 : (t + 1) * c1, :]
+
+    def edges(ky, kx):
+        found = None
+        if ky == 0:
+            found = edge[0]
+        if ky == 2:
+            found = edge[1]
+        if kx == 0:
+            found = edge[2] if found is None else found * edge[2]
+        if kx == 2:
+            found = edge[3] if found is None else found * edge[3]
+        return found
+
+    def conv(m, carry):
+        inputs = xm[m]
+        for t in range(0, 9, 2):
+            if t < 8:
+                pair = mm(inputs, jnp.concatenate([tap(t), tap(t + 1)], axis=1))
+                yb[t, PAD : PAD + pm, :] = pair[:, :c1l]
+                yb[t + 1, PAD : PAD + pm, :] = pair[:, c1l:]
+            else:
+                yb[t, PAD : PAD + pm, :] = mm(inputs, tap(t))
+        hidden = None
+        for kx in range(3):
+            column = None
+            for ky in range(3):
+                off = PAD + (ky - 1) * SIDE + kx - 1
+                value = yb[3 * ky + kx, off : off + pm, :]
+                if ky != 1:
+                    value = value * edge[0 if ky == 0 else 1]
+                column = value if column is None else column + value
+            if kx != 1:
+                column = column * edge[2 if kx == 0 else 3]
+            hidden = column if hidden is None else hidden + column
+        hid[m] = hidden
+        valid = hidden * mk[m]
+        st1[d, pl.ds(m, 1), :] = jnp.sum(valid, axis=0, keepdims=True)
+        st1[d, pl.ds(MICRO + m, 1), :] = jnp.sum(valid * hidden, axis=0, keepdims=True)
+        return carry
+
+    lax.fori_loop(0, MICRO, conv, 0)
+    stats_send(st1, s1_s, s1_r)
+    for j in range(1, nz):
+        gather_forward(pfull, rp, pw_s, pw_r, j)
+    acc[...] = jnp.zeros_like(acc)
+    pacc[...] = jnp.zeros_like(pacc)
+
+    stats_wait(st0, s0_s, s0_r)
+    counts = stats_sum(st0)
+    stats_wait(st1, s1_s, s1_r)
+    totals = stats_sum(st1)
+    for m in range(MICRO):
+        n = counts[m : m + 1, :]
+        cntm[m] = n
+        center = totals[m : m + 1, :] / n
+        spread = totals[MICRO + m : MICRO + m + 1, :] / n - center * center
+        bn1[m, 0:1, :] = center
+        bn1[m, 1:2, :] = lax.rsqrt(spread + norm_eps)
+
+    def activate(m, carry):
+        normed = (hid[m] - bn1[m, 0:1, :]) * bn1[m, 1:2, :]
+        shifted = n1[0:1, :] * normed + n1[1:2, :]
+        active = (shifted * sigmoid(shifted) * mk[m]).astype(BF)
+        mine = part(af, m, c)
+        mine[...] = active
+        remote(mine, mine, af_s.at[0, m], af_r.at[c, m], oppdev).start()
+        remote(mine, mine, af_s.at[1, m], af_r.at[c, m], sibdev).start()
+        return carry
+
+    lax.fori_loop(0, MICRO, activate, 0)
+    gather_start(cfull, rc, kw_s, kw_r)
+    gather_finish(pfull, rp, pw_s, pw_r)
+    loads[4].wait()
+
+    def turn(m, chunk):
+        at[m, lanes_sub(chunk), :] = part(af, m, chunk)[...].T
+
+    def lanes_sub(chunk):
+        return pl.ds(pl.multiple_of(chunk * c1l, c1l), c1l)
+
+    def stage_a(m):
+        got = part(af, m, opp)
+        copy = remote(got, got, af_s.at[2, m], af_r.at[opp, m], sibdev)
+        copy.wait_recv()
+        copy.start()
+        turn(m, c)
+        turn(m, opp)
+        got = part(af, m, sib)
+        remote(got, got, af_s.at[2, m], af_r.at[sib, m], sibdev).wait_recv()
+        turn(m, sib)
+        got = part(af, m, dia)
+        remote(got, got, af_s.at[2, m], af_r.at[dia, m], sibdev).wait_recv()
+        turn(m, dia)
+        second = mm(af[rows(m), :], pfull[...])
+        sec[m] = second
+        mask = mk[m]
+        for q in range(nq):
+            piece = second[:, q * 128 : (q + 1) * 128]
+            valid = piece * mask
+            st2[m, d, q : q + 1, :] = jnp.sum(valid, axis=0, keepdims=True)
+            st2[m, d, nq + q : nq + q + 1, :] = jnp.sum(valid * piece, axis=0, keepdims=True)
+        stats_send(st2.at[m], s2_s.at[m], s2_r.at[m])
+
+    low_half = row_iota((2, 8, 128)) * 0 + lax.broadcasted_iota(jnp.int32, (2, 8, 128), 1)
+    tiles = AREA // 4
+    half = tiles // 2
+
+    def image_sums(value):
+        value = value.reshape(imb // 2, tiles, 8, 128)
+        middle = value[:, half]
+        first = jnp.sum(value[:, :half], axis=1) + jnp.where(low_half < 4, middle, 0.0)
+        last = jnp.sum(value[:, half + 1 :], axis=1) + jnp.where(low_half < 4, 0.0, middle)
+        first = jnp.sum(first, axis=1)
+        last = jnp.sum(last, axis=1)
+        found = []
+        for i in range(imb // 2):
+            found += [first[i : i + 1], last[i : i + 1]]
+        return jnp.concatenate(found, axis=0)
+
+    def image_spread(value):
+        pieces = []
+        for i in range(imb // 2):
+            first = jnp.broadcast_to(value[2 * i : 2 * i + 1], (8, 128))
+            last = jnp.broadcast_to(value[2 * i + 1 : 2 * i + 2], (8, 128))
+            middle = jnp.where(low_half[0] < 4, first, last)
+            pieces.append(jnp.broadcast_to(first[None], (half, 8, 128)))
+            pieces.append(middle[None])
+            pieces.append(jnp.broadcast_to(last[None], (half, 8, 128)))
+        return jnp.concatenate(pieces, axis=0).reshape(pm, 128)
+
+    def stage_b(m):
+        stats_wait(st2.at[m], s2_s.at[m], s2_r.at[m])
+        total = stats_sum(st2.at[m])
+        n = cntm[m]
+        mask = mk[m]
+        for q in range(nq):
+            at_q = slice(q * 128, (q + 1) * 128)
+            center = total[q : q + 1] / n
+            spread = total[nq + q : nq + q + 1] / n - center * center
+            scale = lax.rsqrt(spread + norm_eps)
+            bn2[m, 0:1, at_q] = scale
+            normed = (sec[m, :, at_q] - center) * scale
+            sec[m, :, at_q] = normed
+            summed = n2[0:1, at_q] * normed + n2[1:2, at_q]
+            summed = summed + sv[rows(m), at_q].astype(F32)
+            sigma = sigmoid(summed)
+            slope = sigma * (1.0 + summed * (1.0 - sigma)) * mask
+            slp[m, :, at_q] = slope
+            pool[m, :, at_q] = (image_sums(summed * sigma * mask) / cnti[m]).astype(BF).astype(F32)
+            tsum[m, 0, :, at_q] = image_sums(slope)
+            tsum[m, 1, :, at_q] = image_sums(slope * normed)
+        lgt[m, c] = mm(pool[m].astype(BF), cfull[...])
+        for dev, i in ((sibdev, 0), (oppdev, 1), ((d, dia), 2)):
+            remote(lgt.at[m, c], lgt.at[m, c], lg_s.at[i, m], lg_r.at[c, m], dev).start()
+
+    def stage_c(m):
+        for i, chunk in enumerate((sib, opp, dia)):
+            got = lgt.at[m, chunk]
+            remote(got, got, lg_s.at[i, m], lg_r.at[chunk, m], sibdev).wait_recv()
+        logits = lgt[m, 0]
+        for q in range(1, nc):
+            logits = logits + lgt[m, q]
+        logits = logits + cbias[...]
+        top = jnp.max(logits, axis=1, keepdims=True)
+        expo = jnp.exp(logits - top)
+        expo_sum = jnp.sum(expo, axis=1, keepdims=True)
+        image_row = row_iota((imb, classes))
+        target = jnp.zeros((imb, classes), jnp.int32)
+        for i in range(imb):
+            target = jnp.where(image_row == i, labels[m * imb + i], target)
+        onehot = (target == lane_iota((imb, classes))).astype(F32)
+        picked = jnp.sum(logits * onehot, axis=1, keepdims=True)
+        loss = jnp.sum(top + jnp.log(expo_sum) - picked, axis=0, keepdims=True)
+        st4[m, d, 2:3, :] = jnp.broadcast_to(loss, (1, 128))
+        dlogits = ((expo / expo_sum - onehot) / total_images).astype(BF)
+        dlm[m] = dlogits.astype(F32)
+        spread = nt_dot(dlogits, cfull[...])
+        for q in range(nq):
+            at_q = slice(q * 128, (q + 1) * 128)
+            value = spread[:, at_q] / cnti[m]
+            dpd[m, :, at_q] = value
+            st3[m, d, q : q + 1, :] = jnp.sum(value * tsum[m, 0, :, at_q], axis=0, keepdims=True)
+            st3[m, d, nq + q : nq + q + 1, :] = jnp.sum(
+                value * tsum[m, 1, :, at_q], axis=0, keepdims=True
+            )
+        stats_send(st3.at[m], s3_s.at[m], s3_r.at[m])
+
+    def stage_d(m):
+        stats_wait(st3.at[m], s3_s.at[m], s3_r.at[m])
+        total = stats_sum(st3.at[m])
+        n = cntm[m]
+        mask = mk[m]
+        for q in range(nq):
+            at_q = slice(q * 128, (q + 1) * 128)
+            gain = n2[0:1, at_q] * bn2[m, 0:1, at_q]
+            base = gain * total[q : q + 1] / n
+            ramp = gain * total[nq + q : nq + q + 1] / n
+            value = image_spread(gain * dpd[m, :, at_q]) * slp[m, :, at_q]
+            value = value - mask * (base + ramp * sec[m, :, at_q])
+            dsb[:, at_q] = value.astype(BF)
+        for q in range(nq):
+            at_q = slice(q * 128, (q + 1) * 128)
+            bn2[m, 1:2, at_q] = total[nq + q : nq + q + 1]
+            bn2[m, 2:3, at_q] = total[q : q + 1]
+        back = nt_dot(dsb[...], pfull[...])
+        for q in range(nc):
+            piece = back[:, q * c1l : (q + 1) * c1l]
+            da[m, q] = piece
+            dab[m, q] = piece.astype(BF)
+        for i, chunk in ((0, sib), (1, dia)):
+            remote(dab.at[m, chunk], sr.at[m, i], sr_s.at[i, m], sr_r.at[i, m], sibdev).start()
+        pacc[...] += mm(at[m], dsb[...])
+
+    def stage_e(m):
+        for i in (1, 0):
+            remote(sr.at[m, i], sr.at[m, i], sr_s.at[i, m], sr_r.at[i, m], sibdev).wait_recv()
+            if i == 1:
+                es[m] = (da[m, opp] + sr[m, 1].astype(F32)).astype(BF)
+                remote(es.at[m], er.at[m], er_s.at[m], er_r.at[m], oppdev).start()
+        da[m, c] = da[m, c] + sr[m, 0].astype(F32)
+
+    def stage_f(m):
+        remote(es.at[m], er.at[m], er_s.at[m], er_r.at[m], oppdev).wait_recv()
+        upstream = da[m, c] + er[m].astype(F32)
+        normed = (hid[m] - bn1[m, 0:1, :]) * bn1[m, 1:2, :]
+        shifted = n1[0:1, :] * normed + n1[1:2, :]
+        sigma = sigmoid(shifted)
+        upstream = upstream * mk[m] * (sigma * (1.0 + shifted * (1.0 - sigma)))
+        du[m] = upstream
+        st4[m, d, 0:1, :] = jnp.sum(upstream, axis=0, keepdims=True)
+        st4[m, d, 1:2, :] = jnp.sum(upstream * normed, axis=0, keepdims=True)
+        stats_send(st4.at[m], s4_s.at[m], s4_r.at[m])
+
+    def stage_g(m):
+        stats_wait(st4.at[m], s4_s.at[m], s4_r.at[m])
+        total = stats_sum(st4.at[m])
+        n = cntm[m]
+        bn1[m, 2:3, :] = total[1:2]
+        bn1[m, 3:4, :] = total[0:1]
+        bn1[m, 4:5, :] = total[2:3]
+        normed = (hid[m] - bn1[m, 0:1, :]) * bn1[m, 1:2, :]
+        gain = n1[0:1, :] * bn1[m, 1:2, :]
+        value = mk[m] * gain * (du[m] - (total[0:1] + normed * total[1:2]) / n)
+        dhp[PAD : PAD + pm, :] = value.astype(BF).astype(F32)
+
+        def shifted(t):
+            ky, kx = t // 3, t % 3
+            off = PAD - (ky - 1) * SIDE - (kx - 1)
+            piece = dhp[off : off + pm, :]
+            found = edges(2 - ky, 2 - kx)
+            return (piece if found is None else piece * found).astype(BF)
+
+        left = xt[m]
+        for t in range(0, 9, 2):
+            if t < 8:
+                pair = mm(left, jnp.concatenate([shifted(t), shifted(t + 1)], axis=1))
+                acc[t * c1 : (t + 1) * c1, :] += pair[:, :c1l]
+                acc[(t + 1) * c1 : (t + 2) * c1, :] += pair[:, c1l:]
+            else:
+                acc[t * c1 : (t + 1) * c1, :] += mm(left, shifted(t))
+
+    def scatter_start(total, height, sbuf, xbuf, ss, rr):
+        for j in range(nz):
+            u = flip(z, j) * 2 + 1 - x
+            sbuf[j] = total[pl.ds(pl.multiple_of(u * height, height), height), :].astype(BF)
+            remote(sbuf.at[j], xbuf.at[j], ss.at[j], rr.at[j], xdev).start()
+
+    def scatter_middle(total, height, xbuf, zbuf, rbuf, xs, xr, zs, zr):
+        for j in list(range(1, nz)) + [0]:
+            remote(xbuf.at[j], xbuf.at[j], xs.at[j], xr.at[j], xdev).wait_recv()
+            u = flip(z, j) * 2 + x
+            found = total[pl.ds(pl.multiple_of(u * height, height), height), :]
+            found = found + xbuf[j].astype(F32)
+            if j == 0:
+                return found
+            zbuf[j] = found.astype(BF)
+            remote(zbuf.at[j], rbuf.at[j], zs.at[j], zr.at[j], zdev(j)).start()
+
+    def scatter_finish(found, rbuf, zs, zr):
+        for j in range(1, nz):
+            remote(rbuf.at[j], rbuf.at[j], zs.at[j], zr.at[j], zdev(j)).wait_recv()
+            found = found + rbuf[j].astype(F32)
+        return found
+
+    def scatter_drain(sbuf, zbuf, xs, xr, zs, zr):
+        for j in range(nz):
+            remote(sbuf.at[j], sbuf.at[j], xs.at[j], xr.at[j], xdev).wait_send()
+            if j > 0:
+                remote(zbuf.at[j], zbuf.at[j], zs.at[j], zr.at[j], xdev).wait_send()
+
+    stages = (stage_a, stage_b, stage_c, stage_d, stage_e, stage_f, stage_g)
+
+    def step(s, carry):
+        for i in reversed(range(len(stages))):
+            @pl.when((s >= i) & (s < i + MICRO))
+            def run(i=i):
+                stages[i](s - i)
+
+            if i == 3:
+                @pl.when(s == MICRO + 2)
+                def start_proj():
+                    scatter_start(pacc, rp, gps, gpx, gpx_s, gpx_r)
+
+            if i == 2:
+                @pl.when(s == MICRO + 1)
+                def share_cls():
+                    mine = dla.at[pl.ds(pl.multiple_of(d * images, images), images)]
+                    mine[...] = jnp.concatenate([dlm[q] for q in range(MICRO)], axis=0).astype(BF)
+                    pooled = pla.at[pl.ds(pl.multiple_of(d * images, images), images)]
+                    pooled[...] = jnp.concatenate([pool[q] for q in range(MICRO)], axis=0).astype(BF)
+                    gather_start(dla, images, dl_s, dl_r)
+                    gather_start(pla, images, pl_s, pl_r)
+
+            if i == 0:
+                @pl.when(s == 0)
+                def move_cls():
+                    for j in range(1, nz):
+                        gather_forward(cfull, rc, kw_s, kw_r, j)
+                    gather_finish(cfull, rc, kw_s, kw_r)
+
+        return carry
+
+    lax.fori_loop(0, MICRO + len(stages) - 1, step, 0)
+
+    scatter_start(acc, r1, gcs, gcx, gcx_s, gcx_r)
+
+    for j in range(1, nz):
+        gather_forward(dla, images, dl_s, dl_r, j)
+        gather_forward(pla, images, pl_s, pl_r, j)
+    proj_part = scatter_middle(pacc, rp, gpx, gpz, gpr, gpx_s, gpx_r, gpz_s, gpz_r)
+    gproj[...] = scatter_finish(proj_part, gpr, gpz_s, gpz_r)
+    gather_finish(dla, images, dl_s, dl_r)
+    gather_finish(pla, images, pl_s, pl_r)
+    plt[...] = pla[...].T
+    left = plt[pl.ds(pl.multiple_of(d * rc, rc), rc), :]
+    gcls[...] = mm(left, dla[...])
+    gbias[...] = jnp.sum(dla[...].astype(F32), axis=0, keepdims=True)
+    gone[...] = bn1[0, 2:4, :] + bn1[1, 2:4, :] + bn1[2, 2:4, :] + bn1[3, 2:4, :]
+    gtwo[...] = bn2[0, 1:3, :] + bn2[1, 1:3, :] + bn2[2, 1:3, :] + bn2[3, 1:3, :]
+    loss = bn1[0, 4:5, :] + bn1[1, 4:5, :] + bn1[2, 4:5, :] + bn1[3, 4:5, :]
+    gloss[...] = loss / total_images
+
+    conv_part = scatter_middle(acc, r1, gcx, gcz, gcr, gcx_s, gcx_r, gcz_s, gcz_r)
+    gconv[...] = scatter_finish(conv_part, gcr, gcz_s, gcz_r)
+
+    gather_drain(wfull, r1, cw_s, cw_r)
+    gather_drain(pfull, rp, pw_s, pw_r)
+    gather_drain(cfull, rc, kw_s, kw_r)
+    gather_drain(dla, images, dl_s, dl_r)
+    gather_drain(pla, images, pl_s, pl_r)
+    stats_drain(st0, s0_s, s0_r)
+    stats_drain(st1, s1_s, s1_r)
+    scatter_drain(gps, gpz, gpx_s, gpx_r, gpz_s, gpz_r)
+    scatter_drain(gcs, gcz, gcx_s, gcx_r, gcz_s, gcz_r)
+
+    def drain(m, carry):
+        for i in range(3):
+            src = part(xv, m, c)
+            remote(src, src, fx_s.at[i, m], fx_r.at[c, m], sibdev).wait_send()
+            src = part(af, m, c)
+            remote(src, src, af_s.at[i, m], af_r.at[c, m], sibdev).wait_send()
+            src = lgt.at[m, c]
+            remote(src, src, lg_s.at[i, m], lg_r.at[c, m], sibdev).wait_send()
+        for i in range(2):
+            remote(sr.at[m, i], sr.at[m, i], sr_s.at[i, m], sr_r.at[i, m], sibdev).wait_send()
+        remote(es.at[m], er.at[m], er_s.at[m], er_r.at[m], oppdev).wait_send()
+        stats_drain(st2.at[m], s2_s.at[m], s2_r.at[m])
+        stats_drain(st3.at[m], s3_s.at[m], s3_r.at[m])
+        stats_drain(st4.at[m], s4_s.at[m], s4_r.at[m])
+        return carry
+
+    lax.fori_loop(0, MICRO, drain, 0)
+
+
+def fused_gradients(
+    features, shortcut, valid_masks, labels, w_conv, w_proj, w_cls, cls_bias, norm_one, norm_two
+):
+    nd, nc = lax.axis_size("dp"), lax.axis_size("chan")
+    nz = nd // 2
+    pixels, c1l = features.shape
+    c2l = shortcut.shape[1]
+    images = valid_masks.shape[0]
+    imb, pm = images // MICRO, pixels // MICRO
+    r1, rp, rc = w_conv.shape[0], w_proj.shape[0], w_cls.shape[0]
+    classes = w_cls.shape[1]
+    c1 = c1l * nc
+    nq = c2l // 128
+    dims = (nd, nc, pm, imb, c1l, c2l, r1, rp, rc, classes, images * nd)
+    vmem = pltpu.VMEM
+    dma = pltpu.SemaphoreType.DMA
+    m4 = MICRO
+    scratch = [
+        vmem((r1, c1l), F32), vmem((rp, c2l), F32), vmem((rc, classes), F32),
+        vmem((9 * c1, c1l), BF), vmem((c1, c2l), BF), vmem((c2l, classes), BF),
+        vmem((pixels, c1), BF), vmem((pixels, c2l), BF),
+        vmem((m4, pm, c1), BF), vmem((m4, c1, pm), BF),
+        vmem((9, PAD + pm + PAD, c1l), F32), vmem((m4, pm, c1l), F32), vmem((m4, pm, 128), F32),
+        vmem((4, pm, 128), F32), vmem((m4, 1, 128), F32), vmem((m4, imb, 128), F32),
+        vmem((pixels, c1), BF), vmem((m4, c1, pm), BF),
+        vmem((m4, pm, c2l), F32), vmem((m4, pm, c2l), F32),
+        vmem((m4, 8, c1l), F32), vmem((m4, 8, c2l), F32),
+        vmem((m4, 2, imb, c2l), F32), vmem((m4, imb, c2l), F32),
+        vmem((m4, nc, imb, classes), F32), vmem((m4, imb, classes), F32), vmem((m4, imb, c2l), F32),
+        vmem((pm, c2l), BF), vmem((m4, nc, pm, c1l), F32), vmem((m4, nc, pm, c1l), BF),
+        vmem((m4, 2, pm, c1l), BF), vmem((m4, pm, c1l), BF), vmem((m4, pm, c1l), BF),
+        vmem((m4, pm, c1l), F32), vmem((PAD + pm + PAD, c1l), F32),
+        vmem((9 * c1, c1l), F32), vmem((c1, c2l), F32),
+        vmem((nd, 8, c1l), F32), vmem((nd, 8, c1l), F32),
+        vmem((m4, nd, 2 * nq, 128), F32), vmem((m4, nd, 2 * nq, 128), F32),
+        vmem((m4, nd, 8, c1l), F32),
+        vmem((nz, r1, c1l), BF), vmem((nz, r1, c1l), BF),
+        vmem((nz, r1, c1l), BF), vmem((nz, r1, c1l), BF),
+        vmem((nz, rp, c2l), BF), vmem((nz, rp, c2l), BF),
+        vmem((nz, rp, c2l), BF), vmem((nz, rp, c2l), BF),
+        vmem((nd * images, classes), BF), vmem((nd * images, c2l), BF), vmem((c2l, nd * images), BF),
+        dma((5,)),
+        dma((2 * nz,)), dma((nd,)), dma((2 * nz,)), dma((nd,)), dma((2 * nz,)), dma((nd,)),
+        dma((3, m4)), dma((nc, m4)), dma((3, m4)), dma((nc, m4)),
+        dma((nd,)), dma((nd,)), dma((nd,)), dma((nd,)),
+        dma((m4, nd)), dma((m4, nd)), dma((m4, nd)), dma((m4, nd)), dma((m4, nd)), dma((m4, nd)),
+        dma((3, m4)), dma((nc, m4)), dma((2, m4)), dma((2, m4)), dma((m4,)), dma((m4,)),
+        dma((2 * nz,)), dma((nd,)), dma((2 * nz,)), dma((nd,)),
+        dma((nz,)), dma((nz,)), dma((nz,)), dma((nz,)),
+        dma((nz,)), dma((nz,)), dma((nz,)), dma((nz,)),
+    ]
+    whole = pl.BlockSpec(memory_space=pltpu.VMEM)
+    hbm = pl.BlockSpec(memory_space=pl.ANY)
+    scalar = pl.BlockSpec(memory_space=pltpu.SMEM)
+    shape = jax.ShapeDtypeStruct
+    return pl.pallas_call(
+        functools.partial(fused_kernel, dims),
+        out_shape=(
+            shape((r1, c1l), F32), shape((rp, c2l), F32), shape((rc, classes), F32),
+            shape((1, classes), F32), shape((2, c1l), F32), shape((2, c2l), F32),
+            shape((1, 128), F32),
+        ),
+        in_specs=[hbm, hbm, whole, scalar, hbm, hbm, hbm, whole, whole, whole],
+        out_specs=(whole,) * 7,
+        scratch_shapes=scratch,
+        compiler_params=pltpu.CompilerParams(
+            collective_id=0, has_side_effects=True, vmem_limit_bytes=58 * 1024 * 1024
+        ),
+    )(
+        features, shortcut, valid_masks, labels, w_conv, w_proj, w_cls,
+        cls_bias.reshape(1, classes), norm_one, norm_two,
+    )
+
+
+def adam_kernel(*refs):
+    for i, (rate, decay) in enumerate(ADAM_RATES):
+        weight, moment, second, grad = (ref[...] for ref in refs[4 * i : 4 * i + 4])
+        outs = refs[4 * len(ADAM_RATES) + 1 + 3 * i :]
+        new_weight, new_moment, new_second = adam_step(weight, moment, second, grad, rate, decay)
+        outs[0][...] = new_weight
+        outs[1][...] = new_moment
+        outs[2][...] = new_second
+        if i < 3:
+            refs[7 * len(ADAM_RATES) + 1 + i][...] = new_weight.astype(BF)
+    refs[-1][...] = refs[4 * len(ADAM_RATES)][...]
+
+
+ADAM_RATES = (
+    (rate_matrix, weight_decay),
+    (rate_matrix, weight_decay),
+    (rate_matrix, weight_decay),
+    (rate_small, 0.0),
+    (rate_small, 0.0),
+    (rate_small, 0.0),
+)
+
+
+def fused_device(
+    features, shortcut, valid_masks, labels, w_conv, w_proj, w_cls, cls_bias, norm_one, norm_two,
+    conv_moment, conv_second, proj_moment, proj_second, cls_moment, cls_second,
+    bias_moment, bias_second, one_moment, one_second, two_moment, two_second,
+):
+    grads = fused_gradients(
+        features, shortcut, valid_masks, labels, w_conv, w_proj, w_cls, cls_bias, norm_one, norm_two
+    )
+    states = (
+        (w_conv, conv_moment, conv_second),
+        (w_proj, proj_moment, proj_second),
+        (w_cls, cls_moment, cls_second),
+        (cls_bias.reshape(1, -1), bias_moment.reshape(1, -1), bias_second.reshape(1, -1)),
+        (norm_one, one_moment, one_second),
+        (norm_two, two_moment, two_second),
+    )
+    operands, outs = [], []
+    for state, grad in zip(states, grads[:6]):
+        operands += list(state) + [grad]
+        outs += [jax.ShapeDtypeStruct(grad.shape, F32)] * 3
+    outs += [jax.ShapeDtypeStruct(grads[i].shape, BF) for i in range(3)]
+    outs.append(jax.ShapeDtypeStruct(grads[6].shape, F32))
+    whole = pl.BlockSpec(memory_space=pltpu.VMEM)
+    done = list(
+        pl.pallas_call(
+            adam_kernel,
+            out_shape=tuple(outs),
+            in_specs=[whole] * (len(operands) + 1),
+            out_specs=(whole,) * len(outs),
+            compiler_params=pltpu.CompilerParams(vmem_limit_bytes=40 * 1024 * 1024),
+        )(*operands, grads[6])
+    )
+    for i in (9, 10, 11):
+        done[i] = done[i].reshape(-1)
+    return tuple(done[:21]) + (done[21][0, 0],)
+
+
+def run_device(*args):
+    features, shortcut, valid_masks = args[:3]
+    w_cls = args[6]
+    fits = (
+        lax.axis_size("chan") == 4
+        and lax.axis_size("dp") % 2 == 0
+        and features.shape[1] == 128
+        and shortcut.shape[1] % 128 == 0
+        and w_cls.shape[0] % 16 == 0
+        and valid_masks.shape[0] % (4 * MICRO) == 0
+    )
+    return (fused_device if fits else per_device)(*args)
+
+
 def solution(mesh):
     placed = (
         P("dp", "chan"),
@@ -249,7 +1001,7 @@
         P(None, "chan"),
     )
     return jax.shard_map(
-        per_device,
+        run_device,
         mesh=mesh,
         in_specs=placed,
         out_specs=(

time: 573 us -> 134 us (0.23)
  blocking collectives: 188 us -> 0 us
  waiting for transfers between devices: 166 us -> 0 us
  local copies, waits for them, and re-layouts: 135 us -> 5.57 us
  Pallas kernels: 0 us -> 128 us
  other arithmetic: 38.8 us -> 0 us
  matrix products: 26.5 us -> 0 us
  between operations: 16.6 us -> 0.97 us
    reduce_scatter x3 -> x0, waiting for transfers between devices: 146 us -> none  [the longest x1 64 us: per_device(): lax.psum_scatter(local_cls.astype(jnp.bfloat16), 'dp', scatter_dimension=...]
    pallas_call x0 -> x2, Pallas kernels: none -> 128 us  [the longest x1 126 us: fused_gradients(): pl.pallas_call(functools.partial(fused_kernel, dims), out_shape=(shape((r...]
    psum x5 -> x0, blocking collectives: 120 us -> none  [the longest x2 55.3 us: norm_forward(): lax.psum((jnp.sum(hidden * weights, axis=1), jnp.sum(hidden * hidden * we...]
    all_gather x2 -> x0, blocking collectives: 68.1 us -> none  [the longest x1 34.4 us: per_device(): lax.all_gather(w_cls.astype(jnp.bfloat16), 'dp', axis=0, tiled=True)]
    concatenate x18 -> x0, local copies, waits for them, and re-layouts: 60.2 us -> none  [tap_columns(): jnp.concatenate(pieces, axis=3).reshape(images * SIDE * SIDE, 9 * width)]
    unnamed x174 -> x50, local copies, waits for them, and re-layouts: 33.2 us -> 5.57 us
    dot_general x8 -> x0, matrix products: 26.5 us -> none  [the longest x3 12.6 us: contract_rows(): lax.dot_general(left, right, (((0,), (0,)), ((), ())), preferred_element_...]
    all_gather x3 -> x0, waiting for transfers between devices: 19.4 us -> none  [the longest x1 19.4 us: per_device(): gathered = lax.all_gather(masked, 'chan', axis=1, tiled=True)]
  transfers between devices with their start and end apart: 7 -> 0, of which waited for: 4 -> 0; matrix products, arithmetic and copies ran while one was open for 22% -> 0% of each run, Pallas kernels for 0% -> 0%
where the time goes in v2:
time: 134 us
  Pallas kernels  128 us (96%)
  local copies, waits for them, and re-layouts  5.57 us (4%)
    pallas_call x1, Pallas kernels, fused_gradients(): pl.pallas_call(functools.partial(fused_kernel, dims), out_shape=(shape((r...  126 us
    unnamed x50, local copies, waits for them, and re-layouts  5.57 us

profile of v2, /device:TPU:0, one launch (start us, length us, event | category | flops | bytes accessed | tf_op | source)
XLA Modules:
  0.0 134.1 jit_solution(61958592330800422)
XLA Ops:
  0.7 0.0 copy-start.13
  0.7 0.0 copy-start.20
  0.7 0.0 copy-start.1
  0.7 0.0 copy-start.2
  0.7 0.0 copy-start
  0.7 0.0 copy-start.17
  0.7 0.0 copy-start.16
  0.7 0.0 copy-start.22
  0.7 0.0 copy-start.21
  0.8 0.0 copy-start.15
  0.8 0.0 copy-start.14
  0.8 0.0 copy-start.7
  0.8 0.0 copy-start.6
  0.8 0.0 copy-start.10
  0.8 0.0 copy-start.9
  0.8 0.0 copy-start.4
  0.8 0.0 copy-start.3
  0.8 0.0 copy-start.12
  0.8 125.7 %shard_map.381 = (f32[576,128]{1,0:T(8,128)}, f32[64,512]{1,0:T(8,128)}, f32[64,1000]{1,0:T(8,128)}, f32[1,1000]{1,0:T(1,128)}, f32[2,128]{1,0:T(2,128)}, /*index=5*/f32[2,512]{1,0:T(2,128)}, f32[1,128]{1,0:T(1,128)}) custom-call(bf16[1600,128]{1,0:T(8,128)(2,1)} %refs_0_.2, bf16[1600,512]{1,0:T(8,128)(2,1)} %refs_1_.2, s32[16,100]{1,0:T(8,128)} %refs_2_.2, ...), custom_call_target="tpu_custom_call" | custom-call | tf_op jit(solution)/shard_map/pallas_call | solution.py:885
  126.5 0.0 copy-done.13
  126.6 0.0 copy-done.20
  126.6 0.0 copy-done.1
  126.6 0.0 copy-done.2
  126.6 0.0 copy-done
  126.6 0.0 copy-done.17
  126.6 0.0 copy-done.16
  126.6 0.0 copy-done.22
  126.6 0.0 copy-done.21
  126.6 0.0 copy-done.15
  126.6 0.0 copy-done.14
  126.7 0.0 copy-done.7
  126.7 0.0 copy-done.6
  126.7 0.0 copy-done.10
  126.7 0.0 copy-done.9
  126.7 0.0 copy-done.4
  126.7 0.0 copy-done.3
  126.7 0.0 copy-done.12
  126.7 0.0 copy-start.5
  126.7 1.0 copy-done.5
  127.7 0.0 copy-start.8
  127.7 0.9 copy-done.8
  128.6 0.0 copy-start.11
  128.6 0.9 copy-done.11
  129.5 0.0 copy-start.18
  129.5 0.7 copy-done.18
  130.2 0.0 copy-start.19
  130.2 0.7 copy-done.19
  130.9 0.0 copy-start.23
  130.9 0.7 copy-done.23
  131.6 0.0 copy-start.24
  131.6 0.7 copy-done.24
  132.2 1.9 %shard_map.382 = (f32[576,128]{1,0:T(8,128)}, f32[576,128]{1,0:T(8,128)}, f32[576,128]{1,0:T(8,128)}, f32[64,512]{1,0:T(8,128)}, f32[64,512]{1,0:T(8,128)}, /*in...) custom-call(f32[576,128]{1,0:T(8,128)S(1)} %copy-done, ...), custom_call_target="tpu_custom_call" | custom-call | tf_op jit(solution)/shard_map/pallas_call | solution.py:951
Async XLA Ops:
  0.7 125.9 %copy-start.13 = (f32[2,512]{1,0:T(2,128)S(1)}, f32[2,512]{1,0:T(2,128)}, u32[]{:S(2)}) copy-start(f32[2,512]{1,0:T(2,128)} %refs_20_.1) | copy-start | bytes 12292
  0.7 125.9 %copy-start.20 = (f32[2,128]{1,0:T(2,128)S(1)}, f32[2,128]{1,0:T(2,128)}, u32[]{:S(2)}) copy-start(f32[2,128]{1,0:T(2,128)} %refs_16_.1) | copy-start | bytes 3076
  0.7 125.9 %copy-start.1 = (f32[64,1000]{1,0:T(8,128)S(1)}, f32[64,1000]{1,0:T(8,128)}, u32[]{:S(2)}) copy-start(f32[64,1000]{1,0:T(8,128)} %refs_8_.3) | copy-start | bytes 768004
  0.7 125.9 %copy-start.2 = (f32[64,512]{1,0:T(8,128)S(1)}, f32[64,512]{1,0:T(8,128)}, u32[]{:S(2)}) copy-start(f32[64,512]{1,0:T(8,128)} %refs_4_.3) | copy-start | bytes 393220
  0.7 125.9 %copy-start = (f32[576,128]{1,0:T(8,128)S(1)}, f32[576,128]{1,0:T(8,128)}, u32[]{:S(2)}) copy-start(f32[576,128]{1,0:T(8,128)} %refs_0_.3) | copy-start | bytes 884740
  0.7 125.9 %copy-start.17 = (f32[2,512]{1,0:T(2,128)S(1)}, f32[2,512]{1,0:T(2,128)}, u32[]{:S(2)}) copy-start(f32[2,512]{1,0:T(2,128)} %refs_22_.1) | copy-start | bytes 12292
  0.7 125.9 %copy-start.16 = (f32[2,512]{1,0:T(2,128)S(1)}, f32[2,512]{1,0:T(2,128)}, u32[]{:S(2)}) copy-start(f32[2,512]{1,0:T(2,128)} %refs_21_.1) | copy-start | bytes 12292
  0.7 125.9 %copy-start.22 = (f32[2,128]{1,0:T(2,128)S(1)}, f32[2,128]{1,0:T(2,128)}, u32[]{:S(2)}) copy-start(f32[2,128]{1,0:T(2,128)} %refs_18_.1) | copy-start | bytes 3076
  0.7 125.9 %copy-start.21 = (f32[2,128]{1,0:T(2,128)S(1)}, f32[2,128]{1,0:T(2,128)}, u32[]{:S(2)}) copy-start(f32[2,128]{1,0:T(2,128)} %refs_17_.1) | copy-start | bytes 3076
  0.8 125.9 %copy-start.15 = (f32[1000]{0:T(1024)S(1)}, f32[1000]{0:T(1024)}, u32[]{:S(2)}) copy-start(f32[1000]{0:T(1024)} %param.39) | copy-start | bytes 12004
  0.8 125.9 %copy-start.14 = (f32[1000]{0:T(1024)S(1)}, f32[1000]{0:T(1024)}, u32[]{:S(2)}) copy-start(f32[1000]{0:T(1024)} %param.38) | copy-start | bytes 12004
  0.8 125.9 %copy-start.7 = (f32[64,1000]{1,0:T(8,128)S(1)}, f32[64,1000]{1,0:T(8,128)}, u32[]{:S(2)}) copy-start(f32[64,1000]{1,0:T(8,128)} %refs_10_.1) | copy-start | bytes 768004
  0.8 125.9 %copy-start.6 = (f32[64,1000]{1,0:T(8,128)S(1)}, f32[64,1000]{1,0:T(8,128)}, u32[]{:S(2)}) copy-start(f32[64,1000]{1,0:T(8,128)} %refs_9_.3) | copy-start | bytes 768004
  0.8 125.9 %copy-start.10 = (f32[64,512]{1,0:T(8,128)S(1)}, f32[64,512]{1,0:T(8,128)}, u32[]{:S(2)}) copy-start(f32[64,512]{1,0:T(8,128)} %refs_6_.3) | copy-start | bytes 393220
  0.8 125.9 %copy-start.9 = (f32[64,512]{1,0:T(8,128)S(1)}, f32[64,512]{1,0:T(8,128)}, u32[]{:S(2)}) copy-start(f32[64,512]{1,0:T(8,128)} %refs_5_.3) | copy-start | bytes 393220
  0.8 125.9 %copy-start.4 = (f32[576,128]{1,0:T(8,128)S(1)}, f32[576,128]{1,0:T(8,128)}, u32[]{:S(2)}) copy-start(f32[576,128]{1,0:T(8,128)} %refs_2_.3) | copy-start | bytes 884740
  0.8 125.9 %copy-start.3 = (f32[576,128]{1,0:T(8,128)S(1)}, f32[576,128]{1,0:T(8,128)}, u32[]{:S(2)}) copy-start(f32[576,128]{1,0:T(8,128)} %refs_1_.3) | copy-start | bytes 884740
  0.8 125.9 %copy-start.12 = (f32[1000]{0:T(1024)S(1)}, f32[1000]{0:T(1024)}, u32[]{:S(2)}) copy-start(f32[1000]{0:T(1024)} %param.29) | copy-start | bytes 12004
  126.7 1.0 copy-start.5
  127.7 0.9 copy-start.8
  128.6 0.9 copy-start.11
  129.5 0.7 copy-start.18
  130.2 0.7 copy-start.19
  130.9 0.7 copy-start.23
  131.6 0.7 copy-start.24

commit v3 on v2

--- a/solution.py
+++ b/solution.py
@@ -266,15 +266,13 @@
 def fused_kernel(dims, *refs):
     nd, nc, pm, imb, c1l, c2l, r1, rp, rc, classes, total_images = dims
     (
-        feat, short, masks, labels, wconv, wproj, wcls, cbias, n1, n2,
-        gconv, gproj, gcls, gbias, gone, gtwo, gloss,
+        feat, short, masks, labels, wconv, wproj, wcls, cbias, n1, n2, gout,
         wf, pf, cf, wfull, pfull, cfull, xv, sv, xm, xt, yb, hid, mk, edge, cntm, cnti,
         af, at, sec, slp, bn1, bn2, tsum, pool, lgt, dlm, dpd, dsb, da, dab, sr, es, er,
-        du, dhp, acc, pacc, st0, st1, st2, st3, st4,
-        gcs, gcx, gcz, gcr, gps, gpx, gpz, gpr, dla, pla, plt,
-        ld_s, cw_s, cw_r, pw_s, pw_r, kw_s, kw_r, fx_s, fx_r, af_s, af_r, s0_s, s0_r, s1_s, s1_r,
-        s2_s, s2_r, s3_s, s3_r, s4_s, s4_r, lg_s, lg_r, sr_s, sr_r, er_s, er_r,
-        dl_s, dl_r, pl_s, pl_r, gcx_s, gcx_r, gcz_s, gcz_r, gpx_s, gpx_r, gpz_s, gpz_r,
+        du, dhp, acc, pacc, st1, st2, st3, st4,
+        gcs, gcx, gcz, gcr, gps, gpx, gpz, gpr, dla, plt,
+        ld_s, cw_s, cw_r, pw_s, pw_r, kw_s, kw_r, dl_s, dl_r, fx_s, fx_r, af_s, af_r, st_s, st_r,
+        lg_s, lg_r, sr_s, sr_r, er_s, er_r, gc_s, gc_r, gp_s, gp_r,
     ) = refs
     nz = nd // 2
     c1 = c1l * nc
@@ -302,18 +300,27 @@
     def unit(buf, u, rows):
         return buf.at[pl.ds(pl.multiple_of(u * rows, rows), rows)]
 
+    def span(buf, units, rows):
+        return buf.at[pl.ds(0, units * rows)]
+
+    def gather_near(buf, rows, ss, rr, js):
+        mine = unit(buf, d, rows)
+        for j in js:
+            if j == 0:
+                remote(mine, mine, ss.at[0], rr.at[d], xdev).start()
+            elif j < nz:
+                remote(mine, mine, ss.at[1], rr.at[d], zdev(j)).start()
+
     def gather_start(buf, rows, ss, rr):
-        mine = unit(buf, d, rows)
-        remote(mine, mine, ss.at[0], rr.at[d], xdev).start()
-        for j in range(1, nz):
-            remote(mine, mine, ss.at[j], rr.at[d], zdev(j)).start()
+        gather_near(buf, rows, ss, rr, range(nz))
 
     def gather_forward(buf, rows, ss, rr, j):
-        u = flip(z, j) * 2 + x
-        got = unit(buf, u, rows)
-        copy = remote(got, got, ss.at[nz + j], rr.at[u], xdev)
-        copy.wait_recv()
-        copy.start()
+        if j < nz:
+            u = flip(z, j) * 2 + x
+            got = unit(buf, u, rows)
+            copy = remote(got, got, ss.at[0], rr.at[u], xdev)
+            copy.wait_recv()
+            copy.start()
 
     def gather_finish(buf, rows, ss, rr):
         for j in range(nz):
@@ -322,34 +329,28 @@
             remote(got, got, ss.at[0], rr.at[u], xdev).wait_recv()
 
     def gather_drain(buf, rows, ss, rr):
-        mine = unit(buf, d, rows)
-        for j in range(2 * nz):
-            if j != nz:
-                remote(mine, mine, ss.at[j], rr.at[d], xdev).wait_send()
-
-    def peers():
-        return [flip(d, p) for p in range(1, nd)]
+        for i, units in ((0, nz), (1, nz - 1)):
+            if units:
+                sent = span(buf, units, rows)
+                remote(sent, sent, ss.at[i], rr.at[d], xdev).wait_send()
 
     def stats_send(buf, ss, rr):
         for p in range(1, nd):
-            u = flip(d, p)
-            remote(buf.at[d], buf.at[d], ss.at[p], rr.at[d], (u, c)).start()
+            remote(buf.at[0], buf.at[p], ss, rr, (flip(d, p), c)).start()
 
     def stats_wait(buf, ss, rr):
-        for p in range(1, nd):
-            u = flip(d, p)
-            remote(buf.at[u], buf.at[u], ss.at[p], rr.at[u], (u, c)).wait_recv()
+        got = buf.at[pl.ds(1, nd - 1)]
+        remote(got, got, ss, rr, xdev).wait_recv()
 
     def stats_sum(buf):
-        total = buf[0]
-        for p in range(1, nd):
-            total = total + buf[p]
+        total = buf[d]
+        for u in range(1, nd):
+            total = total + buf[flip(d, u)]
         return total
 
     def stats_drain(buf, ss, rr):
-        for p in range(1, nd):
-            u = flip(d, p)
-            remote(buf.at[d], buf.at[d], ss.at[p], rr.at[d], (u, c)).wait_send()
+        got = buf.at[pl.ds(1, nd - 1)]
+        remote(got, got, ss, rr, xdev).wait_send()
 
     def rows(m):
         return pl.ds(pl.multiple_of(m * pm, pm), pm)
@@ -374,18 +375,19 @@
         load.start()
 
     barrier = pltpu.get_barrier_semaphore()
-    others = [(u, c) for u in peers()] + [sibdev, oppdev, (d, dia)]
+    powers = [j for j in (1, 2) if j < nz]
+    others = [sibdev, oppdev, xdev] + [zdev(j) for j in powers]
     for dev in others:
         pl.semaphore_signal(barrier, inc=1, device_id=dev, device_id_type=MESH)
     loads[0].wait()
     wfull[pl.ds(pl.multiple_of(d * r1, r1), r1), :] = wf[...].astype(BF)
     pl.semaphore_wait(barrier, len(others))
 
-    gather_start(wfull, r1, cw_s, cw_r)
+    gather_near(wfull, r1, cw_s, cw_r, [0] + powers)
     for m in range(MICRO):
         src = feat.at[pl.ds(m * pm, pm)]
-        remote(src, part(xv, m, c), fx_s.at[0, m], fx_r.at[c, m], oppdev).start()
-        remote(src, part(xv, m, c), fx_s.at[1, m], fx_r.at[c, m], sibdev).start()
+        remote(src, part(xv, m, c), fx_s, fx_r.at[c, m], oppdev).start()
+        remote(src, part(xv, m, c), fx_s, fx_r.at[c, m], sibdev).start()
 
     loads[1].wait()
     pfull[pl.ds(pl.multiple_of(d * rp, rp), rp), :] = pf[...].astype(BF)
@@ -417,8 +419,7 @@
         mk[m] = spread
         cntm[m] = jnp.sum(spread, axis=0, keepdims=True)
         cnti[m] = jnp.broadcast_to(image_count[m * imb : (m + 1) * imb], (imb, 128))
-        st0[d, m : m + 1, :] = cntm[m]
-    stats_send(st0, s0_s, s0_r)
+        st1[m, 0, 2:3, :] = cntm[m]
 
     yb[:, 0:PAD, :] = jnp.zeros((9, PAD, c1l), F32)
     yb[:, PAD + pm :, :] = jnp.zeros((9, PAD, c1l), F32)
@@ -427,19 +428,19 @@
 
     for m in range(MICRO):
         got = part(xv, m, opp)
-        copy = remote(got, got, fx_s.at[2, m], fx_r.at[opp, m], sibdev)
+        copy = remote(got, got, fx_s, fx_r.at[opp, m], sibdev)
         copy.wait_recv()
         copy.start()
-        if 1 <= m < nz:
+        if m >= 1:
             gather_forward(wfull, r1, cw_s, cw_r, m)
-    for j in range(MICRO, nz):
-        gather_forward(wfull, r1, cw_s, cw_r, j)
+        if m == 1:
+            gather_near(wfull, r1, cw_s, cw_r, [3])
     loads[3].wait()
 
     def take_features(m, carry):
         for chunk in (sib, dia):
             got = part(xv, m, chunk)
-            remote(got, got, fx_s.at[2, m], fx_r.at[chunk, m], sibdev).wait_recv()
+            remote(got, got, fx_s, fx_r.at[chunk, m], sibdev).wait_recv()
         flat_mask = mk[m].astype(BF)
         for q in range(nc):
             piece = xv[rows(m), q * c1l : (q + 1) * c1l] * flat_mask
@@ -489,41 +490,37 @@
             hidden = column if hidden is None else hidden + column
         hid[m] = hidden
         valid = hidden * mk[m]
-        st1[d, pl.ds(m, 1), :] = jnp.sum(valid, axis=0, keepdims=True)
-        st1[d, pl.ds(MICRO + m, 1), :] = jnp.sum(valid * hidden, axis=0, keepdims=True)
+        st1[m, 0, 0:1, :] = jnp.sum(valid, axis=0, keepdims=True)
+        st1[m, 0, 1:2, :] = jnp.sum(valid * hidden, axis=0, keepdims=True)
+        stats_send(st1.at[m], st_s.at[0, m], st_r.at[0, m])
         return carry
 
     lax.fori_loop(0, MICRO, conv, 0)
-    stats_send(st1, s1_s, s1_r)
+    gather_start(cfull, rc, kw_s, kw_r)
     for j in range(1, nz):
         gather_forward(pfull, rp, pw_s, pw_r, j)
     acc[...] = jnp.zeros_like(acc)
     pacc[...] = jnp.zeros_like(pacc)
 
-    stats_wait(st0, s0_s, s0_r)
-    counts = stats_sum(st0)
-    stats_wait(st1, s1_s, s1_r)
-    totals = stats_sum(st1)
-    for m in range(MICRO):
-        n = counts[m : m + 1, :]
+    def activate(m, carry):
+        stats_wait(st1.at[m], st_s.at[0, m], st_r.at[0, m])
+        totals = stats_sum(st1.at[m])
+        n = totals[2:3]
         cntm[m] = n
-        center = totals[m : m + 1, :] / n
-        spread = totals[MICRO + m : MICRO + m + 1, :] / n - center * center
+        center = totals[0:1] / n
         bn1[m, 0:1, :] = center
-        bn1[m, 1:2, :] = lax.rsqrt(spread + norm_eps)
-
-    def activate(m, carry):
+        bn1[m, 1:2, :] = lax.rsqrt(totals[1:2] / n - center * center + norm_eps)
         normed = (hid[m] - bn1[m, 0:1, :]) * bn1[m, 1:2, :]
         shifted = n1[0:1, :] * normed + n1[1:2, :]
         active = (shifted * sigmoid(shifted) * mk[m]).astype(BF)
         mine = part(af, m, c)
         mine[...] = active
-        remote(mine, mine, af_s.at[0, m], af_r.at[c, m], oppdev).start()
-        remote(mine, mine, af_s.at[1, m], af_r.at[c, m], sibdev).start()
+        remote(mine, mine, af_s, af_r.at[c, m], oppdev).start()
+        remote(mine, mine, af_s, af_r.at[c, m], sibdev).start()
         return carry
 
     lax.fori_loop(0, MICRO, activate, 0)
-    gather_start(cfull, rc, kw_s, kw_r)
+    gather_forward(cfull, rc, kw_s, kw_r, 1)
     gather_finish(pfull, rp, pw_s, pw_r)
     loads[4].wait()
 
@@ -535,16 +532,16 @@
 
     def stage_a(m):
         got = part(af, m, opp)
-        copy = remote(got, got, af_s.at[2, m], af_r.at[opp, m], sibdev)
+        copy = remote(got, got, af_s, af_r.at[opp, m], sibdev)
         copy.wait_recv()
         copy.start()
         turn(m, c)
         turn(m, opp)
         got = part(af, m, sib)
-        remote(got, got, af_s.at[2, m], af_r.at[sib, m], sibdev).wait_recv()
+        remote(got, got, af_s, af_r.at[sib, m], sibdev).wait_recv()
         turn(m, sib)
         got = part(af, m, dia)
-        remote(got, got, af_s.at[2, m], af_r.at[dia, m], sibdev).wait_recv()
+        remote(got, got, af_s, af_r.at[dia, m], sibdev).wait_recv()
         turn(m, dia)
         second = mm(af[rows(m), :], pfull[...])
         sec[m] = second
@@ -552,9 +549,9 @@
         for q in range(nq):
             piece = second[:, q * 128 : (q + 1) * 128]
             valid = piece * mask
-            st2[m, d, q : q + 1, :] = jnp.sum(valid, axis=0, keepdims=True)
-            st2[m, d, nq + q : nq + q + 1, :] = jnp.sum(valid * piece, axis=0, keepdims=True)
-        stats_send(st2.at[m], s2_s.at[m], s2_r.at[m])
+            st2[m, 0, q : q + 1, :] = jnp.sum(valid, axis=0, keepdims=True)
+            st2[m, 0, nq + q : nq + q + 1, :] = jnp.sum(valid * piece, axis=0, keepdims=True)
+        stats_send(st2.at[m], st_s.at[1, m], st_r.at[1, m])
 
     low_half = row_iota((2, 8, 128)) * 0 + lax.broadcasted_iota(jnp.int32, (2, 8, 128), 1)
     tiles = AREA // 4
@@ -584,7 +581,7 @@
         return jnp.concatenate(pieces, axis=0).reshape(pm, 128)
 
     def stage_b(m):
-        stats_wait(st2.at[m], s2_s.at[m], s2_r.at[m])
+        stats_wait(st2.at[m], st_s.at[1, m], st_r.at[1, m])
         total = stats_sum(st2.at[m])
         n = cntm[m]
         mask = mk[m]
@@ -605,13 +602,12 @@
             tsum[m, 0, :, at_q] = image_sums(slope)
             tsum[m, 1, :, at_q] = image_sums(slope * normed)
         lgt[m, c] = mm(pool[m].astype(BF), cfull[...])
-        for dev, i in ((sibdev, 0), (oppdev, 1), ((d, dia), 2)):
-            remote(lgt.at[m, c], lgt.at[m, c], lg_s.at[i, m], lg_r.at[c, m], dev).start()
+        for dev in (oppdev, (d, dia), sibdev):
+            remote(lgt.at[m, c], lgt.at[m, c], lg_s, lg_r.at[m], dev).start()
 
     def stage_c(m):
-        for i, chunk in enumerate((sib, opp, dia)):
-            got = lgt.at[m, chunk]
-            remote(got, got, lg_s.at[i, m], lg_r.at[chunk, m], sibdev).wait_recv()
+        got = lgt.at[m, pl.ds(0, nc - 1)]
+        remote(got, got, lg_s, lg_r.at[m], sibdev).wait_recv()
         logits = lgt[m, 0]
         for q in range(1, nc):
             logits = logits + lgt[m, q]
@@ -626,7 +622,7 @@
         onehot = (target == lane_iota((imb, classes))).astype(F32)
         picked = jnp.sum(logits * onehot, axis=1, keepdims=True)
         loss = jnp.sum(top + jnp.log(expo_sum) - picked, axis=0, keepdims=True)
-        st4[m, d, 2:3, :] = jnp.broadcast_to(loss, (1, 128))
+        st4[m, 0, 2:3, :] = jnp.broadcast_to(loss, (1, 128))
         dlogits = ((expo / expo_sum - onehot) / total_images).astype(BF)
         dlm[m] = dlogits.astype(F32)
         spread = nt_dot(dlogits, cfull[...])
@@ -634,14 +630,14 @@
             at_q = slice(q * 128, (q + 1) * 128)
             value = spread[:, at_q] / cnti[m]
             dpd[m, :, at_q] = value
-            st3[m, d, q : q + 1, :] = jnp.sum(value * tsum[m, 0, :, at_q], axis=0, keepdims=True)
-            st3[m, d, nq + q : nq + q + 1, :] = jnp.sum(
+            st3[m, 0, q : q + 1, :] = jnp.sum(value * tsum[m, 0, :, at_q], axis=0, keepdims=True)
+            st3[m, 0, nq + q : nq + q + 1, :] = jnp.sum(
                 value * tsum[m, 1, :, at_q], axis=0, keepdims=True
             )
-        stats_send(st3.at[m], s3_s.at[m], s3_r.at[m])
+        stats_send(st3.at[m], st_s.at[2, m], st_r.at[2, m])
 
     def stage_d(m):
-        stats_wait(st3.at[m], s3_s.at[m], s3_r.at[m])
+        stats_wait(st3.at[m], st_s.at[2, m], st_r.at[2, m])
         total = stats_sum(st3.at[m])
         n = cntm[m]
         mask = mk[m]
@@ -660,34 +656,30 @@
         back = nt_dot(dsb[...], pfull[...])
         for q in range(nc):
             piece = back[:, q * c1l : (q + 1) * c1l]
-            da[m, q] = piece
-            dab[m, q] = piece.astype(BF)
-        for i, chunk in ((0, sib), (1, dia)):
-            remote(dab.at[m, chunk], sr.at[m, i], sr_s.at[i, m], sr_r.at[i, m], sibdev).start()
+            da[m, q % 2, q // 2] = piece
+            dab[m, q % 2, q // 2] = piece.astype(BF)
+        remote(dab.at[m, 1 - k], sr.at[m], sr_s, sr_r.at[m], sibdev).start()
         pacc[...] += mm(at[m], dsb[...])
 
     def stage_e(m):
-        for i in (1, 0):
-            remote(sr.at[m, i], sr.at[m, i], sr_s.at[i, m], sr_r.at[i, m], sibdev).wait_recv()
-            if i == 1:
-                es[m] = (da[m, opp] + sr[m, 1].astype(F32)).astype(BF)
-                remote(es.at[m], er.at[m], er_s.at[m], er_r.at[m], oppdev).start()
-        da[m, c] = da[m, c] + sr[m, 0].astype(F32)
+        remote(sr.at[m], sr.at[m], sr_s, sr_r.at[m], sibdev).wait_recv()
+        es[m] = (da[m, k, 1 - y] + sr[m, 1 - y].astype(F32)).astype(BF)
+        remote(es.at[m], er.at[m], er_s, er_r.at[m], oppdev).start()
 
     def stage_f(m):
-        remote(es.at[m], er.at[m], er_s.at[m], er_r.at[m], oppdev).wait_recv()
-        upstream = da[m, c] + er[m].astype(F32)
+        remote(es.at[m], er.at[m], er_s, er_r.at[m], oppdev).wait_recv()
+        upstream = da[m, k, y] + sr[m, y].astype(F32) + er[m].astype(F32)
         normed = (hid[m] - bn1[m, 0:1, :]) * bn1[m, 1:2, :]
         shifted = n1[0:1, :] * normed + n1[1:2, :]
         sigma = sigmoid(shifted)
         upstream = upstream * mk[m] * (sigma * (1.0 + shifted * (1.0 - sigma)))
         du[m] = upstream
-        st4[m, d, 0:1, :] = jnp.sum(upstream, axis=0, keepdims=True)
-        st4[m, d, 1:2, :] = jnp.sum(upstream * normed, axis=0, keepdims=True)
-        stats_send(st4.at[m], s4_s.at[m], s4_r.at[m])
+        st4[m, 0, 0:1, :] = jnp.sum(upstream, axis=0, keepdims=True)
+        st4[m, 0, 1:2, :] = jnp.sum(upstream * normed, axis=0, keepdims=True)
+        stats_send(st4.at[m], st_s.at[3, m], st_r.at[3, m])
 
     def stage_g(m):
-        stats_wait(st4.at[m], s4_s.at[m], s4_r.at[m])
+        stats_wait(st4.at[m], st_s.at[3, m], st_r.at[3, m])
         total = stats_sum(st4.at[m])
         n = cntm[m]
         bn1[m, 2:3, :] = total[1:2]
@@ -718,110 +710,142 @@
         for j in range(nz):
             u = flip(z, j) * 2 + 1 - x
             sbuf[j] = total[pl.ds(pl.multiple_of(u * height, height), height), :].astype(BF)
-            remote(sbuf.at[j], xbuf.at[j], ss.at[j], rr.at[j], xdev).start()
-
-    def scatter_middle(total, height, xbuf, zbuf, rbuf, xs, xr, zs, zr):
+            remote(sbuf.at[j], xbuf.at[j], ss.at[0], rr.at[j], xdev).start()
+
+    def scatter_middle(total, height, xbuf, zbuf, rbuf, ss, rr):
         for j in list(range(1, nz)) + [0]:
-            remote(xbuf.at[j], xbuf.at[j], xs.at[j], xr.at[j], xdev).wait_recv()
+            remote(xbuf.at[j], xbuf.at[j], ss.at[0], rr.at[j], xdev).wait_recv()
             u = flip(z, j) * 2 + x
             found = total[pl.ds(pl.multiple_of(u * height, height), height), :]
             found = found + xbuf[j].astype(F32)
             if j == 0:
                 return found
             zbuf[j] = found.astype(BF)
-            remote(zbuf.at[j], rbuf.at[j], zs.at[j], zr.at[j], zdev(j)).start()
-
-    def scatter_finish(found, rbuf, zs, zr):
+            remote(zbuf.at[j], rbuf.at[j], ss.at[1], rr.at[nz], zdev(j)).start()
+
+    def scatter_finish(found, rbuf, ss, rr):
+        if nz > 1:
+            got = rbuf.at[pl.ds(1, nz - 1)]
+            remote(got, got, ss.at[1], rr.at[nz], xdev).wait_recv()
         for j in range(1, nz):
-            remote(rbuf.at[j], rbuf.at[j], zs.at[j], zr.at[j], zdev(j)).wait_recv()
             found = found + rbuf[j].astype(F32)
         return found
 
-    def scatter_drain(sbuf, zbuf, xs, xr, zs, zr):
-        for j in range(nz):
-            remote(sbuf.at[j], sbuf.at[j], xs.at[j], xr.at[j], xdev).wait_send()
-            if j > 0:
-                remote(zbuf.at[j], zbuf.at[j], zs.at[j], zr.at[j], xdev).wait_send()
-
-    stages = (stage_a, stage_b, stage_c, stage_d, stage_e, stage_f, stage_g)
+    def scatter_drain(sbuf, zbuf, ss, rr):
+        remote(sbuf, sbuf, ss.at[0], rr.at[0], xdev).wait_send()
+        if nz > 1:
+            sent = zbuf.at[pl.ds(1, nz - 1)]
+            remote(sent, sent, ss.at[1], rr.at[0], xdev).wait_send()
+
+    def cls_rows(u):
+        return pl.ds(pl.multiple_of(u * images, images), images)
+
+    wide = dla.shape[1] - c2l
+
+    def share_cls():
+        mine = jnp.concatenate([dlm[q] for q in range(MICRO)], axis=0).astype(BF)
+        dla[cls_rows(d), 0:classes] = mine
+        if wide > classes:
+            dla[cls_rows(d), classes:wide] = jnp.zeros((images, wide - classes), BF)
+        mine = jnp.concatenate([pool[q] for q in range(MICRO)], axis=0).astype(BF)
+        dla[cls_rows(d), wide:] = mine
+        gather_start(dla, images, dl_s, dl_r)
+
+    def start_proj():
+        scatter_start(pacc, rp, gps, gpx, gp_s, gp_r)
+
+    def middle_proj():
+        part_sum = scatter_middle(pacc, rp, gpx, gpz, gpr, gp_s, gp_r)
+        for q in range(nq):
+            gout[r1 + q * rp : r1 + (q + 1) * rp, :] = part_sum[:, q * 128 : (q + 1) * 128]
+
+    def finish_cls():
+        gather_finish(cfull, rc, kw_s, kw_r)
+
+    offsets = dict(a=0, b=2, c=4, d=6, e=7, f=9, g=11)
+    stages = dict(a=stage_a, b=stage_b, c=stage_c, d=stage_d, e=stage_e, f=stage_f, g=stage_g)
+    hooks = {
+        (0, "a"): lambda: gather_forward(cfull, rc, kw_s, kw_r, 2),
+        (1, "a"): lambda: gather_forward(cfull, rc, kw_s, kw_r, 3),
+        (2, "a"): finish_cls,
+        (7, "c"): share_cls,
+        (9, "d"): start_proj,
+        (9, "g"): lambda: gather_forward(dla, images, dl_s, dl_r, 1),
+        (11, "f"): lambda: gather_forward(dla, images, dl_s, dl_r, 2),
+        (12, "f"): middle_proj,
+        (13, "f"): lambda: gather_forward(dla, images, dl_s, dl_r, 3),
+    }
 
     def step(s, carry):
-        for i in reversed(range(len(stages))):
+        for name in "acbegfd":
+            i = offsets[name]
+
             @pl.when((s >= i) & (s < i + MICRO))
-            def run(i=i):
-                stages[i](s - i)
-
-            if i == 3:
-                @pl.when(s == MICRO + 2)
-                def start_proj():
-                    scatter_start(pacc, rp, gps, gpx, gpx_s, gpx_r)
-
-            if i == 2:
-                @pl.when(s == MICRO + 1)
-                def share_cls():
-                    mine = dla.at[pl.ds(pl.multiple_of(d * images, images), images)]
-                    mine[...] = jnp.concatenate([dlm[q] for q in range(MICRO)], axis=0).astype(BF)
-                    pooled = pla.at[pl.ds(pl.multiple_of(d * images, images), images)]
-                    pooled[...] = jnp.concatenate([pool[q] for q in range(MICRO)], axis=0).astype(BF)
-                    gather_start(dla, images, dl_s, dl_r)
-                    gather_start(pla, images, pl_s, pl_r)
-
-            if i == 0:
-                @pl.when(s == 0)
-                def move_cls():
-                    for j in range(1, nz):
-                        gather_forward(cfull, rc, kw_s, kw_r, j)
-                    gather_finish(cfull, rc, kw_s, kw_r)
+            def run(name=name, i=i):
+                stages[name](s - i)
+
+            for (when, after), hook in hooks.items():
+                if after == name:
+
+                    @pl.when(s == when)
+                    def extra(hook=hook):
+                        hook()
 
         return carry
 
-    lax.fori_loop(0, MICRO + len(stages) - 1, step, 0)
-
-    scatter_start(acc, r1, gcs, gcx, gcx_s, gcx_r)
-
-    for j in range(1, nz):
-        gather_forward(dla, images, dl_s, dl_r, j)
-        gather_forward(pla, images, pl_s, pl_r, j)
-    proj_part = scatter_middle(pacc, rp, gpx, gpz, gpr, gpx_s, gpx_r, gpz_s, gpz_r)
-    gproj[...] = scatter_finish(proj_part, gpr, gpz_s, gpz_r)
+    lax.fori_loop(0, MICRO + offsets["g"], step, 0)
+
+    scatter_start(acc, r1, gcs, gcx, gc_s, gc_r)
+
     gather_finish(dla, images, dl_s, dl_r)
-    gather_finish(pla, images, pl_s, pl_r)
-    plt[...] = pla[...].T
+    plt[...] = dla[:, wide:].T
     left = plt[pl.ds(pl.multiple_of(d * rc, rc), rc), :]
-    gcls[...] = mm(left, dla[...])
-    gbias[...] = jnp.sum(dla[...].astype(F32), axis=0, keepdims=True)
-    gone[...] = bn1[0, 2:4, :] + bn1[1, 2:4, :] + bn1[2, 2:4, :] + bn1[3, 2:4, :]
-    gtwo[...] = bn2[0, 1:3, :] + bn2[1, 1:3, :] + bn2[2, 1:3, :] + bn2[3, 1:3, :]
+    row = r1 + nq * rp
+    share = mm(left, dla[:, 0:wide])
+    for q in range(wide // 128):
+        gout[row + q * rc : row + (q + 1) * rc, :] = share[:, q * 128 : (q + 1) * 128]
+    row = row + wide // 128 * rc
+    share = jnp.sum(dla[:, 0:wide].astype(F32), axis=0, keepdims=True)
+    for q in range(wide // 128):
+        gout[row + q : row + q + 1, :] = share[:, q * 128 : (q + 1) * 128]
+    row = row + wide // 128
+    share = bn2[0, 1:3, :] + bn2[1, 1:3, :] + bn2[2, 1:3, :] + bn2[3, 1:3, :]
+    for q in range(nq):
+        gout[row + 2 * q : row + 2 * q + 2, :] = share[:, q * 128 : (q + 1) * 128]
+    row = row + 2 * nq
+    gout[row : row + 2, :] = bn1[0, 2:4, :] + bn1[1, 2:4, :] + bn1[2, 2:4, :] + bn1[3, 2:4, :]
     loss = bn1[0, 4:5, :] + bn1[1, 4:5, :] + bn1[2, 4:5, :] + bn1[3, 4:5, :]
-    gloss[...] = loss / total_images
-
-    conv_part = scatter_middle(acc, r1, gcx, gcz, gcr, gcx_s, gcx_r, gcz_s, gcz_r)
-    gconv[...] = scatter_finish(conv_part, gcr, gcz_s, gcz_r)
+    gout[row + 2 : row + 3, :] = loss / total_images
+    if nz > 1:
+        got = gpr.at[pl.ds(1, nz - 1)]
+        remote(got, got, gp_s.at[1], gp_r.at[nz], xdev).wait_recv()
+    for q in range(nq):
+        share = gout[r1 + q * rp : r1 + (q + 1) * rp, :]
+        for j in range(1, nz):
+            share = share + gpr[j, :, q * 128 : (q + 1) * 128].astype(F32)
+        gout[r1 + q * rp : r1 + (q + 1) * rp, :] = share
+
+    conv_part = scatter_middle(acc, r1, gcx, gcz, gcr, gc_s, gc_r)
+    gout[0:r1, :] = scatter_finish(conv_part, gcr, gc_s, gc_r)
 
     gather_drain(wfull, r1, cw_s, cw_r)
     gather_drain(pfull, rp, pw_s, pw_r)
     gather_drain(cfull, rc, kw_s, kw_r)
     gather_drain(dla, images, dl_s, dl_r)
-    gather_drain(pla, images, pl_s, pl_r)
-    stats_drain(st0, s0_s, s0_r)
-    stats_drain(st1, s1_s, s1_r)
-    scatter_drain(gps, gpz, gpx_s, gpx_r, gpz_s, gpz_r)
-    scatter_drain(gcs, gcz, gcx_s, gcx_r, gcz_s, gcz_r)
+    scatter_drain(gps, gpz, gp_s, gp_r)
+    scatter_drain(gcs, gcz, gc_s, gc_r)
+    sent = xv.at[:, pl.ds(0, 3 * c1l)]
+    remote(sent, sent, fx_s, fx_r.at[0, 0], sibdev).wait_send()
+    sent = af.at[:, pl.ds(0, 3 * c1l)]
+    remote(sent, sent, af_s, af_r.at[0, 0], sibdev).wait_send()
+    sent = lgt.at[pl.ds(0, nc - 1)]
+    remote(sent, sent, lg_s, lg_r.at[0], sibdev).wait_send()
+    remote(sr, sr, sr_s, sr_r.at[0], sibdev).wait_send()
+    remote(es, es, er_s, er_r.at[0], oppdev).wait_send()
 
     def drain(m, carry):
-        for i in range(3):
-            src = part(xv, m, c)
-            remote(src, src, fx_s.at[i, m], fx_r.at[c, m], sibdev).wait_send()
-            src = part(af, m, c)
-            remote(src, src, af_s.at[i, m], af_r.at[c, m], sibdev).wait_send()
-            src = lgt.at[m, c]
-            remote(src, src, lg_s.at[i, m], lg_r.at[c, m], sibdev).wait_send()
-        for i in range(2):
-            remote(sr.at[m, i], sr.at[m, i], sr_s.at[i, m], sr_r.at[i, m], sibdev).wait_send()
-        remote(es.at[m], er.at[m], er_s.at[m], er_r.at[m], oppdev).wait_send()
-        stats_drain(st2.at[m], s2_s.at[m], s2_r.at[m])
-        stats_drain(st3.at[m], s3_s.at[m], s3_r.at[m])
-        stats_drain(st4.at[m], s4_s.at[m], s4_r.at[m])
+        for i, buf in enumerate((st1, st2, st3, st4)):
+            stats_drain(buf.at[m], st_s.at[i, m], st_r.at[i, m])
         return carry
 
     lax.fori_loop(0, MICRO, drain, 0)
@@ -840,6 +864,9 @@
     classes = w_cls.shape[1]
     c1 = c1l * nc
     nq = c2l // 128
+    wide = -(-classes // 128) * 128
+    grad_rows = r1 + nq * rp + wide // 128 * (rc + 1) + 2 * nq + 3
+    grad_rows = -(-grad_rows // 8) * 8
     dims = (nd, nc, pm, imb, c1l, c2l, r1, rp, rc, classes, images * nd)
     vmem = pltpu.VMEM
     dma = pltpu.SemaphoreType.DMA
@@ -856,27 +883,23 @@
         vmem((m4, 8, c1l), F32), vmem((m4, 8, c2l), F32),
         vmem((m4, 2, imb, c2l), F32), vmem((m4, imb, c2l), F32),
         vmem((m4, nc, imb, classes), F32), vmem((m4, imb, classes), F32), vmem((m4, imb, c2l), F32),
-        vmem((pm, c2l), BF), vmem((m4, nc, pm, c1l), F32), vmem((m4, nc, pm, c1l), BF),
+        vmem((pm, c2l), BF), vmem((m4, 2, 2, pm, c1l), F32), vmem((m4, 2, 2, pm, c1l), BF),
         vmem((m4, 2, pm, c1l), BF), vmem((m4, pm, c1l), BF), vmem((m4, pm, c1l), BF),
         vmem((m4, pm, c1l), F32), vmem((PAD + pm + PAD, c1l), F32),
         vmem((9 * c1, c1l), F32), vmem((c1, c2l), F32),
-        vmem((nd, 8, c1l), F32), vmem((nd, 8, c1l), F32),
+        vmem((m4, nd, 8, c1l), F32),
         vmem((m4, nd, 2 * nq, 128), F32), vmem((m4, nd, 2 * nq, 128), F32),
         vmem((m4, nd, 8, c1l), F32),
         vmem((nz, r1, c1l), BF), vmem((nz, r1, c1l), BF),
         vmem((nz, r1, c1l), BF), vmem((nz, r1, c1l), BF),
         vmem((nz, rp, c2l), BF), vmem((nz, rp, c2l), BF),
         vmem((nz, rp, c2l), BF), vmem((nz, rp, c2l), BF),
-        vmem((nd * images, classes), BF), vmem((nd * images, c2l), BF), vmem((c2l, nd * images), BF),
+        vmem((nd * images, wide + c2l), BF), vmem((c2l, nd * images), BF),
         dma((5,)),
-        dma((2 * nz,)), dma((nd,)), dma((2 * nz,)), dma((nd,)), dma((2 * nz,)), dma((nd,)),
-        dma((3, m4)), dma((nc, m4)), dma((3, m4)), dma((nc, m4)),
-        dma((nd,)), dma((nd,)), dma((nd,)), dma((nd,)),
-        dma((m4, nd)), dma((m4, nd)), dma((m4, nd)), dma((m4, nd)), dma((m4, nd)), dma((m4, nd)),
-        dma((3, m4)), dma((nc, m4)), dma((2, m4)), dma((2, m4)), dma((m4,)), dma((m4,)),
-        dma((2 * nz,)), dma((nd,)), dma((2 * nz,)), dma((nd,)),
-        dma((nz,)), dma((nz,)), dma((nz,)), dma((nz,)),
-        dma((nz,)), dma((nz,)), dma((nz,)), dma((nz,)),
+        dma((2,)), dma((nd,)), dma((2,)), dma((nd,)), dma((2,)), dma((nd,)), dma((2,)), dma((nd,)),
+        dma, dma((nc, m4)), dma, dma((nc, m4)), dma((4, m4)), dma((4, m4)),
+        dma, dma((m4,)), dma, dma((m4,)), dma, dma((m4,)),
+        dma((2,)), dma((nz + 1,)), dma((2,)), dma((nz + 1,)),
     ]
     whole = pl.BlockSpec(memory_space=pltpu.VMEM)
     hbm = pl.BlockSpec(memory_space=pl.ANY)
@@ -884,13 +907,9 @@
     shape = jax.ShapeDtypeStruct
     return pl.pallas_call(
         functools.partial(fused_kernel, dims),
-        out_shape=(
-            shape((r1, c1l), F32), shape((rp, c2l), F32), shape((rc, classes), F32),
-            shape((1, classes), F32), shape((2, c1l), F32), shape((2, c2l), F32),
-            shape((1, 128), F32),
-        ),
+        out_shape=shape((grad_rows, 128), F32),
         in_specs=[hbm, hbm, whole, scalar, hbm, hbm, hbm, whole, whole, whole],
-        out_specs=(whole,) * 7,
+        out_specs=whole,
         scratch_shapes=scratch,
         compiler_params=pltpu.CompilerParams(
             collective_id=0, has_side_effects=True, vmem_limit_bytes=58 * 1024 * 1024
@@ -901,17 +920,25 @@
     )
 
 
-def adam_kernel(*refs):
+def adam_kernel(grads, *refs):
+    states, outs = refs[:18], refs[18:]
+    row = 0
     for i, (rate, decay) in enumerate(ADAM_RATES):
-        weight, moment, second, grad = (ref[...] for ref in refs[4 * i : 4 * i + 4])
-        outs = refs[4 * len(ADAM_RATES) + 1 + 3 * i :]
-        new_weight, new_moment, new_second = adam_step(weight, moment, second, grad, rate, decay)
-        outs[0][...] = new_weight
-        outs[1][...] = new_moment
-        outs[2][...] = new_second
-        if i < 3:
-            refs[7 * len(ADAM_RATES) + 1 + i][...] = new_weight.astype(BF)
-    refs[-1][...] = refs[4 * len(ADAM_RATES)][...]
+        weight, moment, second = states[3 * i : 3 * i + 3]
+        height, width = weight.shape
+        for start in range(0, width, 128):
+            size = min(128, width - start)
+            at_q = slice(start, start + size)
+            found = adam_step(
+                weight[:, at_q], moment[:, at_q], second[:, at_q],
+                grads[row : row + height, 0:size], rate, decay,
+            )
+            row += height
+            for out, value in zip(outs[3 * i : 3 * i + 3], found):
+                out[:, at_q] = value
+            if i < 3:
+                outs[18 + i][:, at_q] = found[0].astype(BF)
+    outs[21][...] = grads[row : row + 1, :]
 
 
 ADAM_RATES = (
@@ -937,15 +964,15 @@
         (w_proj, proj_moment, proj_second),
         (w_cls, cls_moment, cls_second),
         (cls_bias.reshape(1, -1), bias_moment.reshape(1, -1), bias_second.reshape(1, -1)),
+        (norm_two, two_moment, two_second),
         (norm_one, one_moment, one_second),
-        (norm_two, two_moment, two_second),
     )
     operands, outs = [], []
-    for state, grad in zip(states, grads[:6]):
-        operands += list(state) + [grad]
-        outs += [jax.ShapeDtypeStruct(grad.shape, F32)] * 3
-    outs += [jax.ShapeDtypeStruct(grads[i].shape, BF) for i in range(3)]
-    outs.append(jax.ShapeDtypeStruct(grads[6].shape, F32))
+    for state in states:
+        operands += list(state)
+        outs += [jax.ShapeDtypeStruct(state[0].shape, F32)] * 3
+    outs += [jax.ShapeDtypeStruct(state[0].shape, BF) for state in states[:3]]
+    outs.append(jax.ShapeDtypeStruct((1, 128), F32))
     whole = pl.BlockSpec(memory_space=pltpu.VMEM)
     done = list(
         pl.pallas_call(
@@ -954,11 +981,10 @@
             in_specs=[whole] * (len(operands) + 1),
             out_specs=(whole,) * len(outs),
             compiler_params=pltpu.CompilerParams(vmem_limit_bytes=40 * 1024 * 1024),
-        )(*operands, grads[6])
-    )
-    for i in (9, 10, 11):
-        done[i] = done[i].reshape(-1)
-    return tuple(done[:21]) + (done[21][0, 0],)
+        )(grads, *operands)
+    )
+    biases = [done[i].reshape(-1) for i in (9, 10, 11)]
+    return tuple(done[:9] + biases + done[15:18] + done[12:15] + done[18:21]) + (done[21][0, 0],)
 
 
 def run_device(*args):
@@ -966,7 +992,7 @@
     w_cls = args[6]
     fits = (
         lax.axis_size("chan") == 4
-        and lax.axis_size("dp") % 2 == 0
+        and lax.axis_size("dp") in (2, 4, 8)
         and features.shape[1] == 128
         and shortcut.shape[1] % 128 == 0
         and w_cls.shape[0] % 16 == 0

time: 134 us -> 110 us (0.82)
  Pallas kernels: 128 us -> 108 us
  local copies, waits for them, and re-layouts: 5.57 us -> 1.17 us
    pallas_call x1, Pallas kernels: 126 us -> 106 us  [fused_gradients(): pl.pallas_call(functools.partial(fused_kernel, dims), out_shape=shape((gr...]
    unnamed x50 -> x38, local copies, waits for them, and re-layouts: 5.57 us -> 1.17 us
where the time goes in v3:
time: 110 us
  Pallas kernels  108 us (98%)
  local copies, waits for them, and re-layouts  1.17 us (1%)
    pallas_call x1, Pallas kernels, fused_gradients(): pl.pallas_call(functools.partial(fused_kernel, dims), out_shape=shape((gr...  106 us

profile of v3, /device:TPU:0, one launch (start us, length us, event | category | flops | bytes accessed | tf_op | source)
XLA Modules:
  0.0 109.7 jit_solution(907126190802489514)
XLA Ops:
  0.7 0.0 copy-start.1
  0.7 0.0 copy-start.2
  0.7 0.0 copy-start.3
  0.7 0.0 copy-start.4
  0.7 0.0 copy-start.5
  0.7 0.0 copy-start.6
  0.7 0.0 copy-start.7
  0.7 0.0 copy-start.8
  0.7 0.0 copy-start.9
  0.8 0.0 copy-start.10
  0.8 0.0 copy-start.11
  0.8 0.0 copy-start.12
  0.8 0.0 copy-start.13
  0.8 0.0 copy-start.14
  0.8 0.0 copy-start.15
  0.8 0.0 copy-start.16
  0.8 0.0 copy-start.17
  0.8 0.0 copy-start.18
  0.8 105.7 %shard_map.381.grads = f32[1368,128]{1,0:T(8,128)} custom-call(bf16[1600,128]{1,0:T(8,128)(2,1)} %refs_0_.2, bf16[1600,512]{1,0:T(8,128)(2,1)} %refs_1_.2, s32[16,100]{1,0:T(8,128)} %refs_2_.2, s32[16]{0:T(128)} %refs_3_.2, f32[576,128]{1,0:T(8,128)} %refs_0_.3, f32[64,512]{1,0:T(8,128)} %refs_3_.3, f32[64,1000]{1,0:T(8,128)} %refs_6_.3, f32[1,1000]{1,0:T(1,128)} %bitcast.8, ...), custom_call_target="tpu_custom_call" | custom-call | tf_op jit(solution)/shard_map/pallas_call | solution.py:908
  106.5 0.0 copy-done.1
  106.5 0.0 copy-done.2
  106.6 0.0 copy-done.3
  106.6 0.0 copy-done.4
  106.6 0.0 copy-done.5
  106.6 0.0 copy-done.6
  106.6 0.0 copy-done.7
  106.6 0.0 copy-done.8
  106.6 0.0 copy-done.9
  106.6 0.0 copy-done.10
  106.6 0.0 copy-done.11
  106.6 0.0 copy-done.12
  106.7 0.0 copy-done.13
  106.7 0.0 copy-done.14
  106.7 0.0 copy-done.15
  106.7 0.0 copy-done.16
  106.7 0.0 copy-done.17
  106.7 0.0 copy-done.18
  106.7 0.0 copy-start
  106.7 1.1 copy-done
  107.8 1.9 %shard_map.382 = (f32[576,128]{1,0:T(8,128)}, f32[576,128]{1,0:T(8,128)}, f32[576,128]{1,0:T(8,128)}, f32[64,512]{1,0:T(8,128)}, f32[64,512]{1,0:T(8,128)}, /*in...) custom-call(f32[1368,128]{1,0:T(8,128)S(1)} %copy-done, ...), custom_call_target="tpu_custom_call" | custom-call | tf_op jit(solution)/shard_map/pallas_call | solution.py:978
Async XLA Ops:
  0.7 105.9 %copy-start.1 = (f32[576,128]{1,0:T(8,128)S(1)}, f32[576,128]{1,0:T(8,128)}, u32[]{:S(2)}) copy-start(f32[576,128]{1,0:T(8,128)} %refs_0_.3) | copy-start | bytes 884740
  0.7 105.9 %copy-start.2 = (f32[64,1000]{1,0:T(8,128)S(1)}, f32[64,1000]{1,0:T(8,128)}, u32[]{:S(2)}) copy-start(f32[64,1000]{1,0:T(8,128)} %refs_6_.3) | copy-start | bytes 768004
  0.7 105.9 %copy-start.3 = (f32[64,512]{1,0:T(8,128)S(1)}, f32[64,512]{1,0:T(8,128)}, u32[]{:S(2)}) copy-start(f32[64,512]{1,0:T(8,128)} %refs_3_.3) | copy-start | bytes 393220
  0.7 105.9 %copy-start.4 = (f32[576,128]{1,0:T(8,128)S(1)}, f32[576,128]{1,0:T(8,128)}, u32[]{:S(2)}) copy-start(f32[576,128]{1,0:T(8,128)} %refs_1_.3) | copy-start | bytes 884740
  0.7 105.9 %copy-start.5 = (f32[576,128]{1,0:T(8,128)S(1)}, f32[576,128]{1,0:T(8,128)}, u32[]{:S(2)}) copy-start(f32[576,128]{1,0:T(8,128)} %refs_2_.3) | copy-start | bytes 884740
  0.7 105.9 %copy-start.6 = (f32[64,1000]{1,0:T(8,128)S(1)}, f32[64,1000]{1,0:T(8,128)}, u32[]{:S(2)}) copy-start(f32[64,1000]{1,0:T(8,128)} %refs_7_.1) | copy-start | bytes 768004
  0.7 105.9 %copy-start.7 = (f32[64,1000]{1,0:T(8,128)S(1)}, f32[64,1000]{1,0:T(8,128)}, u32[]{:S(2)}) copy-start(f32[64,1000]{1,0:T(8,128)} %refs_8_.3) | copy-start | bytes 768004
  0.7 105.9 %copy-start.8 = (f32[64,512]{1,0:T(8,128)S(1)}, f32[64,512]{1,0:T(8,128)}, u32[]{:S(2)}) copy-start(f32[64,512]{1,0:T(8,128)} %refs_4_.3) | copy-start | bytes 393220
  0.7 105.9 %copy-start.9 = (f32[64,512]{1,0:T(8,128)S(1)}, f32[64,512]{1,0:T(8,128)}, u32[]{:S(2)}) copy-start(f32[64,512]{1,0:T(8,128)} %refs_5_.3) | copy-start | bytes 393220
  0.8 105.9 %copy-start.10 = (f32[1000]{0:T(1024)S(1)}, f32[1000]{0:T(1024)}, u32[]{:S(2)}) copy-start(f32[1000]{0:T(1024)} %param.29) | copy-start | bytes 12004
  0.8 105.9 %copy-start.11 = (f32[2,512]{1,0:T(2,128)S(1)}, f32[2,512]{1,0:T(2,128)}, u32[]{:S(2)}) copy-start(f32[2,512]{1,0:T(2,128)} %refs_12_.1) | copy-start | bytes 12292
  0.8 105.9 %copy-start.12 = (f32[1000]{0:T(1024)S(1)}, f32[1000]{0:T(1024)}, u32[]{:S(2)}) copy-start(f32[1000]{0:T(1024)} %param.38) | copy-start | bytes 12004
  0.8 105.9 %copy-start.13 = (f32[1000]{0:T(1024)S(1)}, f32[1000]{0:T(1024)}, u32[]{:S(2)}) copy-start(f32[1000]{0:T(1024)} %param.39) | copy-start | bytes 12004
  0.8 105.9 %copy-start.14 = (f32[2,512]{1,0:T(2,128)S(1)}, f32[2,512]{1,0:T(2,128)}, u32[]{:S(2)}) copy-start(f32[2,512]{1,0:T(2,128)} %refs_13_.1) | copy-start | bytes 12292
  0.8 105.9 %copy-start.15 = (f32[2,512]{1,0:T(2,128)S(1)}, f32[2,512]{1,0:T(2,128)}, u32[]{:S(2)}) copy-start(f32[2,512]{1,0:T(2,128)} %refs_14_.1) | copy-start | bytes 12292
  0.8 105.9 %copy-start.16 = (f32[2,128]{1,0:T(2,128)S(1)}, f32[2,128]{1,0:T(2,128)}, u32[]{:S(2)}) copy-start(f32[2,128]{1,0:T(2,128)} %refs_15_.1) | copy-start | bytes 3076
  0.8 105.9 %copy-start.17 = (f32[2,128]{1,0:T(2,128)S(1)}, f32[2,128]{1,0:T(2,128)}, u32[]{:S(2)}) copy-start(f32[2,128]{1,0:T(2,128)} %refs_16_.1) | copy-start | bytes 3076
  0.8 105.9 %copy-start.18 = (f32[2,128]{1,0:T(2,128)S(1)}, f32[2,128]{1,0:T(2,128)}, u32[]{:S(2)}) copy-start(f32[2,128]{1,0:T(2,128)} %refs_17_.1) | copy-start | bytes 3076
  106.7 1.1 %copy-start = (f32[1368,128]{1,0:T(8,128)S(1)}, f32[1368,128]{1,0:T(8,128)}, u32[]{:S(2)}) copy-start(f32[1368,128]{1,0:T(8,128)} %shard_map.381.grads) | copy-start | bytes 2101252

commit v4 on v3

--- a/solution.py
+++ b/solution.py
@@ -300,39 +300,74 @@
     def unit(buf, u, rows):
         return buf.at[pl.ds(pl.multiple_of(u * rows, rows), rows)]
 
-    def span(buf, units, rows):
-        return buf.at[pl.ds(0, units * rows)]
-
-    def gather_near(buf, rows, ss, rr, js):
-        mine = unit(buf, d, rows)
-        for j in js:
-            if j == 0:
-                remote(mine, mine, ss.at[0], rr.at[d], xdev).start()
-            elif j < nz:
-                remote(mine, mine, ss.at[1], rr.at[d], zdev(j)).start()
-
-    def gather_start(buf, rows, ss, rr):
-        gather_near(buf, rows, ss, rr, range(nz))
-
-    def gather_forward(buf, rows, ss, rr, j):
-        if j < nz:
-            u = flip(z, j) * 2 + x
-            got = unit(buf, u, rows)
-            copy = remote(got, got, ss.at[0], rr.at[u], xdev)
+    leftdev = ((z + nz - 1) % nz * 2 + x, c)
+    rightdev = ((z + 1) % nz * 2 + x, c)
+    has_left = lax.div(z + nz - 1, nz)
+    has_right = 1 - lax.div(z + 1, nz)
+
+    def gather_pieces(buf, rr, u):
+        pieces = rr.shape[1]
+        size = buf.shape[0] // (nd * pieces)
+        for h in range(pieces):
+            first = pl.multiple_of(u * (size * pieces) + h * size, size)
+            yield buf.at[pl.ds(first, size)], rr.at[u, h]
+
+    def gather_across(buf, ss, rr):
+        for mine, arrived in gather_pieces(buf, rr, d):
+            remote(mine, mine, ss.at[0], arrived, xdev).start()
+
+    def gather_along(buf, ss, rr):
+        for mine, arrived in gather_pieces(buf, rr, d):
+            @pl.when(has_left > 0)
+            def go_left():
+                remote(mine, mine, ss.at[1], arrived, leftdev).start()
+
+            @pl.when(has_right > 0)
+            def go_right():
+                remote(mine, mine, ss.at[2], arrived, rightdev).start()
+
+    def gather_step(buf, ss, rr, j):
+        if j >= nz:
+            return
+
+        def pass_on(got, arrived, onward, i, dev):
+            copy = remote(got, got, ss.at[0], arrived, xdev)
             copy.wait_recv()
             copy.start()
 
-    def gather_finish(buf, rows, ss, rr):
-        for j in range(nz):
-            u = flip(z, j) * 2 + 1 - x
-            got = unit(buf, u, rows)
-            remote(got, got, ss.at[0], rr.at[u], xdev).wait_recv()
-
-    def gather_drain(buf, rows, ss, rr):
-        for i, units in ((0, nz), (1, nz - 1)):
-            if units:
-                sent = span(buf, units, rows)
-                remote(sent, sent, ss.at[i], rr.at[d], xdev).wait_send()
+            @pl.when(onward > 0)
+            def go_on():
+                remote(got, got, ss.at[i], arrived, dev).start()
+
+        from_left = gather_pieces(buf, rr, (z + nz - j) % nz * 2 + x)
+        from_right = gather_pieces(buf, rr, (z + j) % nz * 2 + x)
+        for one, two in zip(from_left, from_right):
+            @pl.when(z >= j)
+            def left():
+                pass_on(*one, has_right, 2, rightdev)
+
+            @pl.when(z + j < nz)
+            def right():
+                pass_on(*two, has_left, 1, leftdev)
+
+    def gather_finish(buf, ss, rr):
+        for q in range(nz):
+            for got, arrived in gather_pieces(buf, rr, q * 2 + 1 - x):
+                remote(got, got, ss.at[0], arrived, xdev).wait_recv()
+
+    def gather_drain(buf, ss, rr):
+        def sent(i, units):
+            some = buf.at[pl.ds(0, buf.shape[0] // nd * units)]
+            remote(some, some, ss.at[i], rr.at[d, 0], xdev).wait_send()
+
+        sent(0, nz)
+        for q in range(nz):
+            @pl.when(z == q)
+            def mine(q=q):
+                if q > 0:
+                    sent(1, nz - q)
+                if q < nz - 1:
+                    sent(2, q + 1)
 
     def stats_send(buf, ss, rr):
         for p in range(1, nd):
@@ -375,15 +410,23 @@
         load.start()
 
     barrier = pltpu.get_barrier_semaphore()
-    powers = [j for j in (1, 2) if j < nz]
-    others = [sibdev, oppdev, xdev] + [zdev(j) for j in powers]
-    for dev in others:
+    for dev in (sibdev, oppdev, xdev):
         pl.semaphore_signal(barrier, inc=1, device_id=dev, device_id_type=MESH)
+
+    @pl.when(has_left > 0)
+    def greet_left():
+        pl.semaphore_signal(barrier, inc=1, device_id=leftdev, device_id_type=MESH)
+
+    @pl.when(has_right > 0)
+    def greet_right():
+        pl.semaphore_signal(barrier, inc=1, device_id=rightdev, device_id_type=MESH)
+
     loads[0].wait()
     wfull[pl.ds(pl.multiple_of(d * r1, r1), r1), :] = wf[...].astype(BF)
-    pl.semaphore_wait(barrier, len(others))
-
-    gather_near(wfull, r1, cw_s, cw_r, [0] + powers)
+    pl.semaphore_wait(barrier, 3 + has_left + has_right)
+
+    gather_across(wfull, cw_s, cw_r)
+    gather_along(wfull, cw_s, cw_r)
     for m in range(MICRO):
         src = feat.at[pl.ds(m * pm, pm)]
         remote(src, part(xv, m, c), fx_s, fx_r.at[c, m], oppdev).start()
@@ -391,6 +434,7 @@
 
     loads[1].wait()
     pfull[pl.ds(pl.multiple_of(d * rp, rp), rp), :] = pf[...].astype(BF)
+    gather_across(pfull, pw_s, pw_r)
     loads[2].wait()
     cfull[pl.ds(pl.multiple_of(d * rc, rc), rc), :] = cf[...].astype(BF)
 
@@ -426,16 +470,11 @@
     dhp[0:PAD, :] = jnp.zeros((PAD, c1l), F32)
     dhp[PAD + pm :, :] = jnp.zeros((PAD, c1l), F32)
 
-    for m in range(MICRO):
+    def pass_features(m):
         got = part(xv, m, opp)
         copy = remote(got, got, fx_s, fx_r.at[opp, m], sibdev)
         copy.wait_recv()
         copy.start()
-        if m >= 1:
-            gather_forward(wfull, r1, cw_s, cw_r, m)
-        if m == 1:
-            gather_near(wfull, r1, cw_s, cw_r, [3])
-    loads[3].wait()
 
     def take_features(m, carry):
         for chunk in (sib, dia):
@@ -448,9 +487,19 @@
             xt[m, q * c1l : (q + 1) * c1l, :] = piece.T
         return carry
 
+    gather_step(wfull, cw_s, cw_r, 1)
+    pass_features(0)
+    gather_step(wfull, cw_s, cw_r, 2)
+    gather_along(pfull, pw_s, pw_r)
+    gather_along(cfull, kw_s, kw_r)
+    pass_features(1)
+    pass_features(2)
+    loads[3].wait()
+    gather_step(wfull, cw_s, cw_r, 3)
+    gather_across(cfull, kw_s, kw_r)
+    pass_features(3)
     lax.fori_loop(0, MICRO, take_features, 0)
-    gather_finish(wfull, r1, cw_s, cw_r)
-    gather_start(pfull, rp, pw_s, pw_r)
+    gather_finish(wfull, cw_s, cw_r)
 
     def tap(t):
         return wfull[t * c1 : (t + 1) * c1, :]
@@ -493,12 +542,18 @@
         st1[m, 0, 0:1, :] = jnp.sum(valid, axis=0, keepdims=True)
         st1[m, 0, 1:2, :] = jnp.sum(valid * hidden, axis=0, keepdims=True)
         stats_send(st1.at[m], st_s.at[0, m], st_r.at[0, m])
+
+        @pl.when(m == 0)
+        def move_proj():
+            gather_step(pfull, pw_s, pw_r, 1)
+
+        @pl.when(m == 2)
+        def move_cls():
+            gather_step(cfull, kw_s, kw_r, 1)
+
         return carry
 
     lax.fori_loop(0, MICRO, conv, 0)
-    gather_start(cfull, rc, kw_s, kw_r)
-    for j in range(1, nz):
-        gather_forward(pfull, rp, pw_s, pw_r, j)
     acc[...] = jnp.zeros_like(acc)
     pacc[...] = jnp.zeros_like(pacc)
 
@@ -519,9 +574,12 @@
         remote(mine, mine, af_s, af_r.at[c, m], sibdev).start()
         return carry
 
-    lax.fori_loop(0, MICRO, activate, 0)
-    gather_forward(cfull, rc, kw_s, kw_r, 1)
-    gather_finish(pfull, rp, pw_s, pw_r)
+    activate(0, 0)
+    gather_step(pfull, pw_s, pw_r, 2)
+    lax.fori_loop(1, MICRO, activate, 0)
+    gather_step(cfull, kw_s, kw_r, 2)
+    gather_step(pfull, pw_s, pw_r, 3)
+    gather_finish(pfull, pw_s, pw_r)
     loads[4].wait()
 
     def turn(m, chunk):
@@ -706,8 +764,8 @@
             else:
                 acc[t * c1 : (t + 1) * c1, :] += mm(left, shifted(t))
 
-    def scatter_start(total, height, sbuf, xbuf, ss, rr):
-        for j in range(nz):
+    def scatter_start(total, height, sbuf, xbuf, ss, rr, js=range(nz)):
+        for j in js:
             u = flip(z, j) * 2 + 1 - x
             sbuf[j] = total[pl.ds(pl.multiple_of(u * height, height), height), :].astype(BF)
             remote(sbuf.at[j], xbuf.at[j], ss.at[0], rr.at[j], xdev).start()
@@ -749,10 +807,12 @@
             dla[cls_rows(d), classes:wide] = jnp.zeros((images, wide - classes), BF)
         mine = jnp.concatenate([pool[q] for q in range(MICRO)], axis=0).astype(BF)
         dla[cls_rows(d), wide:] = mine
-        gather_start(dla, images, dl_s, dl_r)
-
-    def start_proj():
-        scatter_start(pacc, rp, gps, gpx, gp_s, gp_r)
+        gather_across(dla, dl_s, dl_r)
+        gather_along(dla, dl_s, dl_r)
+
+    def start_proj(j):
+        if j < nz:
+            scatter_start(pacc, rp, gps, gpx, gp_s, gp_r, [j])
 
     def middle_proj():
         part_sum = scatter_middle(pacc, rp, gpx, gpz, gpr, gp_s, gp_r)
@@ -760,20 +820,22 @@
             gout[r1 + q * rp : r1 + (q + 1) * rp, :] = part_sum[:, q * 128 : (q + 1) * 128]
 
     def finish_cls():
-        gather_finish(cfull, rc, kw_s, kw_r)
+        gather_finish(cfull, kw_s, kw_r)
 
     offsets = dict(a=0, b=2, c=4, d=6, e=7, f=9, g=11)
     stages = dict(a=stage_a, b=stage_b, c=stage_c, d=stage_d, e=stage_e, f=stage_f, g=stage_g)
     hooks = {
-        (0, "a"): lambda: gather_forward(cfull, rc, kw_s, kw_r, 2),
-        (1, "a"): lambda: gather_forward(cfull, rc, kw_s, kw_r, 3),
+        (0, "a"): lambda: gather_step(cfull, kw_s, kw_r, 3),
         (2, "a"): finish_cls,
         (7, "c"): share_cls,
-        (9, "d"): start_proj,
-        (9, "g"): lambda: gather_forward(dla, images, dl_s, dl_r, 1),
-        (11, "f"): lambda: gather_forward(dla, images, dl_s, dl_r, 2),
-        (12, "f"): middle_proj,
-        (13, "f"): lambda: gather_forward(dla, images, dl_s, dl_r, 3),
+        (9, "d"): lambda: start_proj(1),
+        (10, "f"): lambda: start_proj(2),
+        (11, "e"): lambda: start_proj(3),
+        (12, "d"): lambda: start_proj(0),
+        (9, "g"): lambda: gather_step(dla, dl_s, dl_r, 1),
+        (11, "f"): lambda: gather_step(dla, dl_s, dl_r, 2),
+        (14, "f"): middle_proj,
+        (13, "f"): lambda: gather_step(dla, dl_s, dl_r, 3),
     }
 
     def step(s, carry):
@@ -797,7 +859,7 @@
 
     scatter_start(acc, r1, gcs, gcx, gc_s, gc_r)
 
-    gather_finish(dla, images, dl_s, dl_r)
+    gather_finish(dla, dl_s, dl_r)
     plt[...] = dla[:, wide:].T
     left = plt[pl.ds(pl.multiple_of(d * rc, rc), rc), :]
     row = r1 + nq * rp
@@ -828,10 +890,10 @@
     conv_part = scatter_middle(acc, r1, gcx, gcz, gcr, gc_s, gc_r)
     gout[0:r1, :] = scatter_finish(conv_part, gcr, gc_s, gc_r)
 
-    gather_drain(wfull, r1, cw_s, cw_r)
-    gather_drain(pfull, rp, pw_s, pw_r)
-    gather_drain(cfull, rc, kw_s, kw_r)
-    gather_drain(dla, images, dl_s, dl_r)
+    gather_drain(wfull, cw_s, cw_r)
+    gather_drain(pfull, pw_s, pw_r)
+    gather_drain(cfull, kw_s, kw_r)
+    gather_drain(dla, dl_s, dl_r)
     scatter_drain(gps, gpz, gp_s, gp_r)
     scatter_drain(gcs, gcz, gc_s, gc_r)
     sent = xv.at[:, pl.ds(0, 3 * c1l)]
@@ -896,7 +958,8 @@
         vmem((nz, rp, c2l), BF), vmem((nz, rp, c2l), BF),
         vmem((nd * images, wide + c2l), BF), vmem((c2l, nd * images), BF),
         dma((5,)),
-        dma((2,)), dma((nd,)), dma((2,)), dma((nd,)), dma((2,)), dma((nd,)), dma((2,)), dma((nd,)),
+        dma((3,)), dma((nd, 3)), dma((3,)), dma((nd, 1)), dma((3,)), dma((nd, 2)),
+        dma((3,)), dma((nd, 1)),
         dma, dma((nc, m4)), dma, dma((nc, m4)), dma((4, m4)), dma((4, m4)),
         dma, dma((m4,)), dma, dma((m4,)), dma, dma((m4,)),
         dma((2,)), dma((nz + 1,)), dma((2,)), dma((nz + 1,)),

time: 110 us -> 99.4 us (0.904)
  Pallas kernels: 108 us -> 97.1 us
    pallas_call x1, Pallas kernels: 106 us -> 95.1 us  [fused_gradients(): pl.pallas_call(functools.partial(fused_kernel, dims), out_shape=shape((gr...]
where the time goes in v4:
time: 99.4 us; the launch traced here: 99.2 us
  Pallas kernels  97.1 us (98%)
  local copies, waits for them, and re-layouts  1.17 us (1%)
    pallas_call x1, Pallas kernels, fused_gradients(): pl.pallas_call(functools.partial(fused_kernel, dims), out_shape=shape((gr...  95.1 us

profile of v4, /device:TPU:0, one launch (start us, length us, event | category | flops | bytes accessed | tf_op | source)
XLA Modules:
  0.0 99.2 jit_solution(11996046430367301667)
XLA Ops:
  0.7 0.0 copy-start.1
  0.7 0.0 copy-start.2
  0.7 0.0 copy-start.3
  0.7 0.0 copy-start.4
  0.7 0.0 copy-start.5
  0.7 0.0 copy-start.6
  0.7 0.0 copy-start.7
  0.7 0.0 copy-start.8
  0.7 0.0 copy-start.9
  0.8 0.0 copy-start.10
  0.8 0.0 copy-start.11
  0.8 0.0 copy-start.12
  0.8 0.0 copy-start.13
  0.8 0.0 copy-start.14
  0.8 0.0 copy-start.15
  0.8 0.0 copy-start.16
  0.8 0.0 copy-start.17
  0.8 0.0 copy-start.18
  0.8 95.1 %shard_map.381.grads = f32[1368,128]{1,0:T(8,128)} custom-call(bf16[1600,128]{1,0:T(8,128)(2,1)} %refs_0_.2, bf16[1600,512]{1,0:T(8,128)(2,1)} %refs_1_.2, s32[16,100]{1,0:T(8,128)} %refs_2_.2, s32[16]{0:T(128)} %refs_3_.2, f32[576,128]{1,0:T(8,128)} %refs_0_.3, f32[64,512]{1,0:T(8,128)} %refs_3_.3, f32[64,1000]{1,0:T(8,128)} %refs_6_.3, f32[1,1000]{1,0:T(1,128)} %bitcast.8, ...), custom_call_target="tpu_custom_call" | custom-call | tf_op jit(solution)/shard_map/pallas_call | solution.py:971
  96.0 0.0 copy-done.1
  96.0 0.0 copy-done.2
  96.0 0.0 copy-done.3
  96.0 0.0 copy-done.4
  96.0 0.0 copy-done.5
  96.0 0.0 copy-done.6
  96.0 0.0 copy-done.7
  96.0 0.0 copy-done.8
  96.1 0.0 copy-done.9
  96.1 0.0 copy-done.10
  96.1 0.0 copy-done.11
  96.1 0.0 copy-done.12
  96.1 0.0 copy-done.13
  96.1 0.0 copy-done.14
  96.1 0.0 copy-done.15
  96.1 0.0 copy-done.16
  96.1 0.0 copy-done.17
  96.1 0.0 copy-done.18
  96.2 0.0 copy-start
  96.2 1.1 %copy-done = f32[1368,128]{1,0:T(8,128)S(1)} copy-done((f32[1368,128]{1,0:T(8,128)S(1)}, f32[1368,128]{1,0:T(8,128)}, u32[]{:S(2)}) %copy-start) | copy-done | bytes 700440
  97.3 1.9 %shard_map.382 = (f32[576,128]{1,0:T(8,128)}, f32[576,128]{1,0:T(8,128)}, f32[576,128]{1,0:T(8,128)}, f32[64,512]{1,0:T(8,128)}, f32[64,512]{1,0:T(8,128)}, /*in...) custom-call(f32[1368,128]{1,0:T(8,128)S(1)} %copy-done, ...), custom_call_target="tpu_custom_call" | custom-call | tf_op jit(solution)/shard_map/pallas_call | solution.py:1041
Async XLA Ops:
  0.7 95.3 %copy-start.1 = (f32[576,128]{1,0:T(8,128)S(1)}, f32[576,128]{1,0:T(8,128)}, u32[]{:S(2)}) copy-start(f32[576,128]{1,0:T(8,128)} %refs_0_.3) | copy-start | bytes 884740
  0.7 95.3 %copy-start.2 = (f32[64,1000]{1,0:T(8,128)S(1)}, f32[64,1000]{1,0:T(8,128)}, u32[]{:S(2)}) copy-start(f32[64,1000]{1,0:T(8,128)} %refs_6_.3) | copy-start | bytes 768004
  0.7 95.3 %copy-start.3 = (f32[64,512]{1,0:T(8,128)S(1)}, f32[64,512]{1,0:T(8,128)}, u32[]{:S(2)}) copy-start(f32[64,512]{1,0:T(8,128)} %refs_3_.3) | copy-start | bytes 393220
  0.7 95.3 %copy-start.4 = (f32[576,128]{1,0:T(8,128)S(1)}, f32[576,128]{1,0:T(8,128)}, u32[]{:S(2)}) copy-start(f32[576,128]{1,0:T(8,128)} %refs_1_.3) | copy-start | bytes 884740
  0.7 95.3 %copy-start.5 = (f32[576,128]{1,0:T(8,128)S(1)}, f32[576,128]{1,0:T(8,128)}, u32[]{:S(2)}) copy-start(f32[576,128]{1,0:T(8,128)} %refs_2_.3) | copy-start | bytes 884740
  0.7 95.3 %copy-start.6 = (f32[64,1000]{1,0:T(8,128)S(1)}, f32[64,1000]{1,0:T(8,128)}, u32[]{:S(2)}) copy-start(f32[64,1000]{1,0:T(8,128)} %refs_7_.1) | copy-start | bytes 768004
  0.7 95.3 %copy-start.7 = (f32[64,1000]{1,0:T(8,128)S(1)}, f32[64,1000]{1,0:T(8,128)}, u32[]{:S(2)}) copy-start(f32[64,1000]{1,0:T(8,128)} %refs_8_.3) | copy-start | bytes 768004
  0.7 95.3 %copy-start.8 = (f32[64,512]{1,0:T(8,128)S(1)}, f32[64,512]{1,0:T(8,128)}, u32[]{:S(2)}) copy-start(f32[64,512]{1,0:T(8,128)} %refs_4_.3) | copy-start | bytes 393220
  0.7 95.3 %copy-start.9 = (f32[64,512]{1,0:T(8,128)S(1)}, f32[64,512]{1,0:T(8,128)}, u32[]{:S(2)}) copy-start(f32[64,512]{1,0:T(8,128)} %refs_5_.3) | copy-start | bytes 393220
  0.8 95.3 %copy-start.10 = (f32[1000]{0:T(1024)S(1)}, f32[1000]{0:T(1024)}, u32[]{:S(2)}) copy-start(f32[1000]{0:T(1024)} %param.29) | copy-start | bytes 12004
  0.8 95.3 %copy-start.11 = (f32[2,512]{1,0:T(2,128)S(1)}, f32[2,512]{1,0:T(2,128)}, u32[]{:S(2)}) copy-start(f32[2,512]{1,0:T(2,128)} %refs_12_.1) | copy-start | bytes 12292
  0.8 95.3 %copy-start.12 = (f32[1000]{0:T(1024)S(1)}, f32[1000]{0:T(1024)}, u32[]{:S(2)}) copy-start(f32[1000]{0:T(1024)} %param.38) | copy-start | bytes 12004
  0.8 95.3 %copy-start.13 = (f32[1000]{0:T(1024)S(1)}, f32[1000]{0:T(1024)}, u32[]{:S(2)}) copy-start(f32[1000]{0:T(1024)} %param.39) | copy-start | bytes 12004
  0.8 95.3 %copy-start.14 = (f32[2,512]{1,0:T(2,128)S(1)}, f32[2,512]{1,0:T(2,128)}, u32[]{:S(2)}) copy-start(f32[2,512]{1,0:T(2,128)} %refs_13_.1) | copy-start | bytes 12292
  0.8 95.3 %copy-start.15 = (f32[2,512]{1,0:T(2,128)S(1)}, f32[2,512]{1,0:T(2,128)}, u32[]{:S(2)}) copy-start(f32[2,512]{1,0:T(2,128)} %refs_14_.1) | copy-start | bytes 12292
  0.8 95.3 %copy-start.16 = (f32[2,128]{1,0:T(2,128)S(1)}, f32[2,128]{1,0:T(2,128)}, u32[]{:S(2)}) copy-start(f32[2,128]{1,0:T(2,128)} %refs_15_.1) | copy-start | bytes 3076
  0.8 95.3 %copy-start.17 = (f32[2,128]{1,0:T(2,128)S(1)}, f32[2,128]{1,0:T(2,128)}, u32[]{:S(2)}) copy-start(f32[2,128]{1,0:T(2,128)} %refs_16_.1) | copy-start | bytes 3076
  0.8 95.3 %copy-start.18 = (f32[2,128]{1,0:T(2,128)S(1)}, f32[2,128]{1,0:T(2,128)}, u32[]{:S(2)}) copy-start(f32[2,128]{1,0:T(2,128)} %refs_17_.1) | copy-start | bytes 3076
  96.2 1.1 %copy-start = (f32[1368,128]{1,0:T(8,128)S(1)}, f32[1368,128]{1,0:T(8,128)}, u32[]{:S(2)}) copy-start(f32[1368,128]{1,0:T(8,128)} %shard_map.381.grads) | copy-start | bytes 2101252

commit v5 on v4

--- a/solution.py
+++ b/solution.py
@@ -326,7 +326,16 @@
             def go_right():
                 remote(mine, mine, ss.at[2], arrived, rightdev).start()
 
-    def gather_step(buf, ss, rr, j):
+    outer = 1 - has_left * has_right
+
+    def gather_far(buf, ss, rr):
+        if nz == 4:
+            for mine, arrived in gather_pieces(buf, rr, d):
+                @pl.when(outer > 0)
+                def go_far():
+                    remote(mine, mine, ss.at[3], arrived, zdev(3)).start()
+
+    def gather_step(buf, ss, rr, j, relay=True):
         if j >= nz:
             return
 
@@ -335,9 +344,10 @@
             copy.wait_recv()
             copy.start()
 
-            @pl.when(onward > 0)
-            def go_on():
-                remote(got, got, ss.at[i], arrived, dev).start()
+            if relay:
+                @pl.when(onward > 0)
+                def go_on():
+                    remote(got, got, ss.at[i], arrived, dev).start()
 
         from_left = gather_pieces(buf, rr, (z + nz - j) % nz * 2 + x)
         from_right = gather_pieces(buf, rr, (z + j) % nz * 2 + x)
@@ -355,7 +365,7 @@
             for got, arrived in gather_pieces(buf, rr, q * 2 + 1 - x):
                 remote(got, got, ss.at[0], arrived, xdev).wait_recv()
 
-    def gather_drain(buf, ss, rr):
+    def gather_drain(buf, ss, rr, far=False):
         def sent(i, units):
             some = buf.at[pl.ds(0, buf.shape[0] // nd * units)]
             remote(some, some, ss.at[i], rr.at[d, 0], xdev).wait_send()
@@ -365,12 +375,14 @@
             @pl.when(z == q)
             def mine(q=q):
                 if q > 0:
-                    sent(1, nz - q)
+                    sent(1, min(nz - q, 2) if far else nz - q)
                 if q < nz - 1:
-                    sent(2, q + 1)
+                    sent(2, min(q + 1, 2) if far else q + 1)
+                if far and nz == 4 and q in (0, nz - 1):
+                    sent(3, 1)
 
     def stats_send(buf, ss, rr):
-        for p in range(1, nd):
+        for p in reversed(range(1, nd)):
             remote(buf.at[0], buf.at[p], ss, rr, (flip(d, p), c)).start()
 
     def stats_wait(buf, ss, rr):
@@ -491,6 +503,7 @@
     pass_features(0)
     gather_step(wfull, cw_s, cw_r, 2)
     gather_along(pfull, pw_s, pw_r)
+    gather_far(pfull, pw_s, pw_r)
     gather_along(cfull, kw_s, kw_r)
     pass_features(1)
     pass_features(2)
@@ -547,8 +560,16 @@
         def move_proj():
             gather_step(pfull, pw_s, pw_r, 1)
 
+        @pl.when(m == 1)
+        def move_proj_far():
+            gather_step(pfull, pw_s, pw_r, 3)
+
         @pl.when(m == 2)
         def move_cls():
+            gather_far(cfull, kw_s, kw_r)
+
+        @pl.when(m == 3)
+        def pass_cls():
             gather_step(cfull, kw_s, kw_r, 1)
 
         return carry
@@ -575,10 +596,9 @@
         return carry
 
     activate(0, 0)
-    gather_step(pfull, pw_s, pw_r, 2)
+    gather_step(pfull, pw_s, pw_r, 2, False)
     lax.fori_loop(1, MICRO, activate, 0)
-    gather_step(cfull, kw_s, kw_r, 2)
-    gather_step(pfull, pw_s, pw_r, 3)
+    gather_step(cfull, kw_s, kw_r, 3)
     gather_finish(pfull, pw_s, pw_r)
     loads[4].wait()
 
@@ -659,6 +679,8 @@
             pool[m, :, at_q] = (image_sums(summed * sigma * mask) / cnti[m]).astype(BF).astype(F32)
             tsum[m, 0, :, at_q] = image_sums(slope)
             tsum[m, 1, :, at_q] = image_sums(slope * normed)
+
+    def stage_l(m):
         lgt[m, c] = mm(pool[m].astype(BF), cfull[...])
         for dev in (oppdev, (d, dia), sibdev):
             remote(lgt.at[m, c], lgt.at[m, c], lg_s, lg_r.at[m], dev).start()
@@ -764,30 +786,74 @@
             else:
                 acc[t * c1 : (t + 1) * c1, :] += mm(left, shifted(t))
 
-    def scatter_start(total, height, sbuf, xbuf, ss, rr, js=range(nz)):
+    orders = [2, 3, 1, 0] if nz == 4 else list(range(nz))
+
+    def scatter_pieces(rr):
+        return (rr.shape[0] - 4) // nz
+
+    def scatter_start(total, sbuf, xbuf, ss, rr, js=orders):
+        height = sbuf.shape[1]
+        size = height // scatter_pieces(rr)
         for j in js:
             u = flip(z, j) * 2 + 1 - x
-            sbuf[j] = total[pl.ds(pl.multiple_of(u * height, height), height), :].astype(BF)
-            remote(sbuf.at[j], xbuf.at[j], ss.at[0], rr.at[j], xdev).start()
-
-    def scatter_middle(total, height, xbuf, zbuf, rbuf, ss, rr):
-        for j in list(range(1, nz)) + [0]:
-            remote(xbuf.at[j], xbuf.at[j], ss.at[0], rr.at[j], xdev).wait_recv()
+            for h in range(height // size):
+                at_h = pl.ds(h * size, size)
+                first = pl.multiple_of(u * height + h * size, size)
+                sbuf[j, at_h] = total[pl.ds(first, size), :].astype(BF)
+                remote(
+                    sbuf.at[j, at_h], xbuf.at[j, at_h], ss.at[0],
+                    rr.at[4 + j * (height // size) + h], xdev,
+                ).start()
+
+    def scatter_middle(total, xbuf, zbuf, rbuf, ss, rr, js, keep):
+        height = xbuf.shape[1]
+        pieces = scatter_pieces(rr)
+        size = height // pieces
+        for j in js:
             u = flip(z, j) * 2 + x
-            found = total[pl.ds(pl.multiple_of(u * height, height), height), :]
-            found = found + xbuf[j].astype(F32)
-            if j == 0:
-                return found
-            zbuf[j] = found.astype(BF)
-            remote(zbuf.at[j], rbuf.at[j], ss.at[1], rr.at[nz], zdev(j)).start()
-
-    def scatter_finish(found, rbuf, ss, rr):
-        if nz > 1:
-            got = rbuf.at[pl.ds(1, nz - 1)]
-            remote(got, got, ss.at[1], rr.at[nz], xdev).wait_recv()
-        for j in range(1, nz):
-            found = found + rbuf[j].astype(F32)
-        return found
+            for h in range(pieces):
+                at_h = pl.ds(h * size, size)
+                got = xbuf.at[j, at_h]
+                remote(got, got, ss.at[0], rr.at[4 + j * pieces + h], xdev).wait_recv()
+                first = pl.multiple_of(u * height + h * size, size)
+                found = total[pl.ds(first, size), :] + got[...].astype(F32)
+                if j == 0:
+                    keep(h * size, found)
+                    continue
+                mine = zbuf.at[j, at_h]
+                if j == 2:
+                    mine[...] = found.astype(BF)
+
+                    @pl.when(outer > 0)
+                    def out_in():
+                        to = rbuf.at[2, at_h]
+                        remote(mine, to, ss.at[1], rr.at[2], zdev(1)).start()
+
+                    @pl.when(outer == 0)
+                    def in_in():
+                        to = rbuf.at[0, at_h]
+                        remote(mine, to, ss.at[1], rr.at[0], zdev(3)).start()
+
+                    continue
+                slot = 2 if j == 3 else 0
+
+                @pl.when(outer > 0)
+                def plain():
+                    mine[...] = found.astype(BF)
+
+                @pl.when(outer == 0)
+                def added():
+                    if h == 0:
+                        relay = rbuf.at[slot]
+                        remote(relay, relay, ss.at[1], rr.at[slot], xdev).wait_recv()
+                    mine[...] = (found + rbuf[slot, at_h].astype(F32)).astype(BF)
+
+                remote(mine, rbuf.at[j, at_h], ss.at[1], rr.at[j], zdev(j)).start()
+
+    def scatter_wait(rbuf, ss, rr):
+        if nz == 4:
+            for j in (3, 1):
+                remote(rbuf.at[j], rbuf.at[j], ss.at[1], rr.at[j], xdev).wait_recv()
 
     def scatter_drain(sbuf, zbuf, ss, rr):
         remote(sbuf, sbuf, ss.at[0], rr.at[0], xdev).wait_send()
@@ -812,34 +878,39 @@
 
     def start_proj(j):
         if j < nz:
-            scatter_start(pacc, rp, gps, gpx, gp_s, gp_r, [j])
-
-    def middle_proj():
-        part_sum = scatter_middle(pacc, rp, gpx, gpz, gpr, gp_s, gp_r)
-        for q in range(nq):
-            gout[r1 + q * rp : r1 + (q + 1) * rp, :] = part_sum[:, q * 128 : (q + 1) * 128]
+            scatter_start(pacc, gps, gpx, gp_s, gp_r, [j])
+
+    def middle_proj(js):
+        def keep(first, value):
+            for q in range(nq):
+                row = r1 + q * rp + first
+                gout[row : row + value.shape[0], :] = value[:, q * 128 : (q + 1) * 128]
+
+        scatter_middle(pacc, gpx, gpz, gpr, gp_s, gp_r, js, keep)
 
     def finish_cls():
         gather_finish(cfull, kw_s, kw_r)
 
-    offsets = dict(a=0, b=2, c=4, d=6, e=7, f=9, g=11)
-    stages = dict(a=stage_a, b=stage_b, c=stage_c, d=stage_d, e=stage_e, f=stage_f, g=stage_g)
+    offsets = dict(a=0, b=2, l=3, c=5, d=8, e=9, f=12, g=14)
+    stages = dict(
+        a=stage_a, b=stage_b, l=stage_l, c=stage_c, d=stage_d, e=stage_e, f=stage_f, g=stage_g
+    )
     hooks = {
-        (0, "a"): lambda: gather_step(cfull, kw_s, kw_r, 3),
-        (2, "a"): finish_cls,
-        (7, "c"): share_cls,
-        (9, "d"): lambda: start_proj(1),
-        (10, "f"): lambda: start_proj(2),
-        (11, "e"): lambda: start_proj(3),
-        (12, "d"): lambda: start_proj(0),
-        (9, "g"): lambda: gather_step(dla, dl_s, dl_r, 1),
-        (11, "f"): lambda: gather_step(dla, dl_s, dl_r, 2),
-        (14, "f"): middle_proj,
-        (13, "f"): lambda: gather_step(dla, dl_s, dl_r, 3),
+        (0, "a"): lambda: gather_step(cfull, kw_s, kw_r, 2, False),
+        (3, "a"): finish_cls,
+        (8, "c"): share_cls,
+        (10, "d"): lambda: gather_step(dla, dl_s, dl_r, 1),
+        (11, "d"): lambda: start_proj(2),
+        (12, "e"): lambda: gather_step(dla, dl_s, dl_r, 2),
+        (12, "f"): lambda: start_proj(3),
+        (13, "f"): lambda: start_proj(1),
+        (14, "g"): lambda: gather_step(dla, dl_s, dl_r, 3),
+        (14, "f"): lambda: start_proj(0),
+        (16, "g"): lambda: middle_proj(orders[:1]),
     }
 
     def step(s, carry):
-        for name in "acbegfd":
+        for name in "alcbedgf":
             i = offsets[name]
 
             @pl.when((s >= i) & (s < i + MICRO))
@@ -857,7 +928,8 @@
 
     lax.fori_loop(0, MICRO + offsets["g"], step, 0)
 
-    scatter_start(acc, r1, gcs, gcx, gc_s, gc_r)
+    scatter_start(acc, gcs, gcx, gc_s, gc_r)
+    middle_proj(orders[1:])
 
     gather_finish(dla, dl_s, dl_r)
     plt[...] = dla[:, wide:].T
@@ -878,21 +950,24 @@
     gout[row : row + 2, :] = bn1[0, 2:4, :] + bn1[1, 2:4, :] + bn1[2, 2:4, :] + bn1[3, 2:4, :]
     loss = bn1[0, 4:5, :] + bn1[1, 4:5, :] + bn1[2, 4:5, :] + bn1[3, 4:5, :]
     gout[row + 2 : row + 3, :] = loss / total_images
-    if nz > 1:
-        got = gpr.at[pl.ds(1, nz - 1)]
-        remote(got, got, gp_s.at[1], gp_r.at[nz], xdev).wait_recv()
-    for q in range(nq):
-        share = gout[r1 + q * rp : r1 + (q + 1) * rp, :]
-        for j in range(1, nz):
-            share = share + gpr[j, :, q * 128 : (q + 1) * 128].astype(F32)
-        gout[r1 + q * rp : r1 + (q + 1) * rp, :] = share
-
-    conv_part = scatter_middle(acc, r1, gcx, gcz, gcr, gc_s, gc_r)
-    gout[0:r1, :] = scatter_finish(conv_part, gcr, gc_s, gc_r)
+    scatter_wait(gpr, gp_s, gp_r)
+    if nz == 4:
+        for q in range(nq):
+            at_q = slice(q * 128, (q + 1) * 128)
+            share = gpr[1, :, at_q].astype(F32) + gpr[3, :, at_q].astype(F32)
+            gout[r1 + q * rp : r1 + (q + 1) * rp, :] += share
+
+    def keep_conv(first, value):
+        gout[first : first + value.shape[0], :] = value
+
+    scatter_middle(acc, gcx, gcz, gcr, gc_s, gc_r, orders, keep_conv)
+    scatter_wait(gcr, gc_s, gc_r)
+    if nz == 4:
+        gout[0:r1, :] += gcr[1].astype(F32) + gcr[3].astype(F32)
 
     gather_drain(wfull, cw_s, cw_r)
-    gather_drain(pfull, pw_s, pw_r)
-    gather_drain(cfull, kw_s, kw_r)
+    gather_drain(pfull, pw_s, pw_r, True)
+    gather_drain(cfull, kw_s, kw_r, True)
     gather_drain(dla, dl_s, dl_r)
     scatter_drain(gps, gpz, gp_s, gp_r)
     scatter_drain(gcs, gcz, gc_s, gc_r)
@@ -958,11 +1033,11 @@
         vmem((nz, rp, c2l), BF), vmem((nz, rp, c2l), BF),
         vmem((nd * images, wide + c2l), BF), vmem((c2l, nd * images), BF),
         dma((5,)),
-        dma((3,)), dma((nd, 3)), dma((3,)), dma((nd, 1)), dma((3,)), dma((nd, 2)),
-        dma((3,)), dma((nd, 1)),
+        dma((4,)), dma((nd, 3)), dma((4,)), dma((nd, 1)), dma((4,)), dma((nd, 2)),
+        dma((4,)), dma((nd, 1)),
         dma, dma((nc, m4)), dma, dma((nc, m4)), dma((4, m4)), dma((4, m4)),
         dma, dma((m4,)), dma, dma((m4,)), dma, dma((m4,)),
-        dma((2,)), dma((nz + 1,)), dma((2,)), dma((nz + 1,)),
+        dma((2,)), dma((4 + 2 * nz,)), dma((2,)), dma((4 + nz,)),
     ]
     whole = pl.BlockSpec(memory_space=pltpu.VMEM)
     hbm = pl.BlockSpec(memory_space=pl.ANY)
@@ -1055,7 +1130,7 @@
     w_cls = args[6]
     fits = (
         lax.axis_size("chan") == 4
-        and lax.axis_size("dp") in (2, 4, 8)
+        and lax.axis_size("dp") in (2, 8)
         and features.shape[1] == 128
         and shortcut.shape[1] % 128 == 0
         and w_cls.shape[0] % 16 == 0

time: 99.4 us -> 93.2 us (0.938)
  Pallas kernels: 97.1 us -> 90.9 us
    pallas_call x1, Pallas kernels: 95.1 us -> 88.9 us  [fused_gradients(): pl.pallas_call(functools.partial(fused_kernel, dims), out_shape=shape((gr...]
where the time goes in v5:
time: 93.2 us; the launch traced here: 93 us
  Pallas kernels  90.9 us (98%)
  local copies, waits for them, and re-layouts  1.17 us (1%)
  between operations  0.97 us (1%)
    pallas_call x1, Pallas kernels, fused_gradients(): pl.pallas_call(functools.partial(fused_kernel, dims), out_shape=shape((gr...  88.9 us
    pallas_call x1, Pallas kernels, fused_device(): pl.pallas_call(adam_kernel, out_shape=tuple(outs), in_specs=[whole] * (le...  1.93 us

profile of v5, /device:TPU:0, one launch (start us, length us, event | category | flops | bytes accessed | tf_op | source)
XLA Modules:
  0.0 93.0 jit_solution(11646955197934736201)
XLA Ops:
  0.7 0.0 copy-start.1
  0.7 0.0 copy-start.2
  0.7 0.0 copy-start.3
  0.7 0.0 copy-start.4
  0.7 0.0 copy-start.5
  0.7 0.0 copy-start.6
  0.7 0.0 copy-start.7
  0.7 0.0 copy-start.8
  0.7 0.0 copy-start.9
  0.8 0.0 copy-start.10
  0.8 0.0 copy-start.11
  0.8 0.0 copy-start.12
  0.8 0.0 copy-start.13
  0.8 0.0 copy-start.14
  0.8 0.0 copy-start.15
  0.8 0.0 copy-start.16
  0.8 0.0 copy-start.17
  0.8 0.0 copy-start.18
  0.8 88.9 %shard_map.381.grads = f32[1368,128]{1,0:T(8,128)} custom-call(bf16[1600,128]{1,0:T(8,128)(2,1)} %refs_0_.2, bf16[1600,512]{1,0:T(8,128)(2,1)} %refs_1_.2, s32[16,100]{1,0:T(8,128)} %refs_2_.2, s32[16]{0:T(128)} %refs_3_.2, f32[576,128]{1,0:T(8,128)} %refs_0_.3, f32[64,512]{1,0:T(8,128)} %refs_3_.3, f32[64,1000]{1,0:T(8,128)} %refs_6_.3, f32[1,1000]{1,0:T(1,128)} %bitcast.8, ...), custom_call_target="tpu_custom_call" | custom-call | tf_op jit(solution)/shard_map/pallas_call | solution.py:1046
  89.8 0.0 copy-done.1
  89.8 0.0 copy-done.2
  89.8 0.0 copy-done.3
  89.8 0.0 copy-done.4
  89.8 0.0 copy-done.5
  89.8 0.0 copy-done.6
  89.8 0.0 copy-done.7
  89.9 0.0 copy-done.8
  89.9 0.0 copy-done.9
  89.9 0.0 copy-done.10
  89.9 0.0 copy-done.11
  89.9 0.0 copy-done.12
  89.9 0.0 copy-done.13
  89.9 0.0 copy-done.14
  89.9 0.0 copy-done.15
  89.9 0.0 copy-done.16
  90.0 0.0 copy-done.17
  90.0 0.0 copy-done.18
  90.0 0.0 copy-start
  90.0 1.1 %copy-done = f32[1368,128]{1,0:T(8,128)S(1)} copy-done((f32[1368,128]{1,0:T(8,128)S(1)}, f32[1368,128]{1,0:T(8,128)}, u32[]{:S(2)}) %copy-start) | copy-done | bytes 700440
  91.1 1.9 %shard_map.382 = (f32[576,128]{1,0:T(8,128)}, f32[576,128]{1,0:T(8,128)}, f32[576,128]{1,0:T(8,128)}, f32[64,512]{1,0:T(8,128)}, f32[64,512]{1,0:T(8,128)}, /*in...) custom-call(f32[1368,128]{1,0:T(8,128)S(1)} %copy-done, ...), custom_call_target="tpu_custom_call" | custom-call | tf_op jit(solution)/shard_map/pallas_call | solution.py:1116
Async XLA Ops:
  0.7 89.1 %copy-start.1 = (f32[576,128]{1,0:T(8,128)S(1)}, f32[576,128]{1,0:T(8,128)}, u32[]{:S(2)}) copy-start(f32[576,128]{1,0:T(8,128)} %refs_0_.3) | copy-start | bytes 884740
  0.7 89.1 %copy-start.2 = (f32[64,1000]{1,0:T(8,128)S(1)}, f32[64,1000]{1,0:T(8,128)}, u32[]{:S(2)}) copy-start(f32[64,1000]{1,0:T(8,128)} %refs_6_.3) | copy-start | bytes 768004
  0.7 89.1 %copy-start.3 = (f32[64,512]{1,0:T(8,128)S(1)}, f32[64,512]{1,0:T(8,128)}, u32[]{:S(2)}) copy-start(f32[64,512]{1,0:T(8,128)} %refs_3_.3) | copy-start | bytes 393220
  0.7 89.1 %copy-start.4 = (f32[576,128]{1,0:T(8,128)S(1)}, f32[576,128]{1,0:T(8,128)}, u32[]{:S(2)}) copy-start(f32[576,128]{1,0:T(8,128)} %refs_1_.3) | copy-start | bytes 884740
  0.7 89.1 %copy-start.5 = (f32[576,128]{1,0:T(8,128)S(1)}, f32[576,128]{1,0:T(8,128)}, u32[]{:S(2)}) copy-start(f32[576,128]{1,0:T(8,128)} %refs_2_.3) | copy-start | bytes 884740
  0.7 89.1 %copy-start.6 = (f32[64,1000]{1,0:T(8,128)S(1)}, f32[64,1000]{1,0:T(8,128)}, u32[]{:S(2)}) copy-start(f32[64,1000]{1,0:T(8,128)} %refs_7_.1) | copy-start | bytes 768004
  0.7 89.1 %copy-start.7 = (f32[64,1000]{1,0:T(8,128)S(1)}, f32[64,1000]{1,0:T(8,128)}, u32[]{:S(2)}) copy-start(f32[64,1000]{1,0:T(8,128)} %refs_8_.3) | copy-start | bytes 768004
  0.7 89.1 %copy-start.8 = (f32[64,512]{1,0:T(8,128)S(1)}, f32[64,512]{1,0:T(8,128)}, u32[]{:S(2)}) copy-start(f32[64,512]{1,0:T(8,128)} %refs_4_.3) | copy-start | bytes 393220
  0.7 89.1 %copy-start.9 = (f32[64,512]{1,0:T(8,128)S(1)}, f32[64,512]{1,0:T(8,128)}, u32[]{:S(2)}) copy-start(f32[64,512]{1,0:T(8,128)} %refs_5_.3) | copy-start | bytes 393220
  0.8 89.1 %copy-start.10 = (f32[1000]{0:T(1024)S(1)}, f32[1000]{0:T(1024)}, u32[]{:S(2)}) copy-start(f32[1000]{0:T(1024)} %param.29) | copy-start | bytes 12004
  0.8 89.1 %copy-start.11 = (f32[2,512]{1,0:T(2,128)S(1)}, f32[2,512]{1,0:T(2,128)}, u32[]{:S(2)}) copy-start(f32[2,512]{1,0:T(2,128)} %refs_12_.1) | copy-start | bytes 12292
  0.8 89.1 %copy-start.12 = (f32[1000]{0:T(1024)S(1)}, f32[1000]{0:T(1024)}, u32[]{:S(2)}) copy-start(f32[1000]{0:T(1024)} %param.38) | copy-start | bytes 12004
  0.8 89.1 %copy-start.13 = (f32[1000]{0:T(1024)S(1)}, f32[1000]{0:T(1024)}, u32[]{:S(2)}) copy-start(f32[1000]{0:T(1024)} %param.39) | copy-start | bytes 12004
  0.8 89.1 %copy-start.14 = (f32[2,512]{1,0:T(2,128)S(1)}, f32[2,512]{1,0:T(2,128)}, u32[]{:S(2)}) copy-start(f32[2,512]{1,0:T(2,128)} %refs_13_.1) | copy-start | bytes 12292
  0.8 89.1 %copy-start.15 = (f32[2,512]{1,0:T(2,128)S(1)}, f32[2,512]{1,0:T(2,128)}, u32[]{:S(2)}) copy-start(f32[2,512]{1,0:T(2,128)} %refs_14_.1) | copy-start | bytes 12292
  0.8 89.1 %copy-start.16 = (f32[2,128]{1,0:T(2,128)S(1)}, f32[2,128]{1,0:T(2,128)}, u32[]{:S(2)}) copy-start(f32[2,128]{1,0:T(2,128)} %refs_15_.1) | copy-start | bytes 3076
  0.8 89.1 %copy-start.17 = (f32[2,128]{1,0:T(2,128)S(1)}, f32[2,128]{1,0:T(2,128)}, u32[]{:S(2)}) copy-start(f32[2,128]{1,0:T(2,128)} %refs_16_.1) | copy-start | bytes 3076
  0.8 89.1 %copy-start.18 = (f32[2,128]{1,0:T(2,128)S(1)}, f32[2,128]{1,0:T(2,128)}, u32[]{:S(2)}) copy-start(f32[2,128]{1,0:T(2,128)} %refs_17_.1) | copy-start | bytes 3076
  90.0 1.1 %copy-start = (f32[1368,128]{1,0:T(8,128)S(1)}, f32[1368,128]{1,0:T(8,128)}, u32[]{:S(2)}) copy-start(f32[1368,128]{1,0:T(8,128)} %shard_map.381.grads) | copy-start | bytes 2101252

commit v6 on v5

--- a/solution.py
+++ b/solution.py
@@ -504,12 +504,11 @@
     gather_step(wfull, cw_s, cw_r, 2)
     gather_along(pfull, pw_s, pw_r)
     gather_far(pfull, pw_s, pw_r)
-    gather_along(cfull, kw_s, kw_r)
     pass_features(1)
     pass_features(2)
     loads[3].wait()
     gather_step(wfull, cw_s, cw_r, 3)
-    gather_across(cfull, kw_s, kw_r)
+    gather_step(pfull, pw_s, pw_r, 1)
     pass_features(3)
     lax.fori_loop(0, MICRO, take_features, 0)
     gather_finish(wfull, cw_s, cw_r)
@@ -556,25 +555,17 @@
         st1[m, 0, 1:2, :] = jnp.sum(valid * hidden, axis=0, keepdims=True)
         stats_send(st1.at[m], st_s.at[0, m], st_r.at[0, m])
 
-        @pl.when(m == 0)
-        def move_proj():
-            gather_step(pfull, pw_s, pw_r, 1)
-
-        @pl.when(m == 1)
-        def move_proj_far():
+        @pl.when(m == 3)
+        def bulk_3():
             gather_step(pfull, pw_s, pw_r, 3)
-
-        @pl.when(m == 2)
-        def move_cls():
-            gather_far(cfull, kw_s, kw_r)
-
-        @pl.when(m == 3)
-        def pass_cls():
-            gather_step(cfull, kw_s, kw_r, 1)
+            gather_step(pfull, pw_s, pw_r, 2, False)
 
         return carry
 
     lax.fori_loop(0, MICRO, conv, 0)
+    gather_along(cfull, kw_s, kw_r)
+    gather_across(cfull, kw_s, kw_r)
+    gather_far(cfull, kw_s, kw_r)
     acc[...] = jnp.zeros_like(acc)
     pacc[...] = jnp.zeros_like(pacc)
 
@@ -596,8 +587,8 @@
         return carry
 
     activate(0, 0)
-    gather_step(pfull, pw_s, pw_r, 2, False)
     lax.fori_loop(1, MICRO, activate, 0)
+    gather_step(cfull, kw_s, kw_r, 1)
     gather_step(cfull, kw_s, kw_r, 3)
     gather_finish(pfull, pw_s, pw_r)
     loads[4].wait()
@@ -895,8 +886,11 @@
     stages = dict(
         a=stage_a, b=stage_b, l=stage_l, c=stage_c, d=stage_d, e=stage_e, f=stage_f, g=stage_g
     )
+    def at_a0():
+        gather_step(cfull, kw_s, kw_r, 2, False)
+
     hooks = {
-        (0, "a"): lambda: gather_step(cfull, kw_s, kw_r, 2, False),
+        (0, "a"): at_a0,
         (3, "a"): finish_cls,
         (8, "c"): share_cls,
         (10, "d"): lambda: gather_step(dla, dl_s, dl_r, 1),
@@ -950,17 +944,20 @@
     gout[row : row + 2, :] = bn1[0, 2:4, :] + bn1[1, 2:4, :] + bn1[2, 2:4, :] + bn1[3, 2:4, :]
     loss = bn1[0, 4:5, :] + bn1[1, 4:5, :] + bn1[2, 4:5, :] + bn1[3, 4:5, :]
     gout[row + 2 : row + 3, :] = loss / total_images
+    def keep_conv(first, value):
+        gout[first : first + value.shape[0], :] = value
+
+    def middle_conv(js):
+        scatter_middle(acc, gcx, gcz, gcr, gc_s, gc_r, js, keep_conv)
+
+    middle_conv(orders[:1])
     scatter_wait(gpr, gp_s, gp_r)
     if nz == 4:
         for q in range(nq):
             at_q = slice(q * 128, (q + 1) * 128)
             share = gpr[1, :, at_q].astype(F32) + gpr[3, :, at_q].astype(F32)
             gout[r1 + q * rp : r1 + (q + 1) * rp, :] += share
-
-    def keep_conv(first, value):
-        gout[first : first + value.shape[0], :] = value
-
-    scatter_middle(acc, gcx, gcz, gcr, gc_s, gc_r, orders, keep_conv)
+    middle_conv(orders[1:])
     scatter_wait(gcr, gc_s, gc_r)
     if nz == 4:
         gout[0:r1, :] += gcr[1].astype(F32) + gcr[3].astype(F32)
@@ -1037,7 +1034,7 @@
         dma((4,)), dma((nd, 1)),
         dma, dma((nc, m4)), dma, dma((nc, m4)), dma((4, m4)), dma((4, m4)),
         dma, dma((m4,)), dma, dma((m4,)), dma, dma((m4,)),
-        dma((2,)), dma((4 + 2 * nz,)), dma((2,)), dma((4 + nz,)),
+        dma((2,)), dma((4 + 4 * nz,)), dma((2,)), dma((4 + nz,)),
     ]
     whole = pl.BlockSpec(memory_space=pltpu.VMEM)
     hbm = pl.BlockSpec(memory_space=pl.ANY)

time: 93.2 us -> 90.8 us (0.974)
  Pallas kernels: 90.9 us -> 88.5 us
    pallas_call x1, Pallas kernels: 88.9 us -> 86.6 us  [fused_gradients(): pl.pallas_call(functools.partial(fused_kernel, dims), out_shape=shape((gr...]
where the time goes in v6:
time: 90.8 us; the launch traced here: 90.7 us
  Pallas kernels  88.5 us (97%)
  local copies, waits for them, and re-layouts  1.17 us (1%)
  between operations  0.97 us (1%)
    pallas_call x1, Pallas kernels, fused_gradients(): pl.pallas_call(functools.partial(fused_kernel, dims), out_shape=shape((gr...  86.6 us
    pallas_call x1, Pallas kernels, fused_device(): pl.pallas_call(adam_kernel, out_shape=tuple(outs), in_specs=[whole] * (le...  1.93 us

profile of v6, /device:TPU:0, one launch (start us, length us, event | category | flops | bytes accessed | tf_op | source)
XLA Modules:
  0.0 90.7 jit_solution(15200188620286405351)
XLA Ops:
  0.7 0.0 copy-start.1
  0.7 0.0 copy-start.2
  0.7 0.0 copy-start.3
  0.7 0.0 copy-start.4
  0.7 0.0 copy-start.5
  0.7 0.0 copy-start.6
  0.7 0.0 copy-start.7
  0.7 0.0 copy-start.8
  0.7 0.0 copy-start.9
  0.8 0.0 copy-start.10
  0.8 0.0 copy-start.11
  0.8 0.0 copy-start.12
  0.8 0.0 copy-start.13
  0.8 0.0 copy-start.14
  0.8 0.0 copy-start.15
  0.8 0.0 copy-start.16
  0.8 0.0 copy-start.17
  0.8 0.0 copy-start.18
  0.8 86.6 %shard_map.381.grads = f32[1368,128]{1,0:T(8,128)} custom-call(bf16[1600,128]{1,0:T(8,128)(2,1)} %refs_0_.2, bf16[1600,512]{1,0:T(8,128)(2,1)} %refs_1_.2, s32[16,100]{1,0:T(8,128)} %refs_2_.2, s32[16]{0:T(128)} %refs_3_.2, f32[576,128]{1,0:T(8,128)} %refs_0_.3, f32[64,512]{1,0:T(8,128)} %refs_3_.3, f32[64,1000]{1,0:T(8,128)} %refs_6_.3, f32[1,1000]{1,0:T(1,128)} %bitcast.8, ...), custom_call_target="tpu_custom_call" | custom-call | tf_op jit(solution)/shard_map/pallas_call | solution.py:1043
  87.4 0.0 copy-done.1
  87.4 0.0 copy-done.2
  87.5 0.0 copy-done.3
  87.5 0.0 copy-done.4
  87.5 0.0 copy-done.5
  87.5 0.0 copy-done.6
  87.5 0.0 copy-done.7
  87.5 0.0 copy-done.8
  87.5 0.0 copy-done.9
  87.5 0.0 copy-done.10
  87.5 0.0 copy-done.11
  87.5 0.0 copy-done.12
  87.6 0.0 copy-done.13
  87.6 0.0 copy-done.14
  87.6 0.0 copy-done.15
  87.6 0.0 copy-done.16
  87.6 0.0 copy-done.17
  87.6 0.0 copy-done.18
  87.6 0.0 copy-start
  87.6 1.1 %copy-done = f32[1368,128]{1,0:T(8,128)S(1)} copy-done((f32[1368,128]{1,0:T(8,128)S(1)}, f32[1368,128]{1,0:T(8,128)}, u32[]{:S(2)}) %copy-start) | copy-done | bytes 700440
  88.7 1.9 %shard_map.382 = (f32[576,128]{1,0:T(8,128)}, f32[576,128]{1,0:T(8,128)}, f32[576,128]{1,0:T(8,128)}, f32[64,512]{1,0:T(8,128)}, f32[64,512]{1,0:T(8,128)}, /*in...) custom-call(f32[1368,128]{1,0:T(8,128)S(1)} %copy-done, ...), custom_call_target="tpu_custom_call" | custom-call | tf_op jit(solution)/shard_map/pallas_call | solution.py:1113
Async XLA Ops:
  0.7 86.8 %copy-start.1 = (f32[576,128]{1,0:T(8,128)S(1)}, f32[576,128]{1,0:T(8,128)}, u32[]{:S(2)}) copy-start(f32[576,128]{1,0:T(8,128)} %refs_0_.3) | copy-start | bytes 884740
  0.7 86.8 %copy-start.2 = (f32[64,1000]{1,0:T(8,128)S(1)}, f32[64,1000]{1,0:T(8,128)}, u32[]{:S(2)}) copy-start(f32[64,1000]{1,0:T(8,128)} %refs_6_.3) | copy-start | bytes 768004
  0.7 86.8 %copy-start.3 = (f32[64,512]{1,0:T(8,128)S(1)}, f32[64,512]{1,0:T(8,128)}, u32[]{:S(2)}) copy-start(f32[64,512]{1,0:T(8,128)} %refs_3_.3) | copy-start | bytes 393220
  0.7 86.8 %copy-start.4 = (f32[576,128]{1,0:T(8,128)S(1)}, f32[576,128]{1,0:T(8,128)}, u32[]{:S(2)}) copy-start(f32[576,128]{1,0:T(8,128)} %refs_1_.3) | copy-start | bytes 884740
  0.7 86.8 %copy-start.5 = (f32[576,128]{1,0:T(8,128)S(1)}, f32[576,128]{1,0:T(8,128)}, u32[]{:S(2)}) copy-start(f32[576,128]{1,0:T(8,128)} %refs_2_.3) | copy-start | bytes 884740
  0.7 86.8 %copy-start.6 = (f32[64,1000]{1,0:T(8,128)S(1)}, f32[64,1000]{1,0:T(8,128)}, u32[]{:S(2)}) copy-start(f32[64,1000]{1,0:T(8,128)} %refs_7_.1) | copy-start | bytes 768004
  0.7 86.8 %copy-start.7 = (f32[64,1000]{1,0:T(8,128)S(1)}, f32[64,1000]{1,0:T(8,128)}, u32[]{:S(2)}) copy-start(f32[64,1000]{1,0:T(8,128)} %refs_8_.3) | copy-start | bytes 768004
  0.7 86.8 %copy-start.8 = (f32[64,512]{1,0:T(8,128)S(1)}, f32[64,512]{1,0:T(8,128)}, u32[]{:S(2)}) copy-start(f32[64,512]{1,0:T(8,128)} %refs_4_.3) | copy-start | bytes 393220
  0.7 86.8 %copy-start.9 = (f32[64,512]{1,0:T(8,128)S(1)}, f32[64,512]{1,0:T(8,128)}, u32[]{:S(2)}) copy-start(f32[64,512]{1,0:T(8,128)} %refs_5_.3) | copy-start | bytes 393220
  0.8 86.8 %copy-start.10 = (f32[1000]{0:T(1024)S(1)}, f32[1000]{0:T(1024)}, u32[]{:S(2)}) copy-start(f32[1000]{0:T(1024)} %param.29) | copy-start | bytes 12004
  0.8 86.8 %copy-start.11 = (f32[2,512]{1,0:T(2,128)S(1)}, f32[2,512]{1,0:T(2,128)}, u32[]{:S(2)}) copy-start(f32[2,512]{1,0:T(2,128)} %refs_12_.1) | copy-start | bytes 12292
  0.8 86.8 %copy-start.12 = (f32[1000]{0:T(1024)S(1)}, f32[1000]{0:T(1024)}, u32[]{:S(2)}) copy-start(f32[1000]{0:T(1024)} %param.38) | copy-start | bytes 12004
  0.8 86.8 %copy-start.13 = (f32[1000]{0:T(1024)S(1)}, f32[1000]{0:T(1024)}, u32[]{:S(2)}) copy-start(f32[1000]{0:T(1024)} %param.39) | copy-start | bytes 12004
  0.8 86.8 %copy-start.14 = (f32[2,512]{1,0:T(2,128)S(1)}, f32[2,512]{1,0:T(2,128)}, u32[]{:S(2)}) copy-start(f32[2,512]{1,0:T(2,128)} %refs_13_.1) | copy-start | bytes 12292
  0.8 86.8 %copy-start.15 = (f32[2,512]{1,0:T(2,128)S(1)}, f32[2,512]{1,0:T(2,128)}, u32[]{:S(2)}) copy-start(f32[2,512]{1,0:T(2,128)} %refs_14_.1) | copy-start | bytes 12292
  0.8 86.8 %copy-start.16 = (f32[2,128]{1,0:T(2,128)S(1)}, f32[2,128]{1,0:T(2,128)}, u32[]{:S(2)}) copy-start(f32[2,128]{1,0:T(2,128)} %refs_15_.1) | copy-start | bytes 3076
  0.8 86.8 %copy-start.17 = (f32[2,128]{1,0:T(2,128)S(1)}, f32[2,128]{1,0:T(2,128)}, u32[]{:S(2)}) copy-start(f32[2,128]{1,0:T(2,128)} %refs_16_.1) | copy-start | bytes 3076
  0.8 86.8 %copy-start.18 = (f32[2,128]{1,0:T(2,128)S(1)}, f32[2,128]{1,0:T(2,128)}, u32[]{:S(2)}) copy-start(f32[2,128]{1,0:T(2,128)} %refs_17_.1) | copy-start | bytes 3076
  87.6 1.1 %copy-start = (f32[1368,128]{1,0:T(8,128)S(1)}, f32[1368,128]{1,0:T(8,128)}, u32[]{:S(2)}) copy-start(f32[1368,128]{1,0:T(8,128)} %shard_map.381.grads) | copy-start | bytes 2101252

commit v7 on v6

--- a/solution.py
+++ b/solution.py
@@ -266,8 +266,8 @@
 def fused_kernel(dims, *refs):
     nd, nc, pm, imb, c1l, c2l, r1, rp, rc, classes, total_images = dims
     (
-        feat, short, masks, labels, wconv, wproj, wcls, cbias, n1, n2, gout,
-        wf, pf, cf, wfull, pfull, cfull, xv, sv, xm, xt, yb, hid, mk, edge, cntm, cnti,
+        feat, short, masks_in, labels, wconv, wproj, wcls, cbias_in, n1_in, n2_in, gout,
+        masks, cbias, n1, n2, wf, pf, cf, wfull, pfull, cfull, xv, sv, xm, xt, yb, hid, mk, edge, cntm, cnti,
         af, at, sec, slp, bn1, bn2, tsum, pool, lgt, dlm, dpd, dsb, da, dab, sr, es, er,
         du, dhp, acc, pacc, st1, st2, st3, st4,
         gcs, gcx, gcz, gcr, gps, gpx, gpz, gpr, dla, plt,
@@ -310,11 +310,11 @@
         size = buf.shape[0] // (nd * pieces)
         for h in range(pieces):
             first = pl.multiple_of(u * (size * pieces) + h * size, size)
-            yield buf.at[pl.ds(first, size)], rr.at[u, h]
+            yield buf.at[pl.ds(first, size)], rr.at[lax.div(u, 2), h]
 
     def gather_across(buf, ss, rr):
-        for mine, arrived in gather_pieces(buf, rr, d):
-            remote(mine, mine, ss.at[0], arrived, xdev).start()
+        for mine, _ in gather_pieces(buf, rr, d):
+            remote(mine, mine, ss.at[0], rr.at[nz, 0], xdev).start()
 
     def gather_along(buf, ss, rr):
         for mine, arrived in gather_pieces(buf, rr, d):
@@ -340,9 +340,8 @@
             return
 
         def pass_on(got, arrived, onward, i, dev):
-            copy = remote(got, got, ss.at[0], arrived, xdev)
-            copy.wait_recv()
-            copy.start()
+            remote(got, got, ss.at[0], arrived, xdev).wait_recv()
+            remote(got, got, ss.at[0], rr.at[nz, 0], xdev).start()
 
             if relay:
                 @pl.when(onward > 0)
@@ -361,14 +360,13 @@
                 pass_on(*two, has_left, 1, leftdev)
 
     def gather_finish(buf, ss, rr):
-        for q in range(nz):
-            for got, arrived in gather_pieces(buf, rr, q * 2 + 1 - x):
-                remote(got, got, ss.at[0], arrived, xdev).wait_recv()
+        got = buf.at[pl.ds(0, buf.shape[0] // 2)]
+        remote(got, got, ss.at[0], rr.at[nz, 0], xdev).wait_recv()
 
     def gather_drain(buf, ss, rr, far=False):
         def sent(i, units):
             some = buf.at[pl.ds(0, buf.shape[0] // nd * units)]
-            remote(some, some, ss.at[i], rr.at[d, 0], xdev).wait_send()
+            remote(some, some, ss.at[i], rr.at[nz, 0], xdev).wait_send()
 
         sent(0, nz)
         for q in range(nz):
@@ -396,8 +394,8 @@
         return total
 
     def stats_drain(buf, ss, rr):
-        got = buf.at[pl.ds(1, nd - 1)]
-        remote(got, got, ss, rr, xdev).wait_send()
+        sent = buf.at[:, pl.ds(1, nd - 1)]
+        remote(sent, sent, ss, rr, xdev).wait_send()
 
     def rows(m):
         return pl.ds(pl.multiple_of(m * pm, pm), pm)
@@ -417,9 +415,12 @@
         local(wcls, cf, 2),
         local(feat, xv.at[:, lanes(c)], 3),
         local(short, sv, 4),
+        local(masks_in, masks, 5),
+        local(cbias_in, cbias, 6),
+        local(n1_in, n1, 7),
+        local(n2_in, n2, 8),
     ]
-    for load in loads:
-        load.start()
+    loads[0].start()
 
     barrier = pltpu.get_barrier_semaphore()
     for dev in (sibdev, oppdev, xdev):
@@ -433,6 +434,8 @@
     def greet_right():
         pl.semaphore_signal(barrier, inc=1, device_id=rightdev, device_id_type=MESH)
 
+    for i in (1, 2, 5, 3, 4, 6, 7, 8):
+        loads[i].start()
     loads[0].wait()
     wfull[pl.ds(pl.multiple_of(d * r1, r1), r1), :] = wf[...].astype(BF)
     pl.semaphore_wait(barrier, 3 + has_left + has_right)
@@ -441,8 +444,8 @@
     gather_along(wfull, cw_s, cw_r)
     for m in range(MICRO):
         src = feat.at[pl.ds(m * pm, pm)]
-        remote(src, part(xv, m, c), fx_s, fx_r.at[c, m], oppdev).start()
-        remote(src, part(xv, m, c), fx_s, fx_r.at[c, m], sibdev).start()
+        remote(src, part(xv, m, c), fx_s, fx_r.at[0, m], oppdev).start()
+        remote(src, part(xv, m, c), fx_s, fx_r.at[1, m], sibdev).start()
 
     loads[1].wait()
     pfull[pl.ds(pl.multiple_of(d * rp, rp), rp), :] = pf[...].astype(BF)
@@ -463,6 +466,7 @@
     edge[1] = (line < SIDE - 1).astype(F32)
     edge[2] = (across > 0).astype(F32)
     edge[3] = (across < SIDE - 1).astype(F32)
+    loads[5].wait()
     mask_bf = masks[...].astype(F32).astype(BF)
     images = imb * MICRO
     chosen = (pixel[:, :AREA] == lane_iota((pm, AREA))).astype(F32)
@@ -484,14 +488,12 @@
 
     def pass_features(m):
         got = part(xv, m, opp)
-        copy = remote(got, got, fx_s, fx_r.at[opp, m], sibdev)
-        copy.wait_recv()
-        copy.start()
+        remote(got, got, fx_s, fx_r.at[0, m], sibdev).wait_recv()
+        remote(got, got, fx_s, fx_r.at[1, m], sibdev).start()
 
     def take_features(m, carry):
-        for chunk in (sib, dia):
-            got = part(xv, m, chunk)
-            remote(got, got, fx_s, fx_r.at[chunk, m], sibdev).wait_recv()
+        got = xv.at[rows(m), pl.ds(0, 2 * c1l)]
+        remote(got, got, fx_s, fx_r.at[1, m], sibdev).wait_recv()
         flat_mask = mk[m].astype(BF)
         for q in range(nc):
             piece = xv[rows(m), q * c1l : (q + 1) * c1l] * flat_mask
@@ -507,6 +509,7 @@
     pass_features(1)
     pass_features(2)
     loads[3].wait()
+    loads[7].wait()
     gather_step(wfull, cw_s, cw_r, 3)
     gather_step(pfull, pw_s, pw_r, 1)
     pass_features(3)
@@ -553,24 +556,27 @@
         valid = hidden * mk[m]
         st1[m, 0, 0:1, :] = jnp.sum(valid, axis=0, keepdims=True)
         st1[m, 0, 1:2, :] = jnp.sum(valid * hidden, axis=0, keepdims=True)
-        stats_send(st1.at[m], st_s.at[0, m], st_r.at[0, m])
-
-        @pl.when(m == 3)
-        def bulk_3():
+        stats_send(st1.at[m], st_s.at[0], st_r.at[0, m])
+
+        @pl.when(m == 2)
+        def bulk_at_2():
             gather_step(pfull, pw_s, pw_r, 3)
             gather_step(pfull, pw_s, pw_r, 2, False)
 
+        @pl.when(m == 3)
+        def bulk_at_3():
+            gather_along(cfull, kw_s, kw_r)
+            gather_across(cfull, kw_s, kw_r)
+            gather_far(cfull, kw_s, kw_r)
+
         return carry
 
     lax.fori_loop(0, MICRO, conv, 0)
-    gather_along(cfull, kw_s, kw_r)
-    gather_across(cfull, kw_s, kw_r)
-    gather_far(cfull, kw_s, kw_r)
     acc[...] = jnp.zeros_like(acc)
     pacc[...] = jnp.zeros_like(pacc)
 
     def activate(m, carry):
-        stats_wait(st1.at[m], st_s.at[0, m], st_r.at[0, m])
+        stats_wait(st1.at[m], st_s.at[0], st_r.at[0, m])
         totals = stats_sum(st1.at[m])
         n = totals[2:3]
         cntm[m] = n
@@ -582,8 +588,8 @@
         active = (shifted * sigmoid(shifted) * mk[m]).astype(BF)
         mine = part(af, m, c)
         mine[...] = active
-        remote(mine, mine, af_s, af_r.at[c, m], oppdev).start()
-        remote(mine, mine, af_s, af_r.at[c, m], sibdev).start()
+        remote(mine, mine, af_s, af_r.at[0, m], oppdev).start()
+        remote(mine, mine, af_s, af_r.at[1, m], sibdev).start()
         return carry
 
     activate(0, 0)
@@ -592,6 +598,8 @@
     gather_step(cfull, kw_s, kw_r, 3)
     gather_finish(pfull, pw_s, pw_r)
     loads[4].wait()
+    loads[6].wait()
+    loads[8].wait()
 
     def turn(m, chunk):
         at[m, lanes_sub(chunk), :] = part(af, m, chunk)[...].T
@@ -601,16 +609,13 @@
 
     def stage_a(m):
         got = part(af, m, opp)
-        copy = remote(got, got, af_s, af_r.at[opp, m], sibdev)
-        copy.wait_recv()
-        copy.start()
+        remote(got, got, af_s, af_r.at[0, m], sibdev).wait_recv()
+        remote(got, got, af_s, af_r.at[1, m], sibdev).start()
         turn(m, c)
         turn(m, opp)
-        got = part(af, m, sib)
-        remote(got, got, af_s, af_r.at[sib, m], sibdev).wait_recv()
+        got = af.at[rows(m), pl.ds(0, 2 * c1l)]
+        remote(got, got, af_s, af_r.at[1, m], sibdev).wait_recv()
         turn(m, sib)
-        got = part(af, m, dia)
-        remote(got, got, af_s, af_r.at[dia, m], sibdev).wait_recv()
         turn(m, dia)
         second = mm(af[rows(m), :], pfull[...])
         sec[m] = second
@@ -620,7 +625,7 @@
             valid = piece * mask
             st2[m, 0, q : q + 1, :] = jnp.sum(valid, axis=0, keepdims=True)
             st2[m, 0, nq + q : nq + q + 1, :] = jnp.sum(valid * piece, axis=0, keepdims=True)
-        stats_send(st2.at[m], st_s.at[1, m], st_r.at[1, m])
+        stats_send(st2.at[m], st_s.at[1], st_r.at[1, m])
 
     low_half = row_iota((2, 8, 128)) * 0 + lax.broadcasted_iota(jnp.int32, (2, 8, 128), 1)
     tiles = AREA // 4
@@ -650,7 +655,7 @@
         return jnp.concatenate(pieces, axis=0).reshape(pm, 128)
 
     def stage_b(m):
-        stats_wait(st2.at[m], st_s.at[1, m], st_r.at[1, m])
+        stats_wait(st2.at[m], st_s.at[1], st_r.at[1, m])
         total = stats_sum(st2.at[m])
         n = cntm[m]
         mask = mk[m]
@@ -705,10 +710,10 @@
             st3[m, 0, nq + q : nq + q + 1, :] = jnp.sum(
                 value * tsum[m, 1, :, at_q], axis=0, keepdims=True
             )
-        stats_send(st3.at[m], st_s.at[2, m], st_r.at[2, m])
+        stats_send(st3.at[m], st_s.at[2], st_r.at[2, m])
 
     def stage_d(m):
-        stats_wait(st3.at[m], st_s.at[2, m], st_r.at[2, m])
+        stats_wait(st3.at[m], st_s.at[2], st_r.at[2, m])
         total = stats_sum(st3.at[m])
         n = cntm[m]
         mask = mk[m]
@@ -747,10 +752,10 @@
         du[m] = upstream
         st4[m, 0, 0:1, :] = jnp.sum(upstream, axis=0, keepdims=True)
         st4[m, 0, 1:2, :] = jnp.sum(upstream * normed, axis=0, keepdims=True)
-        stats_send(st4.at[m], st_s.at[3, m], st_r.at[3, m])
+        stats_send(st4.at[m], st_s.at[3], st_r.at[3, m])
 
     def stage_g(m):
-        stats_wait(st4.at[m], st_s.at[3, m], st_r.at[3, m])
+        stats_wait(st4.at[m], st_s.at[3], st_r.at[3, m])
         total = stats_sum(st4.at[m])
         n = cntm[m]
         bn1[m, 2:3, :] = total[1:2]
@@ -882,7 +887,7 @@
     def finish_cls():
         gather_finish(cfull, kw_s, kw_r)
 
-    offsets = dict(a=0, b=2, l=3, c=5, d=8, e=9, f=12, g=14)
+    offsets = dict(a=0, b=2, l=3, c=5, d=8, e=9, f=11, g=13)
     stages = dict(
         a=stage_a, b=stage_b, l=stage_l, c=stage_c, d=stage_d, e=stage_e, f=stage_f, g=stage_g
     )
@@ -894,17 +899,17 @@
         (3, "a"): finish_cls,
         (8, "c"): share_cls,
         (10, "d"): lambda: gather_step(dla, dl_s, dl_r, 1),
-        (11, "d"): lambda: start_proj(2),
+        (11, "f"): lambda: start_proj(2),
         (12, "e"): lambda: gather_step(dla, dl_s, dl_r, 2),
         (12, "f"): lambda: start_proj(3),
         (13, "f"): lambda: start_proj(1),
         (14, "g"): lambda: gather_step(dla, dl_s, dl_r, 3),
         (14, "f"): lambda: start_proj(0),
-        (16, "g"): lambda: middle_proj(orders[:1]),
+        (16, "b"): lambda: middle_proj(orders[:1]),
     }
 
     def step(s, carry):
-        for name in "alcbedgf":
+        for name in "alcbedfg":
             i = offsets[name]
 
             @pl.when((s >= i) & (s < i + MICRO))
@@ -977,12 +982,8 @@
     remote(sr, sr, sr_s, sr_r.at[0], sibdev).wait_send()
     remote(es, es, er_s, er_r.at[0], oppdev).wait_send()
 
-    def drain(m, carry):
-        for i, buf in enumerate((st1, st2, st3, st4)):
-            stats_drain(buf.at[m], st_s.at[i, m], st_r.at[i, m])
-        return carry
-
-    lax.fori_loop(0, MICRO, drain, 0)
+    for i, buf in enumerate((st1, st2, st3, st4)):
+        stats_drain(buf, st_s.at[i], st_r.at[i, 0])
 
 
 def fused_gradients(
@@ -1006,6 +1007,8 @@
     dma = pltpu.SemaphoreType.DMA
     m4 = MICRO
     scratch = [
+        vmem((images, SIDE * SIDE), jnp.int32), vmem((1, classes), F32),
+        vmem((2, c1l), F32), vmem((2, c2l), F32),
         vmem((r1, c1l), F32), vmem((rp, c2l), F32), vmem((rc, classes), F32),
         vmem((9 * c1, c1l), BF), vmem((c1, c2l), BF), vmem((c2l, classes), BF),
         vmem((pixels, c1), BF), vmem((pixels, c2l), BF),
@@ -1029,10 +1032,10 @@
         vmem((nz, rp, c2l), BF), vmem((nz, rp, c2l), BF),
         vmem((nz, rp, c2l), BF), vmem((nz, rp, c2l), BF),
         vmem((nd * images, wide + c2l), BF), vmem((c2l, nd * images), BF),
-        dma((5,)),
-        dma((4,)), dma((nd, 3)), dma((4,)), dma((nd, 1)), dma((4,)), dma((nd, 2)),
-        dma((4,)), dma((nd, 1)),
-        dma, dma((nc, m4)), dma, dma((nc, m4)), dma((4, m4)), dma((4, m4)),
+        dma((9,)),
+        dma((4,)), dma((nz + 1, 3)), dma((4,)), dma((nz + 1, 1)), dma((4,)), dma((nz + 1, 2)),
+        dma((4,)), dma((nz + 1, 1)),
+        dma, dma((2, m4)), dma, dma((2, m4)), dma((4,)), dma((4, m4)),
         dma, dma((m4,)), dma, dma((m4,)), dma, dma((m4,)),
         dma((2,)), dma((4 + 4 * nz,)), dma((2,)), dma((4 + nz,)),
     ]
@@ -1043,7 +1046,7 @@
     return pl.pallas_call(
         functools.partial(fused_kernel, dims),
         out_shape=shape((grad_rows, 128), F32),
-        in_specs=[hbm, hbm, whole, scalar, hbm, hbm, hbm, whole, whole, whole],
+        in_specs=[hbm, hbm, hbm, scalar, hbm, hbm, hbm, hbm, hbm, hbm],
         out_specs=whole,
         scratch_shapes=scratch,
         compiler_params=pltpu.CompilerParams(

time: 90.8 us -> 88.7 us (0.977)
  Pallas kernels: 88.5 us -> 86.3 us
    pallas_call x1, Pallas kernels: 86.6 us -> 84.4 us  [fused_gradients(): pl.pallas_call(functools.partial(fused_kernel, dims), out_shape=shape((gr...]
where the time goes in v7:
time: 88.7 us; the launch traced here: 88.5 us
  Pallas kernels  86.3 us (97%)
  local copies, waits for them, and re-layouts  1.17 us (1%)
  between operations  0.97 us (1%)
    pallas_call x1, Pallas kernels, fused_gradients(): pl.pallas_call(functools.partial(fused_kernel, dims), out_shape=shape((gr...  84.4 us
    pallas_call x1, Pallas kernels, fused_device(): pl.pallas_call(adam_kernel, out_shape=tuple(outs), in_specs=[whole] * (le...  1.93 us

profile of v7, /device:TPU:0, one launch (start us, length us, event | category | flops | bytes accessed | tf_op | source)
XLA Modules:
  0.0 88.5 jit_solution(1501513588755227861)
XLA Ops:
  0.7 0.0 copy-start.1
  0.7 0.0 copy-start.2
  0.7 0.0 copy-start.3
  0.7 0.0 copy-start.4
  0.7 0.0 copy-start.5
  0.7 0.0 copy-start.6
  0.7 0.0 copy-start.7
  0.7 0.0 copy-start.8
  0.7 0.0 copy-start.9
  0.8 0.0 copy-start.10
  0.8 0.0 copy-start.11
  0.8 0.0 copy-start.12
  0.8 0.0 copy-start.13
  0.8 0.0 copy-start.14
  0.8 0.0 copy-start.15
  0.8 0.0 copy-start.16
  0.8 0.0 copy-start.17
  0.8 0.0 copy-start.18
  0.8 84.4 %shard_map.381.grads = f32[1368,128]{1,0:T(8,128)} custom-call(bf16[1600,128]{1,0:T(8,128)(2,1)} %refs_0_.2, bf16[1600,512]{1,0:T(8,128)(2,1)} %refs_1_.2, s32[16,100]{1,0:T(8,128)} %refs_2_.2, s32[16]{0:T(128)} %refs_3_.2, f32[576,128]{1,0:T(8,128)} %refs_0_.3, f32[64,512]{1,0:T(8,128)} %refs_3_.3, f32[64,1000]{1,0:T(8,128)} %refs_6_.3, f32[1,1000]{1,0:T(1,128)} %bitcast.8, ...), custom_call_target="tpu_custom_call" | custom-call | tf_op jit(solution)/shard_map/pallas_call | solution.py:1046
  85.3 0.0 copy-done.1
  85.3 0.0 copy-done.2
  85.3 0.0 copy-done.3
  85.3 0.0 copy-done.4
  85.3 0.0 copy-done.5
  85.3 0.0 copy-done.6
  85.3 0.0 copy-done.7
  85.3 0.0 copy-done.8
  85.3 0.0 copy-done.9
  85.4 0.0 copy-done.10
  85.4 0.0 copy-done.11
  85.4 0.0 copy-done.12
  85.4 0.0 copy-done.13
  85.4 0.0 copy-done.14
  85.4 0.0 copy-done.15
  85.4 0.0 copy-done.16
  85.4 0.0 copy-done.17
  85.4 0.0 copy-done.18
  85.4 0.0 copy-start
  85.5 1.1 %copy-done = f32[1368,128]{1,0:T(8,128)S(1)} copy-done((f32[1368,128]{1,0:T(8,128)S(1)}, f32[1368,128]{1,0:T(8,128)}, u32[]{:S(2)}) %copy-start) | copy-done | bytes 700440
  86.5 1.9 %shard_map.382 = (f32[576,128]{1,0:T(8,128)}, f32[576,128]{1,0:T(8,128)}, f32[576,128]{1,0:T(8,128)}, f32[64,512]{1,0:T(8,128)}, f32[64,512]{1,0:T(8,128)}, /*in...) custom-call(f32[1368,128]{1,0:T(8,128)S(1)} %copy-done, ...), custom_call_target="tpu_custom_call" | custom-call | tf_op jit(solution)/shard_map/pallas_call | solution.py:1116
Async XLA Ops:
  0.7 84.6 %copy-start.1 = (f32[576,128]{1,0:T(8,128)S(1)}, f32[576,128]{1,0:T(8,128)}, u32[]{:S(2)}) copy-start(f32[576,128]{1,0:T(8,128)} %refs_0_.3) | copy-start | bytes 884740
  0.7 84.6 %copy-start.2 = (f32[64,1000]{1,0:T(8,128)S(1)}, f32[64,1000]{1,0:T(8,128)}, u32[]{:S(2)}) copy-start(f32[64,1000]{1,0:T(8,128)} %refs_6_.3) | copy-start | bytes 768004
  0.7 84.6 %copy-start.3 = (f32[64,512]{1,0:T(8,128)S(1)}, f32[64,512]{1,0:T(8,128)}, u32[]{:S(2)}) copy-start(f32[64,512]{1,0:T(8,128)} %refs_3_.3) | copy-start | bytes 393220
  0.7 84.6 %copy-start.4 = (f32[576,128]{1,0:T(8,128)S(1)}, f32[576,128]{1,0:T(8,128)}, u32[]{:S(2)}) copy-start(f32[576,128]{1,0:T(8,128)} %refs_1_.3) | copy-start | bytes 884740
  0.7 84.6 %copy-start.5 = (f32[576,128]{1,0:T(8,128)S(1)}, f32[576,128]{1,0:T(8,128)}, u32[]{:S(2)}) copy-start(f32[576,128]{1,0:T(8,128)} %refs_2_.3) | copy-start | bytes 884740
  0.7 84.6 %copy-start.6 = (f32[64,1000]{1,0:T(8,128)S(1)}, f32[64,1000]{1,0:T(8,128)}, u32[]{:S(2)}) copy-start(f32[64,1000]{1,0:T(8,128)} %refs_7_.1) | copy-start | bytes 768004
  0.7 84.6 %copy-start.7 = (f32[64,1000]{1,0:T(8,128)S(1)}, f32[64,1000]{1,0:T(8,128)}, u32[]{:S(2)}) copy-start(f32[64,1000]{1,0:T(8,128)} %refs_8_.3) | copy-start | bytes 768004
  0.7 84.6 %copy-start.8 = (f32[64,512]{1,0:T(8,128)S(1)}, f32[64,512]{1,0:T(8,128)}, u32[]{:S(2)}) copy-start(f32[64,512]{1,0:T(8,128)} %refs_4_.3) | copy-start | bytes 393220
  0.7 84.6 %copy-start.9 = (f32[64,512]{1,0:T(8,128)S(1)}, f32[64,512]{1,0:T(8,128)}, u32[]{:S(2)}) copy-start(f32[64,512]{1,0:T(8,128)} %refs_5_.3) | copy-start | bytes 393220
  0.8 84.6 %copy-start.10 = (f32[1000]{0:T(1024)S(1)}, f32[1000]{0:T(1024)}, u32[]{:S(2)}) copy-start(f32[1000]{0:T(1024)} %param.29) | copy-start | bytes 12004
  0.8 84.6 %copy-start.11 = (f32[2,512]{1,0:T(2,128)S(1)}, f32[2,512]{1,0:T(2,128)}, u32[]{:S(2)}) copy-start(f32[2,512]{1,0:T(2,128)} %refs_12_.1) | copy-start | bytes 12292
  0.8 84.6 %copy-start.12 = (f32[1000]{0:T(1024)S(1)}, f32[1000]{0:T(1024)}, u32[]{:S(2)}) copy-start(f32[1000]{0:T(1024)} %param.38) | copy-start | bytes 12004
  0.8 84.6 %copy-start.13 = (f32[1000]{0:T(1024)S(1)}, f32[1000]{0:T(1024)}, u32[]{:S(2)}) copy-start(f32[1000]{0:T(1024)} %param.39) | copy-start | bytes 12004
  0.8 84.6 %copy-start.14 = (f32[2,512]{1,0:T(2,128)S(1)}, f32[2,512]{1,0:T(2,128)}, u32[]{:S(2)}) copy-start(f32[2,512]{1,0:T(2,128)} %refs_13_.1) | copy-start | bytes 12292
  0.8 84.6 %copy-start.15 = (f32[2,512]{1,0:T(2,128)S(1)}, f32[2,512]{1,0:T(2,128)}, u32[]{:S(2)}) copy-start(f32[2,512]{1,0:T(2,128)} %refs_14_.1) | copy-start | bytes 12292
  0.8 84.6 %copy-start.16 = (f32[2,128]{1,0:T(2,128)S(1)}, f32[2,128]{1,0:T(2,128)}, u32[]{:S(2)}) copy-start(f32[2,128]{1,0:T(2,128)} %refs_15_.1) | copy-start | bytes 3076
  0.8 84.6 %copy-start.17 = (f32[2,128]{1,0:T(2,128)S(1)}, f32[2,128]{1,0:T(2,128)}, u32[]{:S(2)}) copy-start(f32[2,128]{1,0:T(2,128)} %refs_16_.1) | copy-start | bytes 3076
  0.8 84.6 %copy-start.18 = (f32[2,128]{1,0:T(2,128)S(1)}, f32[2,128]{1,0:T(2,128)}, u32[]{:S(2)}) copy-start(f32[2,128]{1,0:T(2,128)} %refs_17_.1) | copy-start | bytes 3076
  85.4 1.1 %copy-start = (f32[1368,128]{1,0:T(8,128)S(1)}, f32[1368,128]{1,0:T(8,128)}, u32[]{:S(2)}) copy-start(f32[1368,128]{1,0:T(8,128)} %shard_map.381.grads) | copy-start | bytes 2101252

commit v8 on v7

--- a/solution.py
+++ b/solution.py
@@ -266,8 +266,8 @@
 def fused_kernel(dims, *refs):
     nd, nc, pm, imb, c1l, c2l, r1, rp, rc, classes, total_images = dims
     (
-        feat, short, masks_in, labels, wconv, wproj, wcls, cbias_in, n1_in, n2_in, gout,
-        masks, cbias, n1, n2, wf, pf, cf, wfull, pfull, cfull, xv, sv, xm, xt, yb, hid, mk, edge, cntm, cnti,
+        feat, short, masks_in, labels, wconv, wproj, wcls, cbias_in, n1_in, n2_in, out,
+        gout, masks, cbias, n1, n2, wf, pf, cf, wfull, pfull, cfull, xv, sv, xm, xt, yb, hid, mk, edge, cntm, cnti,
         af, at, sec, slp, bn1, bn2, tsum, pool, lgt, dlm, dpd, dsb, da, dab, sr, es, er,
         du, dhp, acc, pacc, st1, st2, st3, st4,
         gcs, gcx, gcz, gcr, gps, gpx, gpz, gpr, dla, plt,
@@ -949,6 +949,9 @@
     gout[row : row + 2, :] = bn1[0, 2:4, :] + bn1[1, 2:4, :] + bn1[2, 2:4, :] + bn1[3, 2:4, :]
     loss = bn1[0, 4:5, :] + bn1[1, 4:5, :] + bn1[2, 4:5, :] + bn1[3, 4:5, :]
     gout[row + 2 : row + 3, :] = loss / total_images
+    row = row + 3
+    if row < gout.shape[0]:
+        gout[row:, :] = jnp.zeros((gout.shape[0] - row, 128), F32)
     def keep_conv(first, value):
         gout[first : first + value.shape[0], :] = value
 
@@ -962,11 +965,16 @@
             at_q = slice(q * 128, (q + 1) * 128)
             share = gpr[1, :, at_q].astype(F32) + gpr[3, :, at_q].astype(F32)
             gout[r1 + q * rp : r1 + (q + 1) * rp, :] += share
+    rest = gout.shape[0] - r1
+    small_out = local(gout.at[pl.ds(r1, rest)], out.at[pl.ds(r1, rest)], 9)
+    small_out.start()
     middle_conv(orders[1:])
     scatter_wait(gcr, gc_s, gc_r)
     if nz == 4:
         gout[0:r1, :] += gcr[1].astype(F32) + gcr[3].astype(F32)
 
+    conv_out = local(gout.at[pl.ds(0, r1)], out.at[pl.ds(0, r1)], 10)
+    conv_out.start()
     gather_drain(wfull, cw_s, cw_r)
     gather_drain(pfull, pw_s, pw_r, True)
     gather_drain(cfull, kw_s, kw_r, True)
@@ -984,6 +992,8 @@
 
     for i, buf in enumerate((st1, st2, st3, st4)):
         stats_drain(buf, st_s.at[i], st_r.at[i, 0])
+    small_out.wait()
+    conv_out.wait()
 
 
 def fused_gradients(
@@ -1007,6 +1017,7 @@
     dma = pltpu.SemaphoreType.DMA
     m4 = MICRO
     scratch = [
+        vmem((grad_rows, 128), F32),
         vmem((images, SIDE * SIDE), jnp.int32), vmem((1, classes), F32),
         vmem((2, c1l), F32), vmem((2, c2l), F32),
         vmem((r1, c1l), F32), vmem((rp, c2l), F32), vmem((rc, classes), F32),
@@ -1032,7 +1043,7 @@
         vmem((nz, rp, c2l), BF), vmem((nz, rp, c2l), BF),
         vmem((nz, rp, c2l), BF), vmem((nz, rp, c2l), BF),
         vmem((nd * images, wide + c2l), BF), vmem((c2l, nd * images), BF),
-        dma((9,)),
+        dma((11,)),
         dma((4,)), dma((nz + 1, 3)), dma((4,)), dma((nz + 1, 1)), dma((4,)), dma((nz + 1, 2)),
         dma((4,)), dma((nz + 1, 1)),
         dma, dma((2, m4)), dma, dma((2, m4)), dma((4,)), dma((4, m4)),
@@ -1047,7 +1058,7 @@
         functools.partial(fused_kernel, dims),
         out_shape=shape((grad_rows, 128), F32),
         in_specs=[hbm, hbm, hbm, scalar, hbm, hbm, hbm, hbm, hbm, hbm],
-        out_specs=whole,
+        out_specs=hbm,
         scratch_shapes=scratch,
         compiler_params=pltpu.CompilerParams(
             collective_id=0, has_side_effects=True, vmem_limit_bytes=58 * 1024 * 1024
@@ -1059,7 +1070,13 @@
 
 
 def adam_kernel(grads, *refs):
-    states, outs = refs[:18], refs[18:]
+    states, results, outs, sent = refs[:18], refs[18:40], refs[40:62], refs[62]
+    copies = []
+
+    def send(i):
+        copies.append(pltpu.make_async_copy(outs[i], results[i], sent.at[i]))
+        copies[-1].start()
+
     row = 0
     for i, (rate, decay) in enumerate(ADAM_RATES):
         weight, moment, second = states[3 * i : 3 * i + 3]
@@ -1076,7 +1093,14 @@
                 out[:, at_q] = value
             if i < 3:
                 outs[18 + i][:, at_q] = found[0].astype(BF)
+        for q in range(3 * i, 3 * i + 3):
+            send(q)
+        if i < 3:
+            send(18 + i)
     outs[21][...] = grads[row : row + 1, :]
+    send(21)
+    for copy in copies:
+        copy.wait()
 
 
 ADAM_RATES = (
@@ -1117,7 +1141,9 @@
             adam_kernel,
             out_shape=tuple(outs),
             in_specs=[whole] * (len(operands) + 1),
-            out_specs=(whole,) * len(outs),
+            out_specs=(pl.BlockSpec(memory_space=pl.ANY),) * len(outs),
+            scratch_shapes=[pltpu.VMEM(o.shape, o.dtype) for o in outs]
+            + [pltpu.SemaphoreType.DMA((len(outs),))],
             compiler_params=pltpu.CompilerParams(vmem_limit_bytes=40 * 1024 * 1024),
         )(grads, *operands)
     )

time: 88.7 us -> 88.5 us (level)
  no operation moved by 1% of the time
where the time goes in v8:
time: 88.5 us; the launch traced here: 88.3 us
  Pallas kernels  86.2 us (97%)
  local copies, waits for them, and re-layouts  1.17 us (1%)
  between operations  0.97 us (1%)
    pallas_call x1, Pallas kernels, fused_gradients(): pl.pallas_call(functools.partial(fused_kernel, dims), out_shape=shape((gr...  84.3 us
    pallas_call x1, Pallas kernels, fused_device(): pl.pallas_call(adam_kernel, out_shape=tuple(outs), in_specs=[whole] * (le...  1.84 us

profile of v8, /device:TPU:0, one launch (start us, length us, event | category | flops | bytes accessed | tf_op | source)
XLA Modules:
  0.0 88.3 jit_solution(4789886096426498419)
XLA Ops:
  0.7 0.0 copy-start.1
  0.7 0.0 copy-start.2
  0.7 0.0 copy-start.3
  0.7 0.0 copy-start.4
  0.7 0.0 copy-start.5
  0.7 0.0 copy-start.6
  0.7 0.0 copy-start.7
  0.7 0.0 copy-start.8
  0.7 0.0 copy-start.9
  0.8 0.0 copy-start.10
  0.8 0.0 copy-start.11
  0.8 0.0 copy-start.12
  0.8 0.0 copy-start.13
  0.8 0.0 copy-start.14
  0.8 0.0 copy-start.15
  0.8 0.0 copy-start.16
  0.8 0.0 copy-start.17
  0.8 0.0 copy-start.18
  0.8 84.3 %shard_map.381.grads = f32[1368,128]{1,0:T(8,128)} custom-call(bf16[1600,128]{1,0:T(8,128)(2,1)} %refs_0_.2, bf16[1600,512]{1,0:T(8,128)(2,1)} %refs_1_.2, s32[16,100]{1,0:T(8,128)} %refs_2_.2, s32[16]{0:T(128)} %refs_3_.2, f32[576,128]{1,0:T(8,128)} %refs_0_.3, f32[64,512]{1,0:T(8,128)} %refs_3_.3, f32[64,1000]{1,0:T(8,128)} %refs_6_.3, f32[1,1000]{1,0:T(1,128)} %bitcast.8, ...), custom_call_target="tpu_custom_call" | custom-call | tf_op jit(solution)/shard_map/pallas_call | solution.py:1057
  85.2 0.0 copy-done.1
  85.2 0.0 copy-done.2
  85.2 0.0 copy-done.3
  85.2 0.0 copy-done.4
  85.2 0.0 copy-done.5
  85.2 0.0 copy-done.6
  85.2 0.0 copy-done.7
  85.2 0.0 copy-done.8
  85.2 0.0 copy-done.9
  85.3 0.0 copy-done.10
  85.3 0.0 copy-done.11
  85.3 0.0 copy-done.12
  85.3 0.0 copy-done.13
  85.3 0.0 copy-done.14
  85.3 0.0 copy-done.15
  85.3 0.0 copy-done.16
  85.3 0.0 copy-done.17
  85.3 0.0 copy-done.18
  85.3 0.0 copy-start
  85.4 1.1 %copy-done = f32[1368,128]{1,0:T(8,128)S(1)} copy-done((f32[1368,128]{1,0:T(8,128)S(1)}, f32[1368,128]{1,0:T(8,128)}, u32[]{:S(2)}) %copy-start) | copy-done | bytes 700440
  86.5 1.8 %shard_map.382 = (f32[576,128]{1,0:T(8,128)}, f32[576,128]{1,0:T(8,128)}, f32[576,128]{1,0:T(8,128)}, f32[64,512]{1,0:T(8,128)}, f32[64,512]{1,0:T(8,128)}, /*in...) custom-call(f32[1368,128]{1,0:T(8,128)S(1)} %copy-done, ...), custom_call_target="tpu_custom_call" | custom-call | tf_op jit(solution)/shard_map/pallas_call | solution.py:1140
Async XLA Ops:
  0.7 84.5 %copy-start.1 = (f32[576,128]{1,0:T(8,128)S(1)}, f32[576,128]{1,0:T(8,128)}, u32[]{:S(2)}) copy-start(f32[576,128]{1,0:T(8,128)} %refs_0_.3) | copy-start | bytes 884740
  0.7 84.5 %copy-start.2 = (f32[64,1000]{1,0:T(8,128)S(1)}, f32[64,1000]{1,0:T(8,128)}, u32[]{:S(2)}) copy-start(f32[64,1000]{1,0:T(8,128)} %refs_6_.3) | copy-start | bytes 768004
  0.7 84.5 %copy-start.3 = (f32[64,512]{1,0:T(8,128)S(1)}, f32[64,512]{1,0:T(8,128)}, u32[]{:S(2)}) copy-start(f32[64,512]{1,0:T(8,128)} %refs_3_.3) | copy-start | bytes 393220
  0.7 84.5 %copy-start.4 = (f32[576,128]{1,0:T(8,128)S(1)}, f32[576,128]{1,0:T(8,128)}, u32[]{:S(2)}) copy-start(f32[576,128]{1,0:T(8,128)} %refs_1_.3) | copy-start | bytes 884740
  0.7 84.5 %copy-start.5 = (f32[576,128]{1,0:T(8,128)S(1)}, f32[576,128]{1,0:T(8,128)}, u32[]{:S(2)}) copy-start(f32[576,128]{1,0:T(8,128)} %refs_2_.3) | copy-start | bytes 884740
  0.7 84.5 %copy-start.6 = (f32[64,1000]{1,0:T(8,128)S(1)}, f32[64,1000]{1,0:T(8,128)}, u32[]{:S(2)}) copy-start(f32[64,1000]{1,0:T(8,128)} %refs_7_.1) | copy-start | bytes 768004
  0.7 84.5 %copy-start.7 = (f32[64,1000]{1,0:T(8,128)S(1)}, f32[64,1000]{1,0:T(8,128)}, u32[]{:S(2)}) copy-start(f32[64,1000]{1,0:T(8,128)} %refs_8_.3) | copy-start | bytes 768004
  0.7 84.5 %copy-start.8 = (f32[64,512]{1,0:T(8,128)S(1)}, f32[64,512]{1,0:T(8,128)}, u32[]{:S(2)}) copy-start(f32[64,512]{1,0:T(8,128)} %refs_4_.3) | copy-start | bytes 393220
  0.7 84.5 %copy-start.9 = (f32[64,512]{1,0:T(8,128)S(1)}, f32[64,512]{1,0:T(8,128)}, u32[]{:S(2)}) copy-start(f32[64,512]{1,0:T(8,128)} %refs_5_.3) | copy-start | bytes 393220
  0.8 84.5 %copy-start.10 = (f32[1000]{0:T(1024)S(1)}, f32[1000]{0:T(1024)}, u32[]{:S(2)}) copy-start(f32[1000]{0:T(1024)} %param.29) | copy-start | bytes 12004
  0.8 84.5 %copy-start.11 = (f32[2,512]{1,0:T(2,128)S(1)}, f32[2,512]{1,0:T(2,128)}, u32[]{:S(2)}) copy-start(f32[2,512]{1,0:T(2,128)} %refs_12_.1) | copy-start | bytes 12292
  0.8 84.5 %copy-start.12 = (f32[1000]{0:T(1024)S(1)}, f32[1000]{0:T(1024)}, u32[]{:S(2)}) copy-start(f32[1000]{0:T(1024)} %param.38) | copy-start | bytes 12004
  0.8 84.5 %copy-start.13 = (f32[1000]{0:T(1024)S(1)}, f32[1000]{0:T(1024)}, u32[]{:S(2)}) copy-start(f32[1000]{0:T(1024)} %param.39) | copy-start | bytes 12004
  0.8 84.5 %copy-start.14 = (f32[2,512]{1,0:T(2,128)S(1)}, f32[2,512]{1,0:T(2,128)}, u32[]{:S(2)}) copy-start(f32[2,512]{1,0:T(2,128)} %refs_13_.1) | copy-start | bytes 12292
  0.8 84.5 %copy-start.15 = (f32[2,512]{1,0:T(2,128)S(1)}, f32[2,512]{1,0:T(2,128)}, u32[]{:S(2)}) copy-start(f32[2,512]{1,0:T(2,128)} %refs_14_.1) | copy-start | bytes 12292
  0.8 84.5 %copy-start.16 = (f32[2,128]{1,0:T(2,128)S(1)}, f32[2,128]{1,0:T(2,128)}, u32[]{:S(2)}) copy-start(f32[2,128]{1,0:T(2,128)} %refs_15_.1) | copy-start | bytes 3076
  0.8 84.5 %copy-start.17 = (f32[2,128]{1,0:T(2,128)S(1)}, f32[2,128]{1,0:T(2,128)}, u32[]{:S(2)}) copy-start(f32[2,128]{1,0:T(2,128)} %refs_16_.1) | copy-start | bytes 3076
  0.8 84.5 %copy-start.18 = (f32[2,128]{1,0:T(2,128)S(1)}, f32[2,128]{1,0:T(2,128)}, u32[]{:S(2)}) copy-start(f32[2,128]{1,0:T(2,128)} %refs_17_.1) | copy-start | bytes 3076
  85.3 1.1 %copy-start = (f32[1368,128]{1,0:T(8,128)S(1)}, f32[1368,128]{1,0:T(8,128)}, u32[]{:S(2)}) copy-start(f32[1368,128]{1,0:T(8,128)} %shard_map.381.grads) | copy-start | bytes 2101252
